TPU v7x, 128 devices: a whole 4x4x4 slice. The times are simulated.
128 devices in a mesh: ctx: 32 (over z_hi, x, y), fsdp: 4 (over z_lo, core).
Axes of the slice: x: 4, y: 4, z: 4 (z_hi: 2, z_lo: 2; z = z_hi * 2 + z_lo), core: 2. Of those that a mesh axis runs over, the one named last changes fastest.
Arguments:
- layer_input: bfloat16 [4, 4096, 2048], P('fsdp', 'ctx'), may hold values from -6 to 6
- w_qkv: bfloat16 [2048, 2304], P(('ctx', 'fsdp')), may hold values from -0.125 to 0.125
- w_out: bfloat16 [2048, 1536], P(('ctx', 'fsdp')), may hold values from -6 to 6
- w_gate_up: bfloat16 [2048, 8704], P(('ctx', 'fsdp')), may hold values from -0.125 to 0.125
- w_down: bfloat16 [2048, 4352], P(('ctx', 'fsdp')), may hold values from -0.09375 to 0.09375
- norm_gains: bfloat16 [4224], P(('ctx', 'fsdp')), may hold values from 0.5 to 1.5
- span_map: int32 [4, 32], replicated, may hold values from 0 to 31, each once within a row
- cotangent: bfloat16 [4, 4096, 2048], P('fsdp', 'ctx'), may hold values from -6 to 6
Outputs:
- layer_out: bfloat16 [4, 4096, 2048], P('fsdp', 'ctx')
- input_grad: bfloat16 [4, 4096, 2048], P('fsdp', 'ctx')
- grad_qkv: float32 [2048, 2304], P(('ctx', 'fsdp'))
- grad_out: float32 [2048, 1536], P(('ctx', 'fsdp'))
- grad_gate_up: float32 [2048, 8704], P(('ctx', 'fsdp'))
- grad_down: float32 [2048, 4352], P(('ctx', 'fsdp'))
- grad_gains: float32 [4224], P(('ctx', 'fsdp'))
- stream_rms: float32 [4], replicated
Inputs may be any that keep to these rules, and one draw needn't show every extreme that they name: `span_map`: each row is a permutation of 0 to 31.
All inputs are finite; a program needn't handle non-finite values.
Results may differ from a plain program's by a relative error of at most 0.02.
Values may be sent and summed in bfloat16 or wider, within the bound.
A program may use at most 512 MiB of HBM per device.

v0:
```python
import jax
import jax.numpy as jnp
from jax import lax
from jax.sharding import PartitionSpec as P

D = 2048
HQ = 24
HK = 6
HD = 64
FF = 4352


EPSILON = 1e-06
ROPE_BASE = 10000.0
NEGATIVE = -1e30


def side_by_side(arrays, axis, dim, along):
    ends, at = ([], 0)
    for a in arrays[:-1]:
        at += a.shape[along]
        ends.append(at)
    both = jnp.concatenate(arrays, axis=along)
    return tuple(jnp.split(lax.all_gather(both, axis, axis=dim, tiled=True), ends, axis=along))


def split_up(value, dim, length):
    lengths = value.shape
    pieces = value.reshape(*lengths[:dim], length, lengths[dim] // length, *lengths[dim + 1 :])
    return jnp.moveaxis(pieces, dim, 0)


def sum_at_owner(value, axis, dim):
    pieces = split_up(value, dim, lax.axis_size(axis))
    arrived = lax.all_to_all(pieces, axis, split_axis=0, concat_axis=0, tiled=True)
    return arrived.astype(jnp.float32).sum(axis=0)


def together(arrays, axis):
    flat, at, finished = (jnp.concatenate([a.reshape(-1) for a in arrays]), 0, [])
    so_far = lax.psum(flat, axis)
    for a in arrays:
        finished.append(so_far[at : at + a.size].reshape(a.shape))
        at += a.size
    return tuple(finished)


def row_positions(span_row, row_ids, rows_dev, n_ctx):
    span_rows = rows_dev // 2
    slot_index = row_ids // rows_dev
    half_index = row_ids % rows_dev // span_rows
    compare = slot_index[:, None] == jnp.arange(n_ctx, dtype=jnp.int32)[None, :]
    first_span = jnp.sum(jnp.where(compare, span_row[None, :], 0), axis=1)
    span_index = jnp.where(half_index == 0, first_span, 2 * n_ctx - 1 - first_span)
    return span_index * span_rows + row_ids % span_rows


def rope_tables(positions, head_dim):
    half_dim = head_dim // 2
    frequencies = ROPE_BASE ** (-(jnp.arange(half_dim, dtype=jnp.float32) * 2.0 / head_dim))
    angles = positions.astype(jnp.float32)[:, None] * frequencies[None, :]
    cosine = jnp.cos(angles)
    sine_rows = jnp.sin(angles)
    return (
        jnp.concatenate([cosine, cosine], axis=1),
        jnp.concatenate([sine_rows, sine_rows], axis=1),
    )


def rotate(value_in, cosine, sine_rows):
    half_dim = value_in.shape[-1] // 2
    turned = jnp.concatenate([-value_in[..., half_dim:], value_in[..., :half_dim]], axis=-1)
    return value_in * cosine + turned * sine_rows


def rotate_back(upstream, cosine, sine_rows):
    half_dim = upstream.shape[-1] // 2
    turned = jnp.concatenate([upstream[..., half_dim:], -upstream[..., :half_dim]], axis=-1)
    return upstream * cosine + turned * sine_rows


def norm_rows(value_in, gain_row):
    inverse = lax.rsqrt(jnp.mean(value_in * value_in, axis=-1, keepdims=True) + EPSILON)
    return (value_in * inverse * gain_row, inverse)


def norm_back(value_in, inverse, gain_row, upstream):
    scaled = upstream * gain_row
    backward = inverse * scaled - value_in * inverse**3 * jnp.mean(
        scaled * value_in, axis=-1, keepdims=True
    )
    return (backward, upstream * value_in * inverse)


def split_gains(gain_full):
    gain_vec = gain_full.astype(jnp.float32)
    return (gain_vec[:D], gain_vec[D : 2 * D], gain_vec[2 * D : 2 * D + HD], gain_vec[2 * D + HD :])


def body(layer_input, w_qkv, w_out, w_gate_up, w_down, norm_gains, span_map, cotangent):
    tok_rows = layer_input.shape[1]
    n_ctx = lax.axis_size("ctx")
    n_all = n_ctx * lax.axis_size("fsdp")
    length = tok_rows * n_ctx
    q_group = HQ // HK
    q_width = HQ * HD
    k_width = HK * HD
    score_scale = HD ** (-0.5)
    contract = (((1,), (1,)), ((), ()))
    ctx_index = lax.axis_index("ctx")
    seq_index = lax.axis_index("fsdp")
    seq_match = jnp.arange(span_map.shape[0], dtype=jnp.int32)[:, None] == seq_index
    span_row = jnp.sum(jnp.where(seq_match, span_map, 0), axis=0)
    local_ids = ctx_index * tok_rows + jnp.arange(tok_rows, dtype=jnp.int32)
    positions = row_positions(span_row, local_ids, tok_rows, n_ctx)
    cosine, sine_rows = rope_tables(positions, HD)
    cosine = cosine[:, None, :]
    sine_rows = sine_rows[:, None, :]
    query_pos = jnp.tile(positions, q_group)
    w_joined, w_proj, w_mlp, w_back, gain_full = (
        *side_by_side((w_qkv, w_out, w_gate_up, w_down), ("ctx", "fsdp"), 0, 1),
        lax.all_gather(norm_gains, ("ctx", "fsdp"), axis=0, tiled=True),
    )
    gain_one, gain_two, gain_query, gain_key = split_gains(gain_full)
    stream_in = layer_input[0].astype(jnp.float32)
    normed_one, inverse_one = norm_rows(stream_in, gain_one)
    normed_one = normed_one.astype(jnp.bfloat16)
    joined_rows = jnp.dot(normed_one, w_joined, preferred_element_type=jnp.float32)
    queries = joined_rows[:, :q_width].reshape(tok_rows, HQ, HD)
    keys_raw = joined_rows[:, q_width : q_width + k_width].reshape(tok_rows, HK, HD)
    values_raw = joined_rows[:, q_width + k_width :].reshape(tok_rows, HK, HD)
    query_norm, inverse_query = norm_rows(queries, gain_query)
    key_norm, inverse_key = norm_rows(keys_raw, gain_key)
    query_rot = rotate(query_norm, cosine, sine_rows).astype(jnp.bfloat16)
    key_rot = rotate(key_norm, cosine, sine_rows).astype(jnp.bfloat16)
    kv_local = jnp.concatenate(
        [
            key_rot.reshape(tok_rows, k_width),
            values_raw.astype(jnp.bfloat16).reshape(tok_rows, k_width),
        ],
        axis=1,
    )
    query_heads = (
        query_rot.reshape(tok_rows, HK, q_group, HD)
        .transpose(1, 2, 0, 3)
        .reshape(HK, q_group * tok_rows, HD)
    )
    kv_all = lax.all_gather(kv_local, "ctx", axis=0, tiled=True)
    key_len = min(512, length)
    n_blocks = length // key_len
    kv_blocks = kv_all.reshape(n_blocks, key_len, 2 * k_width)
    block_starts = jnp.arange(n_blocks, dtype=jnp.int32) * key_len

    def block_keys(kv_block, blk_start):
        key_heads = kv_block[:, :k_width].reshape(key_len, HK, HD).transpose(1, 0, 2)
        value_heads = kv_block[:, k_width:].reshape(key_len, HK, HD).transpose(1, 0, 2)
        key_pos = row_positions(
            span_row, blk_start + jnp.arange(key_len, dtype=jnp.int32), tok_rows, n_ctx
        )
        allowed = key_pos[None, None, :] <= query_pos[None, :, None]
        scores = (
            jnp.einsum("hqd,hkd->hqk", query_heads, key_heads, preferred_element_type=jnp.float32)
            * score_scale
        )
        return (key_heads, value_heads, allowed, jnp.where(allowed, scores, NEGATIVE))

    def stat_step(running, block_item):
        row_max, row_sum = running
        key_heads, value_heads, allowed, scores = block_keys(block_item[0], block_item[1])
        new_max = jnp.maximum(row_max, jnp.max(scores, axis=-1))
        exp_terms = jnp.where(allowed, jnp.exp(scores - new_max[..., None]), 0.0)
        row_sum = row_sum * jnp.exp(row_max - new_max) + jnp.sum(exp_terms, axis=-1)
        return ((new_max, row_sum), None)

    start_max = jnp.full((HK, q_group * tok_rows), NEGATIVE, jnp.float32)
    start_sum = jnp.zeros((HK, q_group * tok_rows), jnp.float32)
    (row_max, row_sum), unused = lax.scan(
        stat_step, (start_max, start_sum), (kv_blocks, block_starts)
    )
    log_norm = row_max + jnp.log(row_sum)

    def value_step(attn_acc, block_item):
        key_heads, value_heads, allowed, scores = block_keys(block_item[0], block_item[1])
        prob_rows = jnp.where(allowed, jnp.exp(scores - log_norm[..., None]), 0.0).astype(
            jnp.bfloat16
        )
        return (
            attn_acc
            + jnp.einsum(
                "hqk,hkd->hqd", prob_rows, value_heads, preferred_element_type=jnp.float32
            ),
            None,
        )

    attn_acc, unused = lax.scan(
        value_step, jnp.zeros((HK, q_group * tok_rows, HD), jnp.float32), (kv_blocks, block_starts)
    )
    attended = (
        attn_acc.reshape(HK, q_group, tok_rows, HD).transpose(2, 0, 1, 3).reshape(tok_rows, q_width)
    )
    attn_low = attended.astype(jnp.bfloat16)
    branch_a = lax.dot_general(attn_low, w_proj, contract, preferred_element_type=jnp.float32)
    middle = stream_in + branch_a
    normed_two, inverse_two = norm_rows(middle, gain_two)
    normed_two = normed_two.astype(jnp.bfloat16)
    gate_up = jnp.dot(normed_two, w_mlp, preferred_element_type=jnp.float32)
    gate_part = gate_up[:, :FF]
    up_part = gate_up[:, FF:]
    sigmoid_gate = jax.nn.sigmoid(gate_part)
    silu_gate = gate_part * sigmoid_gate
    hidden = (silu_gate * up_part).astype(jnp.bfloat16)
    branch_f = lax.dot_general(hidden, w_back, contract, preferred_element_type=jnp.float32)
    result = middle + branch_f
    stats_local = jnp.stack(
        [
            jnp.sum(jnp.sqrt(jnp.mean(stream * stream, axis=-1)))
            for stream in (stream_in, branch_a, middle, branch_f)
        ]
    )
    w_joined, w_proj, w_mlp, w_back, gain_full = (
        *side_by_side((w_qkv, w_out, w_gate_up, w_down), ("ctx", "fsdp"), 0, 1),
        lax.all_gather(norm_gains, ("ctx", "fsdp"), axis=0, tiled=True),
    )
    gain_one, gain_two, gain_query, gain_key = split_gains(gain_full)
    grad_low = cotangent[0]
    grad_out_f = grad_low.astype(jnp.float32)
    grad_hidden = jnp.dot(grad_low, w_back, preferred_element_type=jnp.float32)
    grad_gate = grad_hidden * up_part * sigmoid_gate * (1.0 + gate_part * (1.0 - sigmoid_gate))
    grad_up = grad_hidden * silu_gate
    grad_gu = jnp.concatenate([grad_gate, grad_up], axis=1).astype(jnp.bfloat16)
    grad_normed_two = lax.dot_general(grad_gu, w_mlp, contract, preferred_element_type=jnp.float32)
    back_two, gain_two_terms = norm_back(middle, inverse_two, gain_two, grad_normed_two)
    grad_middle = grad_out_f + back_two
    grad_branch = grad_middle.astype(jnp.bfloat16)
    grad_attn = jnp.dot(grad_branch, w_proj, preferred_element_type=jnp.float32).astype(
        jnp.bfloat16
    )
    grad_heads = (
        grad_attn.reshape(tok_rows, HK, q_group, HD)
        .transpose(1, 2, 0, 3)
        .reshape(HK, q_group * tok_rows, HD)
    )
    row_delta = jnp.sum(grad_heads.astype(jnp.float32) * attn_acc, axis=-1)

    def grad_step(grad_query, block_item):
        key_heads, value_heads, allowed, scores = block_keys(block_item[0], block_item[1])
        prob_rows = jnp.where(allowed, jnp.exp(scores - log_norm[..., None]), 0.0)
        grad_probs = jnp.einsum(
            "hqd,hkd->hqk", grad_heads, value_heads, preferred_element_type=jnp.float32
        )
        grad_scores = (prob_rows * (grad_probs - row_delta[..., None])).astype(jnp.bfloat16)
        grad_query = (
            grad_query
            + jnp.einsum("hqk,hkd->hqd", grad_scores, key_heads, preferred_element_type=jnp.float32)
            * score_scale
        )
        grad_keys = (
            jnp.einsum("hqk,hqd->hkd", grad_scores, query_heads, preferred_element_type=jnp.float32)
            * score_scale
        )
        grad_values = jnp.einsum(
            "hqk,hqd->hkd",
            prob_rows.astype(jnp.bfloat16),
            grad_heads,
            preferred_element_type=jnp.float32,
        )
        kv_grad_block = jnp.concatenate(
            [
                grad_keys.transpose(1, 0, 2).reshape(key_len, k_width),
                grad_values.transpose(1, 0, 2).reshape(key_len, k_width),
            ],
            axis=1,
        )
        return (grad_query, kv_grad_block)

    grad_query, kv_grad_blocks = lax.scan(
        grad_step, jnp.zeros((HK, q_group * tok_rows, HD), jnp.float32), (kv_blocks, block_starts)
    )
    grad_kv = lax.psum_scatter(
        kv_grad_blocks.reshape(length, 2 * k_width).astype(jnp.bfloat16),
        "ctx",
        scatter_dimension=0,
        tiled=True,
    ).astype(jnp.float32)
    grad_query = (
        grad_query.reshape(HK, q_group, tok_rows, HD)
        .transpose(2, 0, 1, 3)
        .reshape(tok_rows, HQ, HD)
    )
    grad_key = grad_kv[:, :k_width].reshape(tok_rows, HK, HD)
    grad_value = grad_kv[:, k_width:]
    grad_query_raw, query_gain_terms = norm_back(
        queries, inverse_query, gain_query, rotate_back(grad_query, cosine, sine_rows)
    )
    grad_key_raw, key_gain_terms = norm_back(
        keys_raw, inverse_key, gain_key, rotate_back(grad_key, cosine, sine_rows)
    )
    grad_joined = jnp.concatenate(
        [
            grad_query_raw.reshape(tok_rows, q_width),
            grad_key_raw.reshape(tok_rows, k_width),
            grad_value,
        ],
        axis=1,
    ).astype(jnp.bfloat16)
    grad_normed_one = lax.dot_general(
        grad_joined, w_joined, contract, preferred_element_type=jnp.float32
    )
    back_one, gain_one_terms = norm_back(stream_in, inverse_one, gain_one, grad_normed_one)
    grad_input = grad_middle + back_one

    def outer_product(left_side, right_side):
        return lax.dot_general(
            left_side, right_side, (((0,), (0,)), ((), ())), preferred_element_type=jnp.float32
        )

    ctx_block = lax.psum_scatter(
        jnp.concatenate(
            [
                outer_product(normed_one, grad_joined),
                outer_product(grad_branch, attn_low),
                outer_product(normed_two, grad_gu),
                outer_product(grad_low, hidden),
            ],
            axis=1,
        ).astype(jnp.bfloat16),
        "ctx",
        scatter_dimension=0,
        tiled=True,
    )
    grad_rows = sum_at_owner(ctx_block, "fsdp", 0)
    joined_cols = w_qkv.shape[1]
    proj_cols = w_out.shape[1]
    mlp_cols = w_gate_up.shape[1]
    grad_qkv = grad_rows[:, :joined_cols]
    grad_proj = grad_rows[:, joined_cols : joined_cols + proj_cols]
    grad_mlp = grad_rows[:, joined_cols + proj_cols : joined_cols + proj_cols + mlp_cols]
    grad_down = grad_rows[:, joined_cols + proj_cols + mlp_cols :]
    gain_grads = jnp.concatenate(
        [
            jnp.sum(gain_one_terms, axis=0),
            jnp.sum(gain_two_terms, axis=0),
            jnp.sum(query_gain_terms, axis=(0, 1)),
            jnp.sum(key_gain_terms, axis=(0, 1)),
        ]
    )
    stats_sum, gain_sum = together((stats_local, gain_grads), ("ctx", "fsdp"))
    gain_share = norm_gains.shape[0]
    own_gains = lax.dynamic_slice_in_dim(
        gain_sum, lax.axis_index(("ctx", "fsdp")) * gain_share, gain_share, 0
    )
    stream_rms = stats_sum / (tok_rows * n_all)
    return (
        result[None].astype(jnp.bfloat16),
        grad_input[None].astype(jnp.bfloat16),
        grad_qkv,
        grad_proj,
        grad_mlp,
        grad_down,
        own_gains,
        stream_rms,
    )


def solution(mesh):
    placed = (
        P("fsdp", "ctx", None),
        P(("ctx", "fsdp"), None),
        P(("ctx", "fsdp"), None),
        P(("ctx", "fsdp"), None),
        P(("ctx", "fsdp"), None),
        P(("ctx", "fsdp")),
        P(),
        P("fsdp", "ctx", None),
    )
    return jax.shard_map(
        body,
        mesh=mesh,
        in_specs=placed,
        out_specs=(
            P("fsdp", "ctx", None),
            P("fsdp", "ctx", None),
            P(("ctx", "fsdp"), None),
            P(("ctx", "fsdp"), None),
            P(("ctx", "fsdp"), None),
            P(("ctx", "fsdp"), None),
            P(("ctx", "fsdp")),
            P(),
        ),
        check_vma=False,
    )
```

profile of v0, /device:TPU:1, one launch (start us, length us, event | category | flops | bytes accessed | tf_op | source)
XLA Modules:
  0.0 1858.0 jit_solution(16851485414662303328)
XLA Ops:
  10.1 68.9 %all-reduce = bf16[4224]{0:T(1024)(128)(2,1)S(1)} all-reduce(bf16[4224]{0:T(1024)(128)(2,1)S(1)} %dynamic-update-slice), channel_id=1, replica_groups=mesh['ctx'=32,'fsdp'=4] {'ctx','fsdp'}, use_global_device_ids=true, to_apply=%add | all-reduce | flops 4224 | bytes 16896
  86.4 307.5 %all-gather.3.cloned.1.call-done = bf16[2048,16896]{1,0:T(8,128)(2,1)} async-done(((bf16[16,16896]{1,0:T(8,128)(2,1)}), bf16[2048,16896]{1,0:T(8,128)(2,1)}) %all-gather.3.cloned.1.call-update) | async-done | bytes 69206032 | tf_op jit(solution)/shard_map/all_gather | solution.py:24
  393.9 5.3 fusion.71
  407.2 87.2 %all-gather.5.cloned.1.call-done = bf16[4096,768]{1,0:T(8,128)(2,1)} async-done(((bf16[128,768]{1,0:T(8,128)(2,1)}), bf16[4096,768]{1,0:T(8,128)(2,1)}) %all-gather.5.cloned.1.call-update) | async-done | bytes 6291472 | tf_op jit(solution)/shard_map/all_gather | solution.py:148
  494.5 9.0 copy.148
  503.4 65.3 %while.46 = (s32[]{:T(128)}, f32[6,512]{1,0:T(8,128)S(1)}, f32[6,512]{1,0:T(8,128)S(1)}, s32[8]{0:T(128)}, s32[32]{0:T(128)}, /*index=5*/bf16[8,512,768]{1,2,0:T...) while((s32[]{:T(128)}, f32[6,512]{1,0:T(8,128)S(1)}, ...), condition=%wide.region_9.10_spmd.clone, body=%wide.region_5.9_spmd.clone.sunk | while | flops 214264320 | bytes 16691984 | solution.py:177
  569.4 69.0 %while.47 = (s32[]{:T(128)}, f32[6,512,64]{1,2,0:T(8,128)S(1)}, s32[8]{0:T(128)}, s32[32]{0:T(128)}, bf16[8,512,768]{1,2,0:T(8,128)(2,1)}, /*index=5*/bf16[6,512...) while((s32[]{:T(128)}, f32[6,512,64]{1,2,0:T(8,128)S(1)}, ...), condition=%wide.region_12.13_spmd.clone, body=%wide.region_10.12_spmd.clone.sunk | while | flops 411250176 | bytes 6451983 | solution.py:195
  592.1 3.2 fusion.180
  600.7 3.2 fusion.180
  609.3 3.2 fusion.180
  617.9 3.2 fusion.180
  626.6 3.2 fusion.180
  635.2 3.2 fusion.180
  638.7 6.6 multiply_reduce_fusion.4
  646.0 16.2 fusion.62
  662.1 10.6 multiply_convert_fusion.1
  672.7 20.0 %multiply_reduce_fusion = (f32[2048]{0:T(1024)}, f32[128]{0:T(128)S(1)}, f32[128,2048]{1,0:T(8,128)}) fusion(f32[128,2048]{1,0:T(8,128)} %get-tuple-element.777, f32[128]{0:T(128)S(1)} %get-tuple-element.819, f32[2048]{0:T(1024)S(1)} %copy-done.29, bf16[2048,16896]{1,0:T(8,128)(2,1)} %all-gather.3.cloned.1.call-done, ...), kind=kOutput, calls=%fused_computation.169 | convolution fusion | flops 4569430016 | bytes 39994368 | tf_op jit(solution)/shard_map/dot_general | solution.py:231
  692.7 14.2 multiply_reduce_fusion.1
  707.0 4.9 fusion.80
  713.9 109.7 %while.48 = (s32[]{:T(128)}, f32[6,512,64]{1,2,0:T(8,128)S(1)}, bf16[8,512,768]{1,2,0:T(8,128)(2,1)}, s32[8]{0:T(128)}, s32[32]{0:T(128)}, /*index=5*/bf16[8,512...) while((s32[]{:T(128)}, f32[6,512,64]{1,2,0:T(8,128)S(1)}, ...), condition=%wide.region_18.19_spmd.clone, body=%wide.region_16.18_spmd.clone.sunk | while | flops 1028402688 | bytes 39080800 | solution.py:276
  823.6 8.7 copy.162
  837.6 4.4 convolution_convert_fusion.3
  842.0 8.7 copy.170
  861.4 12.3 fusion.64
  873.8 17.5 convolution_convert_fusion
  891.3 169.3 %reduce-scatter.5.cloned.1.call-done = bf16[128,768]{1,0:T(8,128)(2,1)} async-done(((bf16[4096,768]{1,0:T(8,128)(2,1)}), bf16[128,768]{1,0:T(8,128)(2,1)}) %reduce-scatter.5.cloned.1.call-update) | async-done | bytes 196624 | tf_op jit(solution)/shard_map/reduce_scatter | solution.py:279
  1066.2 7.4 convolution_convert_fusion.2
  1073.7 43.7 %pad_maximum_fusion = bf16[2048,16896]{1,0:T(8,128)(2,1)} fusion(bf16[2048,4352]{1,0:T(8,128)(2,1)} %fusion.64, bf16[2048,8704]{1,0:T(8,128)(2,1)} %convolution_convert_fusion, bf16[2048,1536]{1,0:T(8,128)(2,1)S(1)} %bitcast.251, bf16[2048,2304]{1,0:T(8,128)(2,1)} %convolution_convert_fusion.2), kind=kLoop, calls=%fused_computation.122 | loop fusion | flops 276824064 | bytes 138412032 | tf_op jit(solution)/shard_map/concatenate | solution.py:318
  1119.4 636.3 %reduce-scatter.7.cloned.1.call-done = bf16[64,16896]{1,0:T(8,128)(2,1)} async-done(((bf16[2048,16896]{1,0:T(8,128)(2,1)}), bf16[64,16896]{1,0:T(8,128)(2,1)}) %reduce-scatter.7.cloned.1.call-update) | async-done | bytes 2162704
  1755.7 6.1 all-to-all-start
  1761.9 7.9 fusion.93
  1772.4 71.6 %psum.7 = f32[4228]{0:T(1024)S(1)} all-reduce(f32[4228]{0:T(1024)S(1)} %concatenate.65), channel_id=1, replica_groups=mesh['ctx'=32,'fsdp'=4] {'ctx','fsdp'}, use_global_device_ids=true, to_apply=%region_37.38 | all-reduce | flops 4228 | bytes 33824 | tf_op jit(solution)/shard_map/psum | solution.py:41
  (524 shorter events, 278.0 us)
Async XLA Ops:
  7.2 386.8 %all-gather.3.cloned.1.call-start = ((), (), s32[]{:S(2)}) async-start(), calls=%async_computation.3 | async-start | bytes 69746688 | tf_op jit(solution)/shard_map/all_gather | solution.py:24
  9.1 485.3 %all-gather.5.cloned.1.call-start = ((), (), s32[]{:S(2)}) async-start(), calls=%async_computation.4 | async-start | bytes 6488064 | tf_op jit(solution)/shard_map/all_gather | solution.py:148
  79.6 320.7 %copy-start.44 = (f32[64]{0:T(128)}, f32[64]{0:T(128)S(1)}, u32[]{:S(2)}) copy-start(f32[64]{0:T(128)S(1)} %get-tuple-element.812) | copy-start | bytes 772
  79.6 321.1 %copy-start.34 = (f32[384]{0:T(512)}, f32[384]{0:T(512)S(1)}, u32[]{:S(2)}) copy-start(f32[384]{0:T(512)S(1)} %mul.565) | copy-start | bytes 4612
  82.5 317.9 %copy-start.19 = (f32[128,64]{0,1:T(8,128)}, f32[128,64]{0,1:T(8,128)S(1)}, u32[]{:S(2)}) copy-start(f32[128,64]{0,1:T(8,128)S(1)} %get-tuple-element.826) | copy-start | bytes 98308
  83.2 317.5 %copy-start.11 = (f32[128,384]{1,0:T(8,128)}, f32[128,384]{1,0:T(8,128)S(1)}, u32[]{:S(2)}) copy-start(f32[128,384]{1,0:T(8,128)S(1)} %copy.142) | copy-start | bytes 589828
  85.8 313.5 %copy-start.42 = (f32[128]{0:T(128)}, f32[128]{0:T(128)S(1)}, u32[]{:S(2)}) copy-start(f32[128]{0:T(128)S(1)} %get-tuple-element.822) | copy-start | bytes 1540
  86.4 312.9 %copy-start.27 = (f32[2048]{0:T(1024)}, f32[2048]{0:T(1024)S(1)}, u32[]{:S(2)}) copy-start(f32[2048]{0:T(1024)S(1)} %get-tuple-element.810) | copy-start | bytes 24580
  401.5 659.1 %reduce-scatter.5.cloned.1.call-start = ((), (), s32[]{:S(2)}) async-start(), calls=%async_computation.5 | async-start | bytes 6488064 | tf_op jit(solution)/shard_map/reduce_scatter | solution.py:279
  404.5 98.9 %copy-start = (f32[128,1536]{0,1:T(8,128)}, f32[128,1536]{0,1:T(8,128)S(1)}, u32[]{:S(2)}) copy-start(f32[128,1536]{0,1:T(8,128)S(1)} %copy.144) | copy-start | bytes 2359300
  569.4 69.3 %copy-start.2 = (bf16[1,128,2048]{2,1,0:T(8,128)(2,1)S(1)}, bf16[1,128,2048]{2,1,0:T(8,128)(2,1)}, u32[]{:S(2)}) copy-start(bf16[1,128,2048]{2,1,0:T(8,128)(2,1)} %param.14) | copy-start | bytes 1572868
  638.6 23.5 %copy-start.9 = (bf16[128,6,4,64]{0,3,2,1:T(8,128)(2,1)}, bf16[128,6,4,64]{0,3,2,1:T(8,128)(2,1)S(1)}, u32[]{:S(2)}) copy-start(bf16[128,6,4,64]{0,3,2,1:T(8,128)(2,1)S(1)} %copy.149) | copy-start | bytes 1179652
  646.0 46.8 %copy-start.39 = (f32[128]{0:T(128)}, f32[128]{0:T(128)S(1)}, u32[]{:S(2)}) copy-start(f32[128]{0:T(128)S(1)} %get-tuple-element.819) | copy-start | bytes 1540
  672.7 20.0 %copy-start.18 = (bf16[128,4352]{1,0:T(8,128)(2,1)}, bf16[128,4352]{1,0:T(8,128)(2,1)S(1)}, u32[]{:S(2)}) copy-start(bf16[128,4352]{1,0:T(8,128)(2,1)S(1)} %get-tuple-element.786) | copy-start | bytes 3342340
  707.0 130.6 %copy-start.6 = (f32[128,2048]{1,0:T(8,128)}, f32[128,2048]{1,0:T(8,128)S(1)}, u32[]{:S(2)}) copy-start(f32[128,2048]{1,0:T(8,128)S(1)} %get-tuple-element.795) | copy-start | bytes 3145732
  832.3 923.4 %reduce-scatter.7.cloned.1.call-start = ((), (), s32[]{:S(2)}) async-start(), calls=%async_computation.6 | async-start | bytes 71368704
  861.4 12.3 copy-start.40
  873.7 188.7 %copy-start.8 = (f32[128,384]{0,1:T(8,128)S(1)}, f32[128,384]{0,1:T(8,128)}, u32[]{:S(2)}) copy-start(f32[128,384]{0,1:T(8,128)} %copy-done.7) | copy-start | bytes 589828
  873.7 188.7 %copy-start.17 = (f32[128,64]{0,1:T(8,128)S(1)}, f32[128,64]{0,1:T(8,128)}, u32[]{:S(2)}) copy-start(f32[128,64]{0,1:T(8,128)} %copy-done.15) | copy-start | bytes 98308
  873.7 188.7 %copy-start.21 = (f32[128,64]{0,1:T(8,128)S(1)}, f32[128,64]{0,1:T(8,128)}, u32[]{:S(2)}) copy-start(f32[128,64]{0,1:T(8,128)} %copy-done.19) | copy-start | bytes 98308
  873.7 188.7 %copy-start.45 = (f32[64]{0:T(128)S(1)}, f32[64]{0:T(128)}, u32[]{:S(2)}) copy-start(f32[64]{0:T(128)} %copy-done.44) | copy-start | bytes 772
  873.7 190.5 %copy-start.12 = (f32[128,384]{1,0:T(8,128)S(1)}, f32[128,384]{1,0:T(8,128)}, u32[]{:S(2)}) copy-start(f32[128,384]{1,0:T(8,128)} %copy-done.11) | copy-start | bytes 589828
  873.7 190.5 %copy-start.14 = (f32[128,384]{1,0:T(8,128)S(1)}, f32[128,384]{1,0:T(8,128)}, u32[]{:S(2)}) copy-start(f32[128,384]{1,0:T(8,128)} %copy-done.13) | copy-start | bytes 589828
  873.7 190.5 %copy-start.22 = (f32[128,384]{1,0:T(8,128)S(1)}, f32[128,384]{1,0:T(8,128)}, u32[]{:S(2)}) copy-start(f32[128,384]{1,0:T(8,128)} %copy.167) | copy-start | bytes 589828
  873.8 190.4 %copy-start.35 = (f32[384]{0:T(512)S(1)}, f32[384]{0:T(512)}, u32[]{:S(2)}) copy-start(f32[384]{0:T(512)} %copy-done.34) | copy-start | bytes 4612
  873.8 192.4 %copy-start.28 = (f32[2048]{0:T(1024)S(1)}, f32[2048]{0:T(1024)}, u32[]{:S(2)}) copy-start(f32[2048]{0:T(1024)} %copy-done.27) | copy-start | bytes 24580
  1117.3 644.5 %copy-start.3 = (bf16[1,128,2048]{2,1,0:T(8,128)(2,1)S(1)}, bf16[1,128,2048]{2,1,0:T(8,128)(2,1)}, u32[]{:S(2)}) copy-start(bf16[1,128,2048]{2,1,0:T(8,128)(2,1)} %param.14) | copy-start | bytes 1572868
  1117.4 644.5 %copy-start.24 = (bf16[128,384]{1,0:T(8,128)(2,1)S(1)}, bf16[128,384]{1,0:T(8,128)(2,1)}, u32[]{:S(2)}) copy-start(bf16[128,384]{1,0:T(8,128)(2,1)} %get-tuple-element.804) | copy-start | bytes 294916
  1117.4 644.5 %copy-start.26 = (bf16[128,384]{1,0:T(8,128)(2,1)S(1)}, bf16[128,384]{1,0:T(8,128)(2,1)}, u32[]{:S(2)}) copy-start(bf16[128,384]{1,0:T(8,128)(2,1)} %copy-done.25) | copy-start | bytes 294916
  1117.4 644.5 %copy-start.43 = (f32[128]{0:T(128)S(1)}, f32[128]{0:T(128)}, u32[]{:S(2)}) copy-start(f32[128]{0:T(128)} %copy-done.42) | copy-start | bytes 1540
  1755.7 92.3 %all-to-all-start = ((bf16[4,16,16896]{2,1,0:T(8,128)(2,1)}), bf16[4,16,16896]{2,1,0:T(8,128)(2,1)S(1)}, u32[]{:S(2)}, u32[]{:S(2)}) async-start(bf16[4,16,16896]{2,1,0:T(8,128)(2,1)} %bitcast.277), calls=%async_computation.1 | async-start | bytes 4325376 | tf_op jit(solution)/shard_map/all_to_all | solution.py:35
  1761.9 83.3 %copy-start.47 = (f32[128]{0:T(128)S(1)}, f32[128]{0:T(128)}, u32[]{:S(2)}) copy-start(f32[128]{0:T(128)} %get-tuple-element.821) | copy-start | bytes 1540
  (39 other events, 153.4 us)
Sparse Core Ops, SparseCore 0:
  10.3 383.6 all-gather.2
  401.6 92.7 all-gather.4
  832.4 228.1 reduce-scatter.4
  1117.5 638.1 reduce-scatter.6
where the time goes:
time: 1870 us; the launch traced here: 1860 us
  waiting for transfers between devices  1200 us (64%)
  matrix products  221 us (12%)
  other arithmetic  145 us (8%)
  blocking collectives  141 us (8%)
  local copies, waits for them, and re-layouts  128 us (7%)
    unnamed x5, waiting for transfers between devices  636 us
    all_gather x1, waiting for transfers between devices, side_by_side(): lax.all_gather(both, axis, axis=dim, tiled=True)  308 us
    reduce_scatter x1, waiting for transfers between devices, body(): lax.psum_scatter(kv_grad_blocks.reshape(length, 2 * k_width).astype(jnp.b...  169 us
    all_gather x1, waiting for transfers between devices, body(): kv_all = lax.all_gather(kv_local, 'ctx', axis=0, tiled=True)  87.2 us
    psum x1, blocking collectives, together(): so_far = lax.psum(flat, axis)  71.6 us
    unnamed x1, blocking collectives  68.9 us
    concatenate x1, other arithmetic, body(): jnp.concatenate([outer_product(normed_one, grad_joined), outer_product(gr...  43.7 us
    dot_general x4, matrix products, outer_product(): lax.dot_general(left_side, right_side, (((0,), (0,)), ((), ())), preferre...  41.7 us
  transfers between devices with their start and end apart: 5, of which 4 were waited for; matrix products, arithmetic and copies ran while one was open for 5% of the time, Pallas kernels for 0%

commit v1 on v0

v1 whole, which is shorter than its diff:
```python
import functools

import jax
import jax.numpy as jnp
from jax import lax
from jax.experimental import pallas as pl
from jax.experimental.pallas import tpu as pltpu
from jax.sharding import PartitionSpec as P

D = 2048
HQ = 24
HK = 6
HD = 64
FF = 4352
TOK = 128
SPAN = 64
N_CTX = 32

HH = HK // 2
GROUP = HQ // HK
QH = HQ // 2
QW = QH * HD
KVW = HH * 2 * HD
FH = FF // 2
KEYS = 512
SPANS_STEP = KEYS // SPAN
FULL_STEPS = 7
QROWS = GROUP * SPAN

EPSILON = 1e-06
ROPE_BASE = 10000.0
LOG2E = 1.4426950408889634
MESH = pl.DeviceIdType.MESH
BF = jnp.bfloat16
F32 = jnp.float32
NT = (((1,), (1,)), ((), ()))
NN = (((1,), (0,)), ((), ()))
TN = (((0,), (0,)), ((), ()))
W_DIMS = ("h", "x", "y", "l")
KV_DIMS = ("h", "x", "y")
ORDERS = (("x", "y", "z"), ("y", "z", "x"), ("z", "x", "y"))
KV_ORDERS = (("h", "x", "y"), ("x", "y", "h"), ("y", "h", "x"))
SIZES = {"x": 4, "y": 4, "z": 4, "h": 2}


def here():
    c = lax.axis_index("ctx")
    f = lax.axis_index("fsdp")
    return {
        "x": lax.rem(lax.div(c, 4), 4),
        "y": lax.rem(c, 4),
        "z": lax.div(c, 16) * 2 + lax.div(f, 2),
        "h": lax.div(c, 16),
        "l": lax.rem(f, 2) * 0 + lax.div(f, 2),
        "core": lax.rem(f, 2),
    }


def device_of(x, y, z, core):
    return (lax.div(z, 2) * 16 + x * 4 + y, lax.rem(z, 2) * 2 + core)


def moved(at, axis, by):
    if axis == "core":
        return device_of(at["x"], at["y"], at["z"], 1 - at["core"])
    place = {k: at[k] for k in ("x", "y", "z")}
    if axis == "h":
        place["z"] = lax.rem(at["z"] + 2, 4)
    else:
        place[axis] = lax.rem(at[axis] + by + 4, 4)
    return device_of(place["x"], place["y"], place["z"], at["core"])


def labels(axis, value):
    if axis == "z":
        return {"h": lax.div(value, 2), "l": lax.rem(value, 2)}
    return {axis: value}


def pick(ref, dims, values, tail):
    return ref.at[tuple(values[d] if d in values else slice(None) for d in dims) + tail]


def greet(devices):
    barrier = pltpu.get_barrier_semaphore()
    for d in devices:
        pl.semaphore_signal(barrier, inc=1, device_id=d, device_id_type=MESH)
    pl.semaphore_wait(barrier, len(devices))


def send(src, dst, ssem, rsem, device):
    copy = pltpu.make_async_remote_copy(
        src_ref=src, dst_ref=dst, send_sem=ssem, recv_sem=rsem, device_id=device, device_id_type=MESH
    )
    copy.start()
    return copy


def ring_gather(streams, dims, at, ssem, rsem):
    sent = []
    for phase in range(3):
        first = []
        for k, (ref, order, rows, cols) in enumerate(streams):
            axis = order[phase]
            later = {}
            for a in order[phase + 1 :]:
                later.update(labels(a, at[a]))
            mine = pick(ref, dims, {**later, **labels(axis, at[axis])}, (slice(None), cols))
            if SIZES[axis] == 2:
                first.append((send(mine, mine, ssem.at[k, phase, 0], rsem.at[k, phase, 0], moved(at, axis, 1)),))
            else:
                up = send(mine, mine, ssem.at[k, phase, 0], rsem.at[k, phase, 0], moved(at, axis, 1))
                down = send(mine, mine, ssem.at[k, phase, 1], rsem.at[k, phase, 1], moved(at, axis, 3))
                first.append((up, down))
        second = []
        for k, (ref, order, rows, cols) in enumerate(streams):
            axis = order[phase]
            for c in first[k]:
                c.wait_recv()
                sent.append(c)
            if SIZES[axis] == 2:
                continue
            later = {}
            for a in order[phase + 1 :]:
                later.update(labels(a, at[a]))
            below = lax.rem(at[axis] + 3, 4)
            above = lax.rem(at[axis] + 1, 4)
            low = pick(ref, dims, {**later, **labels(axis, below)}, (pl.ds(0, rows // 2), cols))
            high = pick(ref, dims, {**later, **labels(axis, above)}, (pl.ds(rows // 2, rows // 2), cols))
            second.append(send(low, low, ssem.at[k, phase, 2], rsem.at[k, phase, 2], moved(at, axis, 1)))
            second.append(send(high, high, ssem.at[k, phase, 3], rsem.at[k, phase, 3], moved(at, axis, 3)))
        for c in second:
            c.wait_recv()
            sent.append(c)
    for c in sent:
        c.wait_send()


def neighbours(at, axes):
    out = []
    for a in axes:
        if a in ("core", "h"):
            out.append(moved(at, a, 1))
        else:
            out.append(moved(at, a, 1))
            out.append(moved(at, a, 3))
    return out


def weight_kernel(parts, n_pair, n_in, *refs):
    ins, outs = refs[:n_in], refs[n_in : 2 * n_in]
    psem, lsem, ssem, rsem = refs[2 * n_in :]
    at = here()
    core = at["core"]
    sibling = moved(at, "core", 1)
    greet([sibling] + neighbours(at, ("x", "y", "z")))
    own = {d: at[d] for d in W_DIMS}
    remote, local = [], []
    for i in range(n_in):
        if i < len(parts):
            dst = pick(outs[i], W_DIMS, own, (pl.ds(core * 16, 16), slice(None)))
            remote.append(send(ins[i].at[1 - core], dst, psem.at[i, 0], psem.at[i, 1], sibling))
            local.append(pltpu.make_async_copy(ins[i].at[core], dst, lsem.at[i]))
        else:
            dst = outs[i].at[core]
            remote.append(send(ins[i], dst, psem.at[i, 0], psem.at[i, 1], sibling))
            local.append(pltpu.make_async_copy(ins[i], dst, lsem.at[i]))
        local[-1].start()
    for i in range(len(parts)):
        remote[i].wait_recv()
        local[i].wait()
    streams = []
    for i, pieces in enumerate(parts):
        for start, length, order in pieces:
            streams.append((outs[i], order, 32, pl.ds(start, length)))
    ring_gather(streams, W_DIMS, at, ssem, rsem)
    for i in range(n_in):
        remote[i].wait_send()
        if i >= len(parts):
            remote[i].wait_recv()
            local[i].wait()


def gather_weights(shards, parts, pairs, cid):
    n_in = len(shards) + len(pairs)
    n_streams = sum(len(p) for p in parts)
    outs = [jax.ShapeDtypeStruct((2, 4, 4, 2, 32, s.shape[-1]), s.dtype) for s in shards]
    outs += [jax.ShapeDtypeStruct((2,) + p.shape, p.dtype) for p in pairs]
    anywhere = pl.BlockSpec(memory_space=pl.ANY)
    return pl.pallas_call(
        functools.partial(weight_kernel, parts, len(pairs), n_in),
        out_shape=outs,
        in_specs=[anywhere] * n_in,
        out_specs=[anywhere] * n_in,
        scratch_shapes=[
            pltpu.SemaphoreType.DMA((n_in, 2)),
            pltpu.SemaphoreType.DMA((n_in,)),
            pltpu.SemaphoreType.DMA((n_streams, 3, 4)),
            pltpu.SemaphoreType.DMA((n_streams, 3, 4)),
        ],
        compiler_params=pltpu.CompilerParams(collective_id=cid, has_side_effects=True),
        name=f"gather_weights_{cid}",
    )(*shards, *pairs)


def kv_gather_kernel(src, out, lsem, ssem, rsem):
    at = here()
    greet(neighbours(at, ("h", "x", "y")))
    local = pltpu.make_async_copy(src, pick(out, KV_DIMS, {d: at[d] for d in KV_DIMS}, ()), lsem)
    local.start()
    local.wait()
    streams = [(out, KV_ORDERS[h], 256, pl.ds(h * 2 * HD, 2 * HD)) for h in range(HH)]
    ring_gather(streams, KV_DIMS, at, ssem, rsem)


def gather_kv(kv_local, cid):
    anywhere = pl.BlockSpec(memory_space=pl.ANY)
    return pl.pallas_call(
        kv_gather_kernel,
        out_shape=jax.ShapeDtypeStruct((2, 4, 4, 2 * TOK, KVW), BF),
        in_specs=[anywhere],
        out_specs=anywhere,
        scratch_shapes=[
            pltpu.SemaphoreType.DMA,
            pltpu.SemaphoreType.DMA((HH, 3, 4)),
            pltpu.SemaphoreType.DMA((HH, 3, 4)),
        ],
        compiler_params=pltpu.CompilerParams(collective_id=cid, has_side_effects=True),
        name="gather_kv",
    )(kv_local)


def lead_shape(dims):
    full = {"h": 2, "x": 4, "y": 4, "l": 2}
    return tuple(full[d] for d in dims)


def without(dims, axis):
    gone = ("h", "l") if axis == "z" else (axis,)
    return tuple(d for d in dims if d not in gone)


def sum_streams(specs, dims, at, arrived, mine, ssem, rsem, lsem):
    state = [(s[0], dims, s[3]) for s in specs]
    sent = []
    for phase in range(3):
        flight = []
        for k, (unused, order, rows, cols0, width) in enumerate(specs):
            ref, now, cols = state[k]
            axis = order[phase]
            size = SIZES[axis]
            copies = []
            for i in (1, 3, 2) if size == 4 else (1,):
                target = lax.rem(at[axis] + i, size)
                src = pick(ref, now, labels(axis, target), (slice(None), cols))
                copies.append(
                    send(src, arrived[k][phase].at[i - 1], ssem.at[k, phase, i - 1], rsem.at[k, phase, i - 1], moved(at, axis, i))
                )
            local = None
            if phase == 0:
                src = pick(ref, now, labels(axis, at[axis]), (slice(None), cols))
                local = pltpu.make_async_copy(src, mine[k][0], lsem.at[k])
                local.start()
            flight.append((copies, local))
        for k, (unused, order, rows, cols0, width) in enumerate(specs):
            ref, now, cols = state[k]
            axis = order[phase]
            size = SIZES[axis]
            copies, local = flight[k]
            rest = without(now, axis)
            if local is not None:
                local.wait()
            for c in copies:
                c.wait_recv()
                sent.append(c)
            got = arrived[k][phase]
            lead = lead_shape(rest)
            out = mine[k][phase + 1]

            def add(idx):
                if phase == 0:
                    own = mine[k][0][idx]
                else:
                    own = pick(ref, now, labels(axis, at[axis]), ())[idx]
                total = own.astype(F32)
                for i in range(size - 1):
                    total = total + got[(i,) + idx].astype(F32)
                out[idx] = total.astype(out.dtype)

            spots = [()]
            for n in lead:
                spots = [s + (j,) for s in spots for j in range(n)]
            for s in spots:
                add(s + (slice(None), slice(None)))
            state[k] = (out, rest, slice(None))
    for c in sent:
        c.wait_send()


def sum_scratch(specs, dims, last):
    arrived, mine = [], []
    for order, rows, width in specs:
        now = dims
        a, m = [], []
        for phase in range(3):
            rest = without(now, order[phase])
            lead = lead_shape(rest)
            a.append(pltpu.VMEM((SIZES[order[phase]] - 1,) + lead + (rows, width), BF))
            if phase == 0:
                m.append(pltpu.VMEM(lead + (rows, width), BF))
            m.append(pltpu.VMEM(lead + (rows, width), BF if phase < 2 else last))
            now = rest
        arrived.append(a)
        mine.append(m)
    return arrived, mine


def sum_peers(at, axes):
    out = []
    for a in axes:
        for i in (1, 3, 2) if SIZES[a] == 4 else (1,):
            out.append(moved(at, a, i))
    return out


def kv_sum_kernel(src, out, arrived, mine, ssem, rsem, lsem):
    at = here()
    greet(sum_peers(at, ("h", "x", "y")))
    orders = KV_ORDERS
    specs = [(src, orders[h], 2 * TOK, pl.ds(h * 2 * HD, 2 * HD), 2 * HD) for h in range(HH)]
    sum_streams(specs, KV_DIMS, at, arrived, mine, ssem, rsem, lsem)
    for h in range(HH):
        out[:, h * 2 * HD : (h + 1) * 2 * HD] = mine[h][3][...]


def sum_kv(grads, cid):
    scratch = sum_scratch([(KV_ORDERS[h], 2 * TOK, 2 * HD) for h in range(HH)], KV_DIMS, F32)
    return pl.pallas_call(
        kv_sum_kernel,
        out_shape=jax.ShapeDtypeStruct((2 * TOK, KVW), F32),
        in_specs=[pl.BlockSpec(memory_space=pl.ANY)],
        out_specs=pl.BlockSpec(memory_space=pltpu.VMEM),
        scratch_shapes=[
            scratch[0],
            scratch[1],
            pltpu.SemaphoreType.DMA((HH, 3, 3)),
            pltpu.SemaphoreType.DMA((HH, 3, 3)),
            pltpu.SemaphoreType.DMA((HH,)),
        ],
        compiler_params=pltpu.CompilerParams(
            collective_id=cid, has_side_effects=True, vmem_limit_bytes=48 * 1024 * 1024
        ),
        name="sum_kv",
    )(grads)


SMALL = (("q", 0, 384), ("q", 384, 384), ("q", 768, 384), ("o", 0, 256), ("o", 256, 256), ("o", 512, 256))


def weight_sum_kernel(gq, go, oq, oo, arrived, mine, stage_q, stage_o, got_q, got_o, ssem, rsem, lsem, csem):
    at = here()
    core = at["core"]
    sibling = moved(at, "core", 1)
    greet([sibling] + sum_peers(at, ("x", "y", "z")))
    specs = []
    for k, (name, start, width) in enumerate(SMALL):
        specs.append((gq if name == "q" else go, ORDERS[k % 3], 32, pl.ds(start, width), width))
    sum_streams(specs, W_DIMS, at, arrived, mine, ssem, rsem, lsem)
    for k, (name, start, width) in enumerate(SMALL):
        stage = stage_q if name == "q" else stage_o
        stage[:, start : start + width] = mine[k][3][...]
    other = pl.ds(pl.multiple_of((1 - core) * 16, 16), 16)
    own = pl.ds(pl.multiple_of(core * 16, 16), 16)
    a = send(stage_q.at[other], got_q, csem.at[0], csem.at[1], sibling)
    b = send(stage_o.at[other], got_o, csem.at[2], csem.at[3], sibling)
    oq[core] = stage_q[own, :]
    oo[core] = stage_o[own, :]
    a.wait_recv()
    oq[1 - core] = got_q[...]
    b.wait_recv()
    oo[1 - core] = got_o[...]
    a.wait_send()
    b.wait_send()


def sum_weights(gq, go, cid):
    scratch = sum_scratch([(ORDERS[k % 3], 32, SMALL[k][2]) for k in range(6)], W_DIMS, F32)
    anywhere = pl.BlockSpec(memory_space=pl.ANY)
    vmem = pl.BlockSpec(memory_space=pltpu.VMEM)
    wq, wo = gq.shape[-1], go.shape[-1]
    return pl.pallas_call(
        weight_sum_kernel,
        out_shape=[jax.ShapeDtypeStruct((2, 16, wq), F32), jax.ShapeDtypeStruct((2, 16, wo), F32)],
        in_specs=[anywhere] * 2,
        out_specs=[vmem] * 2,
        scratch_shapes=[
            scratch[0],
            scratch[1],
            pltpu.VMEM((32, wq), F32),
            pltpu.VMEM((32, wo), F32),
            pltpu.VMEM((16, wq), F32),
            pltpu.VMEM((16, wo), F32),
            pltpu.SemaphoreType.DMA((6, 3, 3)),
            pltpu.SemaphoreType.DMA((6, 3, 3)),
            pltpu.SemaphoreType.DMA((6,)),
            pltpu.SemaphoreType.DMA((4,)),
        ],
        compiler_params=pltpu.CompilerParams(
            collective_id=cid, has_side_effects=True, vmem_limit_bytes=48 * 1024 * 1024
        ),
        name="sum_weights",
    )(gq, go)


def total_kernel(x_ref, o_ref, buf, ssem, rsem):
    at = here()
    greet([moved(at, "core", 1)] + sum_peers(at, ("x", "y", "z")))
    value = x_ref[...]
    sent = []
    for phase, axis in enumerate(("core", "z", "y", "x")):
        buf[phase, 0] = value
        copies = []
        for i in (1, 3, 2) if axis != "core" else (1,):
            copies.append(
                send(buf.at[phase, 0], buf.at[phase, i], ssem.at[phase, i], rsem.at[phase, i], moved(at, axis, i))
            )
        for c in copies:
            c.wait_recv()
            sent.append(c)
        if axis == "core":
            value = buf[phase, 0] + buf[phase, 1]
        else:
            value = (buf[phase, 0] + buf[phase, 2]) + (buf[phase, 1] + buf[phase, 3])
    o_ref[...] = value
    for c in sent:
        c.wait_send()


def total_everywhere(x, cid):
    return pl.pallas_call(
        total_kernel,
        out_shape=jax.ShapeDtypeStruct(x.shape, F32),
        in_specs=[pl.BlockSpec(memory_space=pltpu.VMEM)],
        out_specs=pl.BlockSpec(memory_space=pltpu.VMEM),
        scratch_shapes=[
            pltpu.VMEM((4, 4) + x.shape, F32),
            pltpu.SemaphoreType.DMA((4, 4)),
            pltpu.SemaphoreType.DMA((4, 4)),
        ],
        compiler_params=pltpu.CompilerParams(collective_id=cid, has_side_effects=True),
        name="total_everywhere",
    )(x)


def fetch_keys(tab, kvg, kv, sems):
    for s in range(2):

        def go(p, carry):
            slot = tab[s, p]
            row = lax.rem(slot, 2) * SPAN + s * TOK
            pltpu.make_async_copy(
                kvg.at[lax.div(slot, 2), pl.ds(pl.multiple_of(row, SPAN), SPAN)],
                kv.at[s, pl.ds(pl.multiple_of(p * SPAN, SPAN), SPAN)],
                sems.at[s],
            ).start()
            return carry

        lax.fori_loop(0, 2 * N_CTX, go, 0)


def step_of(t, low_steps):
    half = jnp.where(t < low_steps, 0, 1)
    return half, jnp.where(t < low_steps, t, t - low_steps)


def attend_kernel(tab, q_ref, kvg, o_ref, l_ref, kv, acc, total, sems):
    fetch_keys(tab, kvg, kv, sems)
    rate = LOG2E * HD**-0.5
    for s in range(2):
        pltpu.make_async_copy(kv.at[s], kv.at[s], sems.at[s]).wait()
        span = tab[s, 2 * N_CTX]
        low_steps = lax.div(span, SPANS_STEP)
        for h in range(HH):
            acc[...] = jnp.zeros_like(acc)
            total[...] = jnp.zeros_like(total)

            def step(half, block, limit):
                keys = kv[s, pl.ds(pl.multiple_of(block * KEYS, KEYS), KEYS), h * 2 * HD : (h + 1) * 2 * HD]
                scores = lax.dot_general(keys, q_ref[s, h, half], NT, preferred_element_type=F32)
                prob = jnp.exp2(scores * rate)
                if limit is not None:
                    row = lax.broadcasted_iota(jnp.int32, prob.shape, 0)
                    col = lax.rem(lax.broadcasted_iota(jnp.int32, prob.shape, 1), SPAN)
                    prob = jnp.where(row <= col + limit, prob, 0.0)
                total[half] += jnp.sum(prob, axis=0, keepdims=True)
                acc[half] += lax.dot_general(keys, prob.astype(BF), TN, preferred_element_type=F32)

            def full(t, carry):
                half, block = step_of(t, low_steps)
                step(half, block, None)
                return carry

            lax.fori_loop(0, FULL_STEPS, full, 0)
            for half, first in ((0, span), (1, 2 * N_CTX - 1 - span)):
                step(half, lax.div(first, SPANS_STEP), lax.rem(first, SPANS_STEP) * SPAN)
                out = acc[half, HD:, :] / total[half]
                o_ref[s, h, half] = out.T
                l_ref[s, h, half] = jnp.log2(total[half])


def attend(tab, q_pad, kvg):
    vmem = pl.BlockSpec(memory_space=pltpu.VMEM)
    return pl.pallas_call(
        attend_kernel,
        out_shape=[
            jax.ShapeDtypeStruct((2, HH, 2, QROWS, HD), F32),
            jax.ShapeDtypeStruct((2, HH, 2, 1, QROWS), F32),
        ],
        in_specs=[pl.BlockSpec(memory_space=pltpu.SMEM), vmem, pl.BlockSpec(memory_space=pl.ANY)],
        out_specs=[vmem, vmem],
        scratch_shapes=[
            pltpu.VMEM((2, N_CTX * TOK, KVW), BF),
            pltpu.VMEM((2, 2 * HD, QROWS), F32),
            pltpu.VMEM((2, 1, QROWS), F32),
            pltpu.SemaphoreType.DMA((2,)),
        ],
        compiler_params=pltpu.CompilerParams(vmem_limit_bytes=48 * 1024 * 1024),
        cost_estimate=pl.CostEstimate(flops=20_000_000_000, bytes_accessed=20_000_000, transcendentals=8_000_000),
        name="attend",
    )(tab, q_pad, kvg)


def attend_back_kernel(tab, qd_ref, l_ref, delta_ref, kvg, dq_ref, dkv_ref, kv, stage, acc, dq_acc, sems, osems):
    fetch_keys(tab, kvg, kv, sems)
    rate = LOG2E * HD**-0.5
    lanes = lax.broadcasted_iota(jnp.int32, (1, 2 * HD), 1)
    factor = jnp.where(lanes < HD, HD**-0.5, 1.0)
    for s in range(2):
        pltpu.make_async_copy(kv.at[s], kv.at[s], sems.at[s]).wait()
        span = tab[s, 2 * N_CTX]
        low_steps = lax.div(span, SPANS_STEP)
        for h in range(HH):
            dq_acc[...] = jnp.zeros_like(dq_acc)
            acc[...] = jnp.zeros_like(acc)

            def step(half, block, limit):
                rows = pl.ds(pl.multiple_of(block * KEYS, KEYS), KEYS)
                keys = kv[s, rows, h * 2 * HD : (h + 1) * 2 * HD]
                both = lax.dot_general(keys, qd_ref[s, h, half], NT, preferred_element_type=F32)
                prob = jnp.exp2(both[:, :QROWS] * rate - l_ref[s, h, half])
                if limit is not None:
                    row = lax.broadcasted_iota(jnp.int32, prob.shape, 0)
                    col = lax.rem(lax.broadcasted_iota(jnp.int32, prob.shape, 1), SPAN)
                    prob = jnp.where(row <= col + limit, prob, 0.0)
                grad = (prob * (both[:, QROWS:] - delta_ref[s, h, half])).astype(BF)
                pair = jnp.concatenate([grad, prob.astype(BF)], axis=1)
                acc[rows, :] += lax.dot_general(pair, qd_ref[s, h, half], NN, preferred_element_type=F32)
                dq_acc[half] += lax.dot_general(keys, grad, TN, preferred_element_type=F32)

            def full(t, carry):
                half, block = step_of(t, low_steps)
                step(half, block, None)
                return carry

            lax.fori_loop(0, FULL_STEPS, full, 0)
            for half, first in ((0, span), (1, 2 * N_CTX - 1 - span)):
                step(half, lax.div(first, SPANS_STEP), lax.rem(first, SPANS_STEP) * SPAN)
                dq_ref[s, h, half] = (dq_acc[half, :HD, :] * HD**-0.5).T

            def cast(b, carry):
                rows = pl.ds(pl.multiple_of(b * KEYS, KEYS), KEYS)
                stage[s, rows, h * 2 * HD : (h + 1) * 2 * HD] = (acc[rows, :] * factor).astype(BF)
                return carry

            lax.fori_loop(0, N_CTX * TOK // KEYS, cast, 0)

        def put(p, carry):
            slot = tab[s, p]
            row = lax.rem(slot, 2) * SPAN + s * TOK
            pltpu.make_async_copy(
                stage.at[s, pl.ds(pl.multiple_of(p * SPAN, SPAN), SPAN)],
                dkv_ref.at[lax.div(slot, 2), pl.ds(pl.multiple_of(row, SPAN), SPAN)],
                osems.at[s],
            ).start()
            return carry

        lax.fori_loop(0, 2 * N_CTX, put, 0)
    for s in range(2):
        pltpu.make_async_copy(stage.at[s], stage.at[s], osems.at[s]).wait()


def attend_back(tab, qd, log_sum, delta, kvg):
    vmem = pl.BlockSpec(memory_space=pltpu.VMEM)
    anywhere = pl.BlockSpec(memory_space=pl.ANY)
    return pl.pallas_call(
        attend_back_kernel,
        out_shape=[
            jax.ShapeDtypeStruct((2, HH, 2, QROWS, HD), F32),
            jax.ShapeDtypeStruct((N_CTX, 2 * TOK, KVW), BF),
        ],
        in_specs=[pl.BlockSpec(memory_space=pltpu.SMEM), vmem, vmem, vmem, anywhere],
        out_specs=[vmem, anywhere],
        scratch_shapes=[
            pltpu.VMEM((2, N_CTX * TOK, KVW), BF),
            pltpu.VMEM((2, N_CTX * TOK, KVW), BF),
            pltpu.VMEM((N_CTX * TOK, 2 * HD), F32),
            pltpu.VMEM((2, 2 * HD, QROWS), F32),
            pltpu.SemaphoreType.DMA((2,)),
            pltpu.SemaphoreType.DMA((2,)),
        ],
        compiler_params=pltpu.CompilerParams(vmem_limit_bytes=48 * 1024 * 1024),
        cost_estimate=pl.CostEstimate(flops=50_000_000_000, bytes_accessed=30_000_000, transcendentals=8_000_000),
        name="attend_back",
    )(tab, qd, log_sum, delta, kvg)


def permutation(axis, by):
    pairs = []
    for c in range(N_CTX):
        for f in range(4):
            h, x, y = c // 16, (c // 4) % 4, c % 4
            z, core = h * 2 + f // 2, f % 2
            if axis == "x":
                x = (x + by) % 4
            elif axis == "y":
                y = (y + by) % 4
            elif axis == "z":
                z = (z + by) % 4
            else:
                core = 1 - core
            pairs.append((c * 4 + f, ((z // 2) * 16 + x * 4 + y) * 4 + (z % 2) * 2 + core))
    return pairs


def shift(value, axis, by=1):
    return lax.ppermute(value, ("ctx", "fsdp"), permutation(axis, by))


def take(value, dims, axis, index, offset=0):
    for label, i in labels(axis, index).items():
        at = offset + dims.index(label)
        value = lax.dynamic_slice_in_dim(value, i, 1, axis=at)
    gone = tuple(offset + dims.index(d) for d in labels(axis, index))
    return lax.squeeze(value, gone)


def sum_at_owner(left, right, order, at):
    tokens = left.shape[0]
    blocks = left.reshape(tokens, 2, 4, 4, 2, 32)
    axis = order[0]
    dims = W_DIMS
    rest = without(dims, axis)

    def product(target):
        rows = take(blocks, dims, axis, target, 1).reshape(tokens, -1)
        out = lax.dot_general(rows, right, TN, preferred_element_type=F32).astype(BF)
        return out.reshape(lead_shape(rest) + (32, right.shape[1]))

    gathered = [shift(product(lax.rem(at[axis] + i, 4)), axis, i) for i in (1, 3, 2)]
    gathered.append(product(at[axis]))
    for phase in (1, 2):
        dims, axis = rest, order[phase]
        rest = without(dims, axis)

        def block(target, kind):
            total = sum(take(g, dims, axis, target).astype(F32) for g in gathered)
            return total.astype(kind)

        nxt = [shift(block(lax.rem(at[axis] + i, 4), BF), axis, i) for i in (1, 3, 2)]
        nxt.append(block(at[axis], F32))
        gathered = nxt
    return sum(g.astype(F32) for g in gathered)


def norm_rows(value_in, gain_row):
    inverse = lax.rsqrt(jnp.mean(value_in * value_in, axis=-1, keepdims=True) + EPSILON)
    return (value_in * inverse * gain_row, inverse)


def norm_back(value_in, inverse, gain_row, upstream):
    scaled = upstream * gain_row
    backward = inverse * scaled - value_in * inverse**3 * jnp.mean(scaled * value_in, axis=-1, keepdims=True)
    return (backward, upstream * value_in * inverse)


def rotate(value_in, cosine, sine_rows):
    half_dim = value_in.shape[-1] // 2
    turned = jnp.concatenate([-value_in[..., half_dim:], value_in[..., :half_dim]], axis=-1)
    return value_in * cosine + turned * sine_rows


def rotate_back(upstream, cosine, sine_rows):
    half_dim = upstream.shape[-1] // 2
    turned = jnp.concatenate([upstream[..., half_dim:], -upstream[..., :half_dim]], axis=-1)
    return upstream * cosine + turned * sine_rows


def by_head(rows):
    r = rows.reshape(2, 2, SPAN, HH, GROUP, HD)
    return r.transpose(0, 3, 1, 4, 2, 5).reshape(2, HH, 2, QROWS, HD)


def by_token(heads):
    r = heads.reshape(2, HH, 2, GROUP, SPAN, HD)
    return r.transpose(0, 2, 4, 1, 3, 5).reshape(2 * TOK, QH, HD)


def body(layer_input, w_qkv, w_out, w_gate_up, w_down, norm_gains, span_map, cotangent):
    at = here()
    core, low = at["core"], at["l"]
    w_q = w_qkv[:, : HQ * HD].reshape(16, 2, QW).transpose(1, 0, 2)
    w_k = w_qkv[:, HQ * HD : (HQ + HK) * HD].reshape(16, 2, HH, HD)
    w_v = w_qkv[:, (HQ + HK) * HD :].reshape(16, 2, HH, HD)
    w_kv = jnp.concatenate([w_k, w_v], axis=3).reshape(16, 2, KVW).transpose(1, 0, 2)
    gains_row = jnp.pad(norm_gains[None, None, :], ((0, 1), (0, 15), (0, 128 - norm_gains.shape[0])))
    gains_row = jnp.broadcast_to(gains_row[:1], (2, 16, 128))
    shard_one = jnp.concatenate([w_q, w_kv, gains_row], axis=2)
    shard_gate = w_gate_up[:, :FF].reshape(16, 2, FH).transpose(1, 0, 2)
    shard_up = w_gate_up[:, FF:].reshape(16, 2, FH).transpose(1, 0, 2)
    shard_down = w_down.reshape(16, 2, FH).transpose(1, 0, 2)
    shard_out = w_out.reshape(16, 2, QW).transpose(1, 0, 2)

    one_parts = (((0, 384, ORDERS[0]), (384, 384, ORDERS[1]), (768, 512, ORDERS[2])),)
    w_one, x_pair, dy_pair = gather_weights([shard_one], one_parts, [layer_input[0], cotangent[0]], 1)
    w_one = w_one.reshape(D, QW + KVW + 128)
    gain_full = w_one.reshape(128, 16, -1)[:, 0, QW + KVW : QW + KVW + 33].reshape(-1).astype(F32)
    gain_one, gain_two = gain_full[:D], gain_full[D : 2 * D]
    gain_query, gain_key = gain_full[2 * D : 2 * D + HD], gain_full[2 * D + HD :]
    w_joined = w_one[:, : QW + KVW]

    ctx_index = lax.axis_index("ctx")
    maps = lax.dynamic_slice_in_dim(span_map, low * 2, 2, 0)
    own_span = lax.dynamic_slice_in_dim(maps, ctx_index, 1, 1)
    spans = jnp.concatenate([own_span, 2 * N_CTX - 1 - own_span], axis=1)
    positions = (spans[:, :, None] * SPAN + jnp.arange(SPAN, dtype=jnp.int32)).reshape(2 * TOK)
    match = maps[:, None, :] == jnp.arange(N_CTX, dtype=jnp.int32)[None, :, None]
    inverse_map = jnp.sum(jnp.where(match, jnp.arange(N_CTX, dtype=jnp.int32), 0), axis=2)
    tab = jnp.concatenate([inverse_map * 2, inverse_map[:, ::-1] * 2 + 1, own_span], axis=1)
    half_dim = HD // 2
    frequencies = ROPE_BASE ** (-(jnp.arange(half_dim, dtype=F32) * 2.0 / HD))
    angles = positions.astype(F32)[:, None] * frequencies[None, :]
    cosine, sine_rows = jnp.cos(angles), jnp.sin(angles)
    cosine = jnp.concatenate([cosine, cosine], axis=1)[:, None, :]
    sine_rows = jnp.concatenate([sine_rows, sine_rows], axis=1)[:, None, :]

    stream_in = x_pair.reshape(2 * TOK, D).astype(F32)
    dy = dy_pair.reshape(2 * TOK, D)
    normed_one, inverse_one = norm_rows(stream_in, gain_one)
    normed_one = normed_one.astype(BF)
    joined = jnp.dot(normed_one, w_joined, preferred_element_type=F32)
    queries = joined[:, :QW].reshape(2 * TOK, QH, HD)
    kv_raw = joined[:, QW:].reshape(2 * TOK, HH, 2 * HD)
    keys_raw, values_raw = kv_raw[..., :HD], kv_raw[..., HD:]
    query_norm, inverse_query = norm_rows(queries, gain_query)
    key_norm, inverse_key = norm_rows(keys_raw, gain_key)
    query_rot = rotate(query_norm, cosine, sine_rows).astype(BF)
    key_rot = rotate(key_norm, cosine, sine_rows).astype(BF)
    kv_local = jnp.concatenate([key_rot, values_raw.astype(BF)], axis=2).reshape(2 * TOK, KVW)
    kvg = gather_kv(kv_local, 2).reshape(N_CTX, 2 * TOK, KVW)
    q_heads = by_head(query_rot)
    q_pad = jnp.pad(q_heads, ((0, 0),) * 4 + ((0, HD),))
    attn_f32, log_sum = attend(tab, q_pad, kvg)

    two_parts = (
        ((0, FH, ORDERS[0]),),
        ((0, FH, ORDERS[1]),),
        ((0, FH, ORDERS[2]),),
        ((0, 256, ORDERS[0]), (256, 256, ORDERS[1]), (512, 256, ORDERS[2])),
    )
    shards = [shard_gate, shard_up, shard_down, shard_out]
    w_gate, w_up, w_back, w_proj = (w.reshape(D, -1) for w in gather_weights(shards, two_parts, [], 3))

    attn_low = by_token(attn_f32.astype(BF)).reshape(2 * TOK, QW)
    partial_a = lax.dot_general(attn_low, w_proj, NT, preferred_element_type=F32)
    branch_a = partial_a + shift(partial_a, "core")
    middle = stream_in + branch_a
    normed_two, inverse_two = norm_rows(middle, gain_two)
    normed_two = normed_two.astype(BF)
    gate_part = jnp.dot(normed_two, w_gate, preferred_element_type=F32)
    up_part = jnp.dot(normed_two, w_up, preferred_element_type=F32)
    sigmoid_gate = jax.nn.sigmoid(gate_part)
    silu_gate = gate_part * sigmoid_gate
    hidden = (silu_gate * up_part).astype(BF)
    partial_f = lax.dot_general(hidden, w_back, NT, preferred_element_type=F32)
    grad_hidden = jnp.dot(dy, w_back, preferred_element_type=F32)
    grad_gate = (grad_hidden * up_part * sigmoid_gate * (1.0 + gate_part * (1.0 - sigmoid_gate))).astype(BF)
    grad_up = (grad_hidden * silu_gate).astype(BF)
    partial_n = lax.dot_general(grad_gate, w_gate, NT, preferred_element_type=F32)
    partial_n = partial_n + lax.dot_general(grad_up, w_up, NT, preferred_element_type=F32)

    def own_rows(value):
        return lax.dynamic_slice_in_dim(value, core * TOK, TOK, 0)

    def other_rows(value):
        return lax.dynamic_slice_in_dim(value, (1 - core) * TOK, TOK, 0)

    branch_f = own_rows(partial_f) + shift(other_rows(partial_f), "core")
    result = own_rows(middle) + branch_f
    grad_normed_two = partial_n + shift(partial_n, "core")
    back_two, gain_two_terms = norm_back(middle, inverse_two, gain_two, grad_normed_two)
    grad_middle = dy.astype(F32) + back_two
    grad_branch = grad_middle.astype(BF)

    row_gate = sum_at_owner(normed_two, grad_gate, ORDERS[0], at)
    row_up = sum_at_owner(normed_two, grad_up, ORDERS[1], at)
    row_down = sum_at_owner(dy, hidden, ORDERS[2], at)

    grad_attn = jnp.dot(grad_branch, w_proj, preferred_element_type=F32).astype(BF)
    d_heads = by_head(grad_attn.reshape(2 * TOK, QH, HD))
    delta = jnp.sum(d_heads.astype(F32) * attn_f32, axis=-1)[:, :, :, None, :]
    d_pad = jnp.pad(d_heads, ((0, 0),) * 4 + ((HD, 0),))
    qd = jnp.concatenate([q_pad, d_pad], axis=3)
    dq_heads, dkv = attend_back(tab, qd, log_sum, delta, kvg)
    grad_kv = sum_kv(dkv.reshape(2, 4, 4, 2 * TOK, KVW), 4).reshape(2 * TOK, HH, 2 * HD)

    grad_query_raw, query_gain_terms = norm_back(
        queries, inverse_query, gain_query, rotate_back(by_token(dq_heads), cosine, sine_rows)
    )
    grad_key_raw, key_gain_terms = norm_back(
        keys_raw, inverse_key, gain_key, rotate_back(grad_kv[..., :HD], cosine, sine_rows)
    )
    grad_kv_raw = jnp.concatenate([grad_key_raw, grad_kv[..., HD:]], axis=2).reshape(2 * TOK, KVW)
    grad_joined = jnp.concatenate([grad_query_raw.reshape(2 * TOK, QW), grad_kv_raw], axis=1).astype(BF)
    partial_one = lax.dot_general(grad_joined, w_joined, NT, preferred_element_type=F32)
    grad_normed_one = own_rows(partial_one) + shift(other_rows(partial_one), "core")
    back_one, gain_one_terms = norm_back(
        own_rows(stream_in), own_rows(inverse_one), gain_one, grad_normed_one
    )
    grad_input = own_rows(grad_middle) + back_one

    g_qkv = lax.dot_general(normed_one, grad_joined, TN, preferred_element_type=F32).astype(BF)
    g_out = lax.dot_general(grad_branch, attn_low, TN, preferred_element_type=F32).astype(BF)
    own_qkv, own_out = sum_weights(
        g_qkv.reshape(2, 4, 4, 2, 32, QW + KVW), g_out.reshape(2, 4, 4, 2, 32, QW), 5
    )

    def rows_of_half(value):
        mine = lax.dynamic_slice_in_dim(value, core * 16, 16, 0)
        theirs = shift(lax.dynamic_slice_in_dim(value, (1 - core) * 16, 16, 0), "core")
        first = core == 0
        return jnp.where(first, mine, theirs), jnp.where(first, theirs, mine)

    gate_halves = rows_of_half(row_gate)
    up_halves = rows_of_half(row_up)
    down_halves = rows_of_half(row_down)
    grad_mlp = jnp.concatenate([*gate_halves, *up_halves], axis=1)
    grad_down = jnp.concatenate(down_halves, axis=1)
    kv_cols = own_qkv[:, :, QW:].reshape(2, 16, HH, 2, HD)
    grad_qkv = jnp.concatenate(
        [
            own_qkv[0, :, :QW],
            own_qkv[1, :, :QW],
            *(kv_cols[half, :, :, kind].reshape(16, HH * HD) for kind in range(2) for half in range(2)),
        ],
        axis=1,
    )
    grad_proj = jnp.concatenate([own_out[0], own_out[1]], axis=1)

    def mean_root(stream):
        return jnp.sum(jnp.sqrt(jnp.mean(stream * stream, axis=-1)))

    stats = jnp.stack([mean_root(own_rows(s)) for s in (stream_in, branch_a, middle)] + [mean_root(branch_f)])
    sums = jnp.concatenate(
        [
            jnp.sum(gain_one_terms, axis=0),
            jnp.sum(own_rows(gain_two_terms), axis=0),
            jnp.sum(query_gain_terms, axis=(0, 1)),
            jnp.sum(key_gain_terms, axis=(0, 1)),
            stats,
        ]
    )
    sums = jnp.pad(sums, (0, 40 * 128 - sums.shape[0])).reshape(40, 128)
    sums = total_everywhere(sums, 6).reshape(-1)
    share = norm_gains.shape[0]
    own_gains = lax.dynamic_slice_in_dim(sums, lax.axis_index(("ctx", "fsdp")) * share, share, 0)
    stream_rms = sums[4224:4228] / (TOK * N_CTX * 4)
    return (
        result[None].astype(BF),
        grad_input[None].astype(BF),
        grad_qkv,
        grad_proj,
        grad_mlp,
        grad_down,
        own_gains,
        stream_rms,
    )


def solution(mesh):
    rows = P(("ctx", "fsdp"), None)
    tokens = P("fsdp", "ctx", None)
    return jax.shard_map(
        body,
        mesh=mesh,
        in_specs=(tokens, rows, rows, rows, rows, P(("ctx", "fsdp")), P(), tokens),
        out_specs=(tokens, tokens, rows, rows, rows, rows, P(("ctx", "fsdp")), P()),
        check_vma=False,
    )
```

time: 1870 us -> 864 us (0.46)
  waiting for transfers between devices: 1200 us -> 76.4 us
  Pallas kernels: 0 us -> 502 us
  matrix products: 221 us -> 70.5 us
  blocking collectives: 141 us -> 0 us
  other arithmetic: 145 us -> 64.7 us
  starting transfers between devices: 6.47 us -> 57.8 us
  local copies, waits for them, and re-layouts: 128 us -> 84 us
    unnamed x5 -> x0, waiting for transfers between devices: 636 us -> none
    pallas_call x0 -> x8, Pallas kernels: none -> 502 us  [the longest x2 170 us: gather_weights(): pl.pallas_call(functools.partial(weight_kernel, parts, len(pairs), n_in),...]
    all_gather x2 -> x0, waiting for transfers between devices: 395 us -> none  [the longest x1 308 us: side_by_side(): lax.all_gather(both, axis, axis=dim, tiled=True)]
    reduce_scatter x1 -> x0, waiting for transfers between devices: 169 us -> none  [body(): lax.psum_scatter(kv_grad_blocks.reshape(length, 2 * k_width).astype(jnp.b...]
    dot_general x68 -> x24, matrix products: 221 us -> 70.5 us  [the longest x12 17.6 us: product(): lax.dot_general(rows, right, TN, preferred_element_type=F32).astype(BF)]
    ppermute x0 -> x34, waiting for transfers between devices: none -> 76.4 us  [shift(): return lax.ppermute(value, ('ctx', 'fsdp'), permutation(axis, by))]
    psum x1 -> x0, blocking collectives: 71.6 us -> none  [together(): so_far = lax.psum(flat, axis)]
    unnamed x1 -> x0, blocking collectives: 68.9 us -> none
  transfers between devices with their start and end apart: 5 -> 34, of which waited for: 4 -> 7; matrix products, arithmetic and copies ran while one was open for 5% -> 15% of each run, Pallas kernels for 0% -> 28%
where the time goes in v1:
time: 864 us; the launch traced here: 858 us
  Pallas kernels  502 us (58%)
  local copies, waits for them, and re-layouts  84 us (10%)
  waiting for transfers between devices  76.4 us (9%)
  matrix products  70.5 us (8%)
  other arithmetic  64.7 us (7%)
  starting transfers between devices  57.8 us (7%)
    pallas_call x2, Pallas kernels, gather_weights(): pl.pallas_call(functools.partial(weight_kernel, parts, len(pairs), n_in),...  170 us
    pallas_call x1, Pallas kernels, sum_weights(): pl.pallas_call(weight_sum_kernel, out_shape=[jax.ShapeDtypeStruct((2, 16,...  142 us
    ppermute x34, waiting for transfers between devices, shift(): return lax.ppermute(value, ('ctx', 'fsdp'), permutation(axis, by))  76.4 us
    pallas_call x1, Pallas kernels, sum_kv(): pl.pallas_call(kv_sum_kernel, out_shape=jax.ShapeDtypeStruct((2 * TOK, KV...  64.9 us
    ppermute x34, starting transfers between devices, shift(): return lax.ppermute(value, ('ctx', 'fsdp'), permutation(axis, by))  57.8 us
    pallas_call x1, Pallas kernels, gather_kv(): pl.pallas_call(kv_gather_kernel, out_shape=jax.ShapeDtypeStruct((2, 4, 4,...  49.8 us
    pallas_call x1, Pallas kernels, attend_back(): pl.pallas_call(attend_back_kernel, out_shape=[jax.ShapeDtypeStruct((2, HH...  35.2 us
    pallas_call x1, Pallas kernels, attend(): pl.pallas_call(attend_kernel, out_shape=[jax.ShapeDtypeStruct((2, HH, 2,...  25.9 us
  transfers between devices with their start and end apart: 34, of which 7 were waited for; matrix products, arithmetic and copies ran while one was open for 15% of the time, Pallas kernels for 28%

profile of v1, /device:TPU:1, one launch (start us, length us, event | category | flops | bytes accessed | tf_op | source)
XLA Modules:
  0.0 857.9 jit_solution(10671235256444392988)
XLA Ops:
  3.9 40.4 %gather_weights_1.1 = (bf16[2,4,4,2,32,1280]{5,4,3,2,1,0:T(8,128)(2,1)}, bf16[2,128,2048]{2,1,0:T(8,128)(2,1)}, bf16[2,128,2048]{2,1,0:T(8,128)(2,1)}) custom-call(bf16[2,16,1280]{2,1,0:T(8,128)(2,1)} %pad_maximum_fusion.10.refs_0_, bf16[128,2048]{1,0:T(8,128)(2,1)} %bitcast.371, bf16[128,2048]{1,0:T(8,128)(2,1)} %bitcast.372), custom_call_target="tpu_custom_call" | custom-call | tf_op jit(solution)/shard_map/gather_weights_1/pallas_call | solution.py:190
  48.1 4.3 fusion.2
  62.4 49.8 %gather_kv.1 = bf16[2,4,4,256,384]{4,3,2,1,0:T(8,128)(2,1)} custom-call(bf16[256,384]{1,0:T(8,128)(2,1)} %copy.82.src), custom_call_target="tpu_custom_call" | custom-call | tf_op jit(solution)/shard_map/gather_kv/pallas_call | solution.py:218
  120.7 4.1 fusion.11
  126.0 25.9 %attend.1 = (f32[2,3,2,256,64]{4,3,2,1,0:T(8,128)S(1)}, f32[2,3,2,1,256]{4,3,2,1,0:T(1,128)S(1)}) custom-call(s32[2,65]{1,0:T(2,128)S(1)} %pad_add_fusion.tab, bf16[2,3,2,256,128]{4,3,2,1,0:T(8,128)(2,1)S(1)} %pad.17.q_ref, bf16[32,256,384]{2,1,0:T(8,128)(2,1)} %bitcast.333), custom_call_target="tpu_custom_call" | custom-call | flops 20000000000 | bytes 20000000 | tf_op jit(solution)/shard_map/attend/pallas_call | solution.py:513
  161.2 129.8 %gather_weights_3.1 = (bf16[2,4,4,2,32,2176]{5,4,3,2,1,0:T(8,128)(2,1)}, bf16[2,4,4,2,32,2176]{5,4,3,2,1,0:T(8,128)(2,1)}, bf16[2,4,4,2,32,2176]{5,4,3,2,1,0:T(8,128)(2,1)}, bf16[2,4,4,2,32,768]{5,4,3,2,1,0:T(8,128)(2,1)}) custom-call(bf16[2,16,2176]{2,1,0:T(8,128)(2,1)} %bitcast.368, bf16[2,16,2176]{2,1,0:T(8,128)(2,1)} %get-tuple-element.138.refs_1_, ...), custom_call_target="tpu_custom_call" | custom-call | tf_op jit(solution)/shard_map/gather_weights_3/pallas_call | solution.py:190
  291.0 4.4 fusion.59
  295.4 4.2 collective-permute-start
  311.7 3.7 copy.113
  320.5 7.6 fusion.62
  328.1 3.9 multiply_reduce_fusion.1
  336.2 6.6 fusion.60
  342.8 7.1 multiply_convert_fusion
  349.9 5.2 fusion.63
  357.9 5.3 fusion.61
  403.0 35.2 %attend_back.1 = (f32[2,3,2,256,64]{4,3,2,1,0:T(8,128)S(1)}, bf16[32,256,384]{2,1,0:T(8,128)(2,1)}) custom-call(s32[2,65]{1,0:T(2,128)S(1)} %pad_add_fusion.tab, bf16[2,3,2,512,128]{4,3,2,1,0:T(8,128)(2,1)S(1)} %fusion.6.qd_ref, f32[2,3,2,1,256]{4,3,2,1,0:T(1,128)S(1)} %get-tuple-element.29.l_ref, f32[2,3,2,1,256]{4,3,2,1,0:T(1,128)S(1)} %broadcast_in_dim.21.delta_ref, ...), custom_call_target="tpu_custom_call" | custom-call | flops 49999998976 | bytes 30000000 | tf_op jit(solution)/shard_map/attend_back/pallas_call | solution.py:595
  441.8 64.9 %sum_kv.1 = f32[256,384]{1,0:T(8,128)S(1)} custom-call(bf16[2,4,4,256,384]{4,3,2,1,0:T(8,128)(2,1)} %bitcast.335), custom_call_target="tpu_custom_call" | custom-call | tf_op jit(solution)/shard_map/sum_kv/pallas_call | solution.py:338
  520.2 3.8 convolution_convert_fusion
  527.5 142.0 %sum_weights.1 = (f32[2,16,1152]{2,1,0:T(8,128)S(1)}, f32[2,16,768]{2,1,0:T(8,128)S(1)}) custom-call(bf16[2,4,4,2,32,1152]{5,4,3,2,1,0:T(8,128)(2,1)} %bitcast.312, bf16[2,4,4,2,32,768]{5,4,3,2,1,0:T(8,128)(2,1)S(1)} %bitcast.310), custom_call_target="tpu_custom_call" | custom-call | tf_op jit(solution)/shard_map/sum_weights/pallas_call | solution.py:391
  672.6 3.5 multiply_reduce_fusion.4
  678.6 4.0 fusion
  684.4 5.2 fusion.18
  692.2 5.5 fusion.12
  697.7 23.7 %collective-permute-done.14 = bf16[2,4,2,32,2176]{4,3,1,2,0:T(8,128)(2,1)} collective-permute-done((bf16[2,4,2,32,2176]{4,3,1,2,0:T(8,128)(2,1)}, bf16[2,4,2,32,2176]{4,3,1,2,0:T(8,128)(2,1)}, u32[]{:S(2)}, u32[]{:S(2)}) %collective-permute-start.14) | collective-permute-done | bytes 2228256 | tf_op jit(solution)/shard_map/ppermute | solution.py:636
  729.6 40.4 %collective-permute-done.16 = bf16[2,4,2,32,2176]{4,3,1,2,0:T(8,128)(2,1)} collective-permute-done((bf16[2,4,2,32,2176]{4,3,1,2,0:T(8,128)(2,1)}, bf16[2,4,2,32,2176]{4,3,1,2,0:T(8,128)(2,1)}, u32[]{:S(2)}, u32[]{:S(2)}) %collective-permute-start.16) | collective-permute-done | bytes 2228256 | tf_op jit(solution)/shard_map/ppermute | solution.py:636
  772.3 4.0 fusion.15
  777.6 8.9 %collective-permute-start.18 = (bf16[4,32,2176]{2,1,0:T(8,128)(2,1)S(1)}, bf16[4,32,2176]{2,1,0:T(8,128)(2,1)S(1)}, u32[]{:S(2)}, u32[]{:S(2)}) collective-permute-start(bf16[4,32,2176]{2,1,0:T(8,128)(2,1)S(1)} %get-tuple-element.65), channel_id=1, source_target_pairs={{0,66},{1,67},{2,0},{3,1},{4,70},{5,71},{6,4},{7,5},{8,74},{9,75},... | collective-permute-start | bytes 1671176 | tf_op jit(solution)/shard_map/ppermute | solution.py:636
  797.5 3.7 collective-permute-start.31
  801.2 7.8 collective-permute-done.18
  811.1 3.6 collective-permute-start.11
  821.0 3.9 collective-permute-start.33
  837.8 14.3 %total_everywhere.1 = f32[40,128]{1,0:T(8,128)} custom-call(f32[40,128]{1,0:T(8,128)} %pad_bitcast_fusion.x_ref), custom_call_target="tpu_custom_call" | custom-call | tf_op jit(solution)/shard_map/total_everywhere/pallas_call | solution.py:440
  (375 shorter events, 179.1 us)
Async XLA Ops:
  295.4 32.7 %collective-permute-start = (f32[256,2048]{1,0:T(8,128)}, f32[256,2048]{1,0:T(8,128)}, u32[]{:S(2)}, u32[]{:S(2)}) collective-permute-start(f32[256,2048]{1,0:T(8,128)} %fusion.59), channel_id=1, source_target_pairs={{0,1},{1,0},{2,3},{3,2},{4,5},{5,4},{6,7},{7,6},{8,9},{9,8},{10,11... | collective-permute-start | bytes 6291464 | tf_op jit(solution)/shard_map/ppermute | solution.py:636
  357.8 38.6 %collective-permute-start.2 = (f32[256,2048]{1,0:T(8,128)S(1)}, f32[256,2048]{1,0:T(8,128)S(1)}, u32[]{:S(2)}, u32[]{:S(2)}) collective-permute-start(f32[256,2048]{1,0:T(8,128)S(1)} %convolution_add_fusion), channel_id=1, source_target_pairs={{0,1},{1,0},{2,3},{3,2},{4,5},{5,4},{6,7},{7,6},{8,9},{9,8},{10,11... | collective-permute-start | bytes 6291464 | tf_op jit(solution)/shard_map/ppermute | solution.py:636
  364.3 159.7 %collective-permute-start.1 = (f32[128,2048]{1,0:T(8,128)}, f32[128,2048]{1,0:T(8,128)}, u32[]{:S(2)}, u32[]{:S(2)}) collective-permute-start(f32[128,2048]{1,0:T(8,128)} %constant_dynamic-slice_fusion.17), channel_id=1, source_target_pairs={{0,1},{1,0},{2,3},{3,2},{4,5},{5,4},{6,7},{7,6},{8,9},{9,8},{10,11... | collective-permute-start | bytes 3145736 | tf_op jit(solution)/shard_map/ppermute | solution.py:636
  367.0 158.8 %collective-permute-start.24 = (bf16[4,4,32,2176]{3,2,1,0:T(8,128)(2,1)}, bf16[4,4,32,2176]{3,2,1,0:T(8,128)(2,1)}, u32[]{:S(2)}, u32[]{:S(2)}) collective-permute-start(bf16[4,4,32,2176]{3,2,1,0:T(8,128)(2,1)} %bitcast.91), channel_id=1, source_target_pairs={{0,2},{1,3},{2,64},{3,65},{4,6},{5,7},{6,68},{7,69},{8,10},{9,11},... | collective-permute-start | bytes 6684680 | tf_op jit(solution)/shard_map/ppermute | solution.py:636
  369.2 300.5 %collective-permute-start.25 = (bf16[4,4,32,2176]{3,2,1,0:T(8,128)(2,1)}, bf16[4,4,32,2176]{3,2,1,0:T(8,128)(2,1)}, u32[]{:S(2)}, u32[]{:S(2)}) collective-permute-start(bf16[4,4,32,2176]{3,2,1,0:T(8,128)(2,1)} %bitcast.93), channel_id=1, source_target_pairs={{0,66},{1,67},{2,0},{3,1},{4,70},{5,71},{6,4},{7,5},{8,74},{9,75},... | collective-permute-start | bytes 6684680 | tf_op jit(solution)/shard_map/ppermute | solution.py:636
  374.0 297.4 %collective-permute-start.26 = (bf16[4,4,32,2176]{3,2,1,0:T(8,128)(2,1)}, bf16[4,4,32,2176]{3,2,1,0:T(8,128)(2,1)}, u32[]{:S(2)}, u32[]{:S(2)}) collective-permute-start(bf16[4,4,32,2176]{3,2,1,0:T(8,128)(2,1)} %bitcast.95), channel_id=1, source_target_pairs={{0,64},{1,65},{2,66},{3,67},{4,68},{5,69},{6,70},{7,71},{8,72},{9,... | collective-permute-start | bytes 6684680 | tf_op jit(solution)/shard_map/ppermute | solution.py:636
  396.4 279.7 %collective-permute-start.4 = (bf16[2,4,2,32,2176]{4,3,2,0,1:T(8,128)(2,1)}, bf16[2,4,2,32,2176]{4,3,2,0,1:T(8,128)(2,1)}, u32[]{:S(2)}, u32[]{:S(2)}) collective-permute-start(bf16[2,4,2,32,2176]{4,3,2,0,1:T(8,128)(2,1)} %copy.99), channel_id=1, source_target_pairs={{0,16},{1,17},{2,18},{3,19},{4,20},{5,21},{6,22},{7,23},{8,24},{9,... | collective-permute-start | bytes 6684680 | tf_op jit(solution)/shard_map/ppermute | solution.py:636
  524.0 165.6 %collective-permute-start.5 = (bf16[2,4,2,32,2176]{4,3,2,0,1:T(8,128)(2,1)}, bf16[2,4,2,32,2176]{4,3,2,0,1:T(8,128)(2,1)}, u32[]{:S(2)}, u32[]{:S(2)}) collective-permute-start(bf16[2,4,2,32,2176]{4,3,2,0,1:T(8,128)(2,1)} %copy.100), channel_id=1, source_target_pairs={{0,48},{1,49},{2,50},{3,51},{4,52},{5,53},{6,54},{7,55},{8,56},{9,... | collective-permute-start | bytes 6684680 | tf_op jit(solution)/shard_map/ppermute | solution.py:636
  525.8 164.9 %collective-permute-start.6 = (bf16[2,4,2,32,2176]{4,3,2,0,1:T(8,128)(2,1)}, bf16[2,4,2,32,2176]{4,3,2,0,1:T(8,128)(2,1)}, u32[]{:S(2)}, u32[]{:S(2)}) collective-permute-start(bf16[2,4,2,32,2176]{4,3,2,0,1:T(8,128)(2,1)} %copy.101), channel_id=1, source_target_pairs={{0,32},{1,33},{2,34},{3,35},{4,36},{5,37},{6,38},{7,39},{8,40},{9,... | collective-permute-start | bytes 6684680 | tf_op jit(solution)/shard_map/ppermute | solution.py:636
  669.7 51.7 %collective-permute-start.14 = (bf16[2,4,2,32,2176]{4,3,1,2,0:T(8,128)(2,1)}, bf16[2,4,2,32,2176]{4,3,1,2,0:T(8,128)(2,1)}, u32[]{:S(2)}, u32[]{:S(2)}) collective-permute-start(bf16[2,4,2,32,2176]{4,3,1,2,0:T(8,128)(2,1)} %copy.106), channel_id=1, source_target_pairs={{0,4},{1,5},{2,6},{3,7},{4,8},{5,9},{6,10},{7,11},{8,12},{9,13},{1... | collective-permute-start | bytes 6684680 | tf_op jit(solution)/shard_map/ppermute | solution.py:636
  671.4 51.7 %collective-permute-start.15 = (bf16[2,4,2,32,2176]{4,3,1,2,0:T(8,128)(2,1)}, bf16[2,4,2,32,2176]{4,3,1,2,0:T(8,128)(2,1)}, u32[]{:S(2)}, u32[]{:S(2)}) collective-permute-start(bf16[2,4,2,32,2176]{4,3,1,2,0:T(8,128)(2,1)} %copy.107), channel_id=1, source_target_pairs={{0,12},{1,13},{2,14},{3,15},{4,0},{5,1},{6,2},{7,3},{8,4},{9,5},{1... | collective-permute-start | bytes 6684680 | tf_op jit(solution)/shard_map/ppermute | solution.py:636
  676.1 93.9 %collective-permute-start.16 = (bf16[2,4,2,32,2176]{4,3,1,2,0:T(8,128)(2,1)}, bf16[2,4,2,32,2176]{4,3,1,2,0:T(8,128)(2,1)}, u32[]{:S(2)}, u32[]{:S(2)}) collective-permute-start(bf16[2,4,2,32,2176]{4,3,1,2,0:T(8,128)(2,1)} %copy.108), channel_id=1, source_target_pairs={{0,8},{1,9},{2,10},{3,11},{4,12},{5,13},{6,14},{7,15},{8,0},{9,1},... | collective-permute-start | bytes 6684680 | tf_op jit(solution)/shard_map/ppermute | solution.py:636
  689.5 81.9 %collective-permute-start.27 = (bf16[4,32,2176]{2,1,0:T(8,128)(2,1)}, bf16[4,32,2176]{2,1,0:T(8,128)(2,1)}, u32[]{:S(2)}, u32[]{:S(2)}) collective-permute-start(bf16[4,32,2176]{2,1,0:T(8,128)(2,1)} %get-tuple-element.55), channel_id=1, source_target_pairs={{0,16},{1,17},{2,18},{3,19},{4,20},{5,21},{6,22},{7,23},{8,24},{9,... | collective-permute-start | bytes 1671176 | tf_op jit(solution)/shard_map/ppermute | solution.py:636
  690.7 85.6 %collective-permute-start.28 = (bf16[4,32,2176]{2,1,0:T(8,128)(2,1)}, bf16[4,32,2176]{2,1,0:T(8,128)(2,1)}, u32[]{:S(2)}, u32[]{:S(2)}) collective-permute-start(bf16[4,32,2176]{2,1,0:T(8,128)(2,1)} %get-tuple-element.58), channel_id=1, source_target_pairs={{0,48},{1,49},{2,50},{3,51},{4,52},{5,53},{6,54},{7,55},{8,56},{9,... | collective-permute-start | bytes 1671176 | tf_op jit(solution)/shard_map/ppermute | solution.py:636
  721.4 56.2 %collective-permute-start.29 = (bf16[4,32,2176]{2,1,0:T(8,128)(2,1)}, bf16[4,32,2176]{2,1,0:T(8,128)(2,1)}, u32[]{:S(2)}, u32[]{:S(2)}) collective-permute-start(bf16[4,32,2176]{2,1,0:T(8,128)(2,1)} %get-tuple-element.57), channel_id=1, source_target_pairs={{0,32},{1,33},{2,34},{3,35},{4,36},{5,37},{6,38},{7,39},{8,40},{9,... | collective-permute-start | bytes 1671176 | tf_op jit(solution)/shard_map/ppermute | solution.py:636
  723.1 63.4 %collective-permute-start.7 = (bf16[2,2,32,2176]{3,2,1,0:T(8,128)(2,1)}, bf16[2,2,32,2176]{3,2,1,0:T(8,128)(2,1)}, u32[]{:S(2)}, u32[]{:S(2)}) collective-permute-start(bf16[2,2,32,2176]{3,2,1,0:T(8,128)(2,1)} %get-tuple-element.59), channel_id=1, source_target_pairs={{0,4},{1,5},{2,6},{3,7},{4,8},{5,9},{6,10},{7,11},{8,12},{9,13},{1... | collective-permute-start | bytes 1671176 | tf_op jit(solution)/shard_map/ppermute | solution.py:636
  770.0 19.2 %collective-permute-start.8 = (bf16[2,2,32,2176]{3,2,1,0:T(8,128)(2,1)}, bf16[2,2,32,2176]{3,2,1,0:T(8,128)(2,1)S(1)}, u32[]{:S(2)}, u32[]{:S(2)}) collective-permute-start(bf16[2,2,32,2176]{3,2,1,0:T(8,128)(2,1)} %get-tuple-element.61), channel_id=1, source_target_pairs={{0,12},{1,13},{2,14},{3,15},{4,0},{5,1},{6,2},{7,3},{8,4},{9,5},{1... | collective-permute-start | bytes 1671176 | tf_op jit(solution)/shard_map/ppermute | solution.py:636
  771.5 22.3 %collective-permute-start.9 = (bf16[2,2,32,2176]{3,2,1,0:T(8,128)(2,1)}, bf16[2,2,32,2176]{3,2,1,0:T(8,128)(2,1)S(1)}, u32[]{:S(2)}, u32[]{:S(2)}) collective-permute-start(bf16[2,2,32,2176]{3,2,1,0:T(8,128)(2,1)} %get-tuple-element.60), channel_id=1, source_target_pairs={{0,8},{1,9},{2,10},{3,11},{4,12},{5,13},{6,14},{7,15},{8,0},{9,1},... | collective-permute-start | bytes 1671176 | tf_op jit(solution)/shard_map/ppermute | solution.py:636
  776.3 21.1 %collective-permute-start.17 = (bf16[4,32,2176]{2,1,0:T(8,128)(2,1)S(1)}, bf16[4,32,2176]{2,1,0:T(8,128)(2,1)S(1)}, u32[]{:S(2)}, u32[]{:S(2)}) collective-permute-start(bf16[4,32,2176]{2,1,0:T(8,128)(2,1)S(1)} %get-tuple-element.63), channel_id=1, source_target_pairs={{0,2},{1,3},{2,64},{3,65},{4,6},{5,7},{6,68},{7,69},{8,10},{9,11},... | collective-permute-start | bytes 1671176 | tf_op jit(solution)/shard_map/ppermute | solution.py:636
  777.6 31.4 %collective-permute-start.18 = (bf16[4,32,2176]{2,1,0:T(8,128)(2,1)S(1)}, bf16[4,32,2176]{2,1,0:T(8,128)(2,1)S(1)}, u32[]{:S(2)}, u32[]{:S(2)}) collective-permute-start(bf16[4,32,2176]{2,1,0:T(8,128)(2,1)S(1)} %get-tuple-element.65), channel_id=1, source_target_pairs={{0,66},{1,67},{2,0},{3,1},{4,70},{5,71},{6,4},{7,5},{8,74},{9,75},... | collective-permute-start | bytes 1671176 | tf_op jit(solution)/shard_map/ppermute | solution.py:636
  786.5 24.2 %collective-permute-start.19 = (bf16[4,32,2176]{2,1,0:T(8,128)(2,1)S(1)}, bf16[4,32,2176]{2,1,0:T(8,128)(2,1)S(1)}, u32[]{:S(2)}, u32[]{:S(2)}) collective-permute-start(bf16[4,32,2176]{2,1,0:T(8,128)(2,1)S(1)} %get-tuple-element.64), channel_id=1, source_target_pairs={{0,64},{1,65},{2,66},{3,67},{4,68},{5,69},{6,70},{7,71},{8,72},{9,... | collective-permute-start | bytes 1671176 | tf_op jit(solution)/shard_map/ppermute | solution.py:636
  789.2 43.8 %collective-permute-start.3 = (f32[128,2048]{1,0:T(8,128)S(1)}, f32[128,2048]{1,0:T(8,128)S(1)}, u32[]{:S(2)}, u32[]{:S(2)}) collective-permute-start(f32[128,2048]{1,0:T(8,128)S(1)} %copy-done.38), channel_id=1, source_target_pairs={{0,1},{1,0},{2,3},{3,2},{4,5},{5,4},{6,7},{7,6},{8,9},{9,8},{10,11... | collective-permute-start | bytes 3145736 | tf_op jit(solution)/shard_map/ppermute | solution.py:636
  793.8 17.3 %collective-permute-start.30 = (bf16[32,2176]{1,0:T(8,128)(2,1)S(1)}, bf16[32,2176]{1,0:T(8,128)(2,1)S(1)}, u32[]{:S(2)}, u32[]{:S(2)}) collective-permute-start(bf16[32,2176]{1,0:T(8,128)(2,1)S(1)} %get-tuple-element.74), channel_id=1, source_target_pairs={{0,4},{1,5},{2,6},{3,7},{4,8},{5,9},{6,10},{7,11},{8,12},{9,13},{1... | collective-permute-start | bytes 417800 | tf_op jit(solution)/shard_map/ppermute | solution.py:636
  797.5 17.2 %collective-permute-start.31 = (bf16[32,2176]{1,0:T(8,128)(2,1)S(1)}, bf16[32,2176]{1,0:T(8,128)(2,1)S(1)}, u32[]{:S(2)}, u32[]{:S(2)}) collective-permute-start(bf16[32,2176]{1,0:T(8,128)(2,1)S(1)} %get-tuple-element.76), channel_id=1, source_target_pairs={{0,12},{1,13},{2,14},{3,15},{4,0},{5,1},{6,2},{7,3},{8,4},{9,5},{1... | collective-permute-start | bytes 417800 | tf_op jit(solution)/shard_map/ppermute | solution.py:636
  809.0 6.9 collective-permute-start.32
  810.7 6.8 collective-permute-start.10
  811.1 8.8 %collective-permute-start.11 = (bf16[32,2176]{1,0:T(8,128)(2,1)S(1)}, bf16[32,2176]{1,0:T(8,128)(2,1)S(1)}, u32[]{:S(2)}, u32[]{:S(2)}) collective-permute-start(bf16[32,2176]{1,0:T(8,128)(2,1)S(1)} %get-tuple-element.79), channel_id=1, source_target_pairs={{0,66},{1,67},{2,0},{3,1},{4,70},{5,71},{6,4},{7,5},{8,74},{9,75},... | collective-permute-start | bytes 417800 | tf_op jit(solution)/shard_map/ppermute | solution.py:636
  814.7 6.3 collective-permute-start.12
  816.0 9.9 %collective-permute-start.20 = (bf16[32,2176]{1,0:T(8,128)(2,1)S(1)}, bf16[32,2176]{1,0:T(8,128)(2,1)S(1)}, u32[]{:S(2)}, u32[]{:S(2)}) collective-permute-start(bf16[32,2176]{1,0:T(8,128)(2,1)S(1)} %get-tuple-element.80), channel_id=1, source_target_pairs={{0,16},{1,17},{2,18},{3,19},{4,20},{5,21},{6,22},{7,23},{8,24},{9,... | collective-permute-start | bytes 417800 | tf_op jit(solution)/shard_map/ppermute | solution.py:636
  817.6 9.2 %collective-permute-start.21 = (bf16[32,2176]{1,0:T(8,128)(2,1)S(1)}, bf16[32,2176]{1,0:T(8,128)(2,1)S(1)}, u32[]{:S(2)}, u32[]{:S(2)}) collective-permute-start(bf16[32,2176]{1,0:T(8,128)(2,1)S(1)} %get-tuple-element.82), channel_id=1, source_target_pairs={{0,48},{1,49},{2,50},{3,51},{4,52},{5,53},{6,54},{7,55},{8,56},{9,... | collective-permute-start | bytes 417800 | tf_op jit(solution)/shard_map/ppermute | solution.py:636
  819.9 6.9 collective-permute-start.22
  821.0 9.4 %collective-permute-start.33 = (f32[16,2176]{1,0:T(8,128)S(1)}, f32[16,2176]{1,0:T(8,128)S(1)}, u32[]{:S(2)}, u32[]{:S(2)}) collective-permute-start(f32[16,2176]{1,0:T(8,128)S(1)} %constant_dynamic-slice_fusion.1), channel_id=1, source_target_pairs={{0,1},{1,0},{2,3},{3,2},{4,5},{5,4},{6,7},{7,6},{8,9},{9,8},{10,11... | collective-permute-start | bytes 417800 | tf_op jit(solution)/shard_map/ppermute | solution.py:636
  (74 other events, 1290.2 us)

commit v2 on v1

v2 whole, which is shorter than its diff:
```python
import functools

import jax
import jax.numpy as jnp
from jax import lax
from jax.experimental import pallas as pl
from jax.experimental.pallas import tpu as pltpu
from jax.sharding import PartitionSpec as P

D = 2048
HQ = 24
HK = 6
HD = 64
FF = 4352
TOK = 128
SPAN = 64
N_CTX = 32

HH = HK // 2
GROUP = HQ // HK
QH = HQ // 2
QW = QH * HD
KVW = HH * 2 * HD
FH = FF // 2
KEYS = 512
SPANS_STEP = KEYS // SPAN
FULL_STEPS = 7
QROWS = GROUP * SPAN

EPSILON = 1e-06
ROPE_BASE = 10000.0
LOG2E = 1.4426950408889634
MESH = pl.DeviceIdType.MESH
BF = jnp.bfloat16
F32 = jnp.float32
NT = (((1,), (1,)), ((), ()))
NN = (((1,), (0,)), ((), ()))
TN = (((0,), (0,)), ((), ()))
W_DIMS = ("h", "x", "y", "l")
KV_DIMS = ("h", "x", "y")
ORDERS = (("x", "y", "z"), ("y", "z", "x"), ("z", "x", "y"))
KV_ORDERS = (("h", "x", "y"), ("x", "y", "h"), ("y", "h", "x"))
KV_SUM_ORDERS = (("y", "x", "h"), ("h", "y", "x"), ("x", "h", "y"))
SUMS = (
    (0, 0, 1152, ORDERS[0]),
    (1, 0, 1152, ORDERS[1]),
    (2, 0, 1152, ORDERS[2]),
    (0, 1152, 1024, ORDERS[0]),
    (1, 1152, 1024, ORDERS[1]),
    (2, 1152, 1024, ORDERS[2]),
    (4, 0, 384, ORDERS[0]),
    (4, 384, 384, ORDERS[1]),
    (4, 768, 384, ORDERS[2]),
    (3, 0, 256, ORDERS[0]),
    (3, 256, 256, ORDERS[1]),
    (3, 512, 256, ORDERS[2]),
)
SIZES = {"x": 4, "y": 4, "z": 4, "h": 2}


def here():
    c = lax.axis_index("ctx")
    f = lax.axis_index("fsdp")
    return {
        "x": lax.rem(lax.div(c, 4), 4),
        "y": lax.rem(c, 4),
        "z": lax.div(c, 16) * 2 + lax.div(f, 2),
        "h": lax.div(c, 16),
        "l": lax.div(f, 2),
        "core": lax.rem(f, 2),
    }


def device_of(x, y, z, core):
    return (lax.div(z, 2) * 16 + x * 4 + y, lax.rem(z, 2) * 2 + core)


def moved(at, axis, by):
    if axis == "core":
        return device_of(at["x"], at["y"], at["z"], 1 - at["core"])
    place = {k: at[k] for k in ("x", "y", "z")}
    if axis == "h":
        place["z"] = lax.rem(at["z"] + 2, 4)
    else:
        place[axis] = lax.rem(at[axis] + by + 4, 4)
    return device_of(place["x"], place["y"], place["z"], at["core"])


def labels(axis, value):
    if axis == "z":
        return {"h": lax.div(value, 2), "l": lax.rem(value, 2)}
    return {axis: value}


def pick(ref, dims, values, tail):
    return ref.at[tuple(values[d] if d in values else slice(None) for d in dims) + tail]


def greet(devices):
    barrier = pltpu.get_barrier_semaphore()
    for d in devices:
        pl.semaphore_signal(barrier, inc=1, device_id=d, device_id_type=MESH)
    pl.semaphore_wait(barrier, len(devices))


def send(src, dst, ssem, rsem, device):
    copy = pltpu.make_async_remote_copy(
        src_ref=src, dst_ref=dst, send_sem=ssem, recv_sem=rsem, device_id=device, device_id_type=MESH
    )
    copy.start()
    return copy


class Gathering:
    def __init__(self, ref, dims, at, order, rows, cols, ssem, rsem):
        self.ref, self.dims, self.at, self.order, self.rows, self.cols = ref, dims, at, order, rows, cols
        self.ssem, self.rsem, self.phase, self.sent = ssem, rsem, 0, []

    def block(self, coordinate, rows):
        later = {}
        for a in self.order[self.phase + 1 :]:
            later.update(labels(a, self.at[a]))
        return pick(self.ref, self.dims, {**later, **labels(self.axis, coordinate)}, (rows, self.cols))

    def send(self, n, ref, by):
        c = send(ref, ref, self.ssem.at[self.phase, n], self.rsem.at[self.phase, n], moved(self.at, self.axis, by))
        self.sent.append(c)
        return c

    def start(self):
        self.axis = self.order[self.phase]
        mine = self.block(self.at[self.axis], slice(None))
        self.first = [self.send(0, mine, 1)]
        if SIZES[self.axis] == 4:
            self.first.append(self.send(1, mine, 3))

    def pass_on(self):
        for c in self.first:
            c.wait_recv()
        self.second = []
        if SIZES[self.axis] == 4:
            half = self.rows // 2
            me = self.at[self.axis]
            self.second.append(self.send(2, self.block(lax.rem(me + 3, 4), pl.ds(0, half)), 1))
            self.second.append(self.send(3, self.block(lax.rem(me + 1, 4), pl.ds(half, half)), 3))

    def finish(self):
        for c in self.second:
            c.wait_recv()
        self.phase += 1

    def wait_sent(self):
        for c in self.sent:
            c.wait_send()


def neighbours(at, axes):
    out = []
    for a in axes:
        if a in ("core", "h"):
            out.append(moved(at, a, 1))
        else:
            out.append(moved(at, a, 1))
            out.append(moved(at, a, 3))
    return out


GATHER = (
    (0, 0, 1152, ORDERS[0]),
    (1, 0, 1152, ORDERS[1]),
    (2, 0, 1152, ORDERS[2]),
    (0, 1152, 1024, ORDERS[0]),
    (1, 1152, 1024, ORDERS[1]),
    (2, 1152, 1024, ORDERS[2]),
    (3, 0, 256, ORDERS[0]),
    (3, 256, 256, ORDERS[1]),
    (3, 512, 256, ORDERS[2]),
)


def lane_of(shape):
    return lax.broadcasted_iota(jnp.int32, shape, len(shape) - 1)


def swap_halves(v):
    return jnp.where(lax.rem(lane_of(v.shape), HD) < HD // 2, pltpu.roll(v, 96, 1), pltpu.roll(v, 32, 1))


def head_sums(v):
    low = lane_of(v.shape) < HD
    a = jnp.sum(jnp.where(low, v, 0.0), axis=1, keepdims=True)
    b = jnp.sum(jnp.where(low, 0.0, v), axis=1, keepdims=True)
    return jnp.where(low, a, b)


def tile_gain(row, is_key):
    low = lane_of(row.shape) < HD
    turned = pltpu.roll(row, HD, 1)
    return jnp.where(low, turned, 1.0) if is_key else jnp.where(low, row, turned)


def front_kernel(
    shard_one, shard_gate, shard_up, shard_down, shard_out, x, dy, gains, cosine, sine,
    w_one, w_gate, w_up, w_down, w_out, x_pair, dy_pair, gain_all, joined, normed, query, kvg,
    one, kv_src, small_buf, psem, lsem, tssem, trsem, ossem, orsem, gssem, grsem, kssem, krsem, ksem,
):
    at = here()
    core = at["core"]
    sibling = moved(at, "core", 1)
    greet([sibling] + sum_peers(at, ("x", "y", "z")))
    own = {d: at[d] for d in W_DIMS}
    total = Total(gains[...], at, small_buf, tssem, trsem)
    remote, local = [], []
    pairs = [(shard_one, one), (shard_gate, w_gate), (shard_up, w_up), (shard_down, w_down), (shard_out, w_out)]
    for i, (src, ref) in enumerate(pairs):
        dst = pick(ref, W_DIMS, own, (pl.ds(core * 16, 16), slice(None)))
        remote.append(send(src.at[1 - core], dst, psem.at[i, 0], psem.at[i, 1], sibling))
        local.append(pltpu.make_async_copy(src.at[core], dst, lsem.at[i]))
        local[-1].start()
    for i, (src, ref) in ((5, (x, x_pair)), (6, (dy, dy_pair))):
        remote.append(send(src, ref.at[core], psem.at[i, 0], psem.at[i, 1], sibling))
        local.append(pltpu.make_async_copy(src, ref.at[core], lsem.at[i]))
        local[-1].start()

    def arrived(i):
        remote[i].wait_recv()
        local[i].wait()

    ones = [
        Gathering(one, W_DIMS, at, ORDERS[k], 32, pl.ds(k * 384, 384), ossem.at[k], orsem.at[k]) for k in range(3)
    ]
    rest = [
        Gathering(pairs[1 + a][1], W_DIMS, at, order, 32, pl.ds(start, width), gssem.at[k], grsem.at[k])
        for k, (a, start, width, order) in enumerate(GATHER)
    ]
    kvs = [
        Gathering(kvg.at[h], KV_DIMS, at, KV_ORDERS[h], 2 * TOK, slice(None), kssem.at[h], krsem.at[h]) for h in range(HH)
    ]

    def every(streams, *steps):
        for s in streams:
            for step in steps:
                getattr(s, step)()

    arrived(0)
    every(ones, "start")
    for i in range(1, 5):
        arrived(i)
    every(rest, "start")
    total.step()
    every(ones, "pass_on")
    every(rest, "pass_on")
    total.step()
    every(ones, "finish", "start")
    every(rest, "finish")
    total.step()
    every(ones, "pass_on")
    total.step()
    gain_all[...] = total.value
    every(ones, "finish", "start")
    every(rest, "start")
    arrived(5)
    gain_row = jnp.concatenate([total.value[j : j + 1] for j in range(D // 128)], axis=1)

    def norm(r, carry):
        rows = pl.ds(pl.multiple_of(r * 32, 32), 32)
        for s in range(2):
            v = x_pair[s, rows, :].astype(F32)
            inverse = lax.rsqrt(jnp.sum(v * v, axis=1, keepdims=True) * (1.0 / D) + EPSILON)
            normed[pl.ds(pl.multiple_of(s * TOK + r * 32, 32), 32), :] = (v * inverse * gain_row).astype(BF)
        return carry

    lax.fori_loop(0, TOK // 32, norm, 0)
    every(ones, "pass_on")
    every(ones, "finish")
    keep = pltpu.make_async_copy(one, w_one, lsem.at[7])
    keep.start()
    head_gains = total.value[32:33]

    def product(start, width):
        w = one[:, :, :, :, :, start : start + width].reshape(D, width)
        joined[:, start : start + width] = jnp.dot(normed[...], w, preferred_element_type=F32)

    def rope(tile, is_key):
        v = joined[:, tile * 128 : (tile + 1) * 128]
        low = lane_of(v.shape) < HD
        c, n = cosine[...], sine[...]
        inverse = lax.rsqrt(head_sums(v * v) * (1.0 / HD) + EPSILON)
        if is_key:
            inverse = jnp.where(low, inverse, 1.0)
            c, n = jnp.where(low, c, 1.0), jnp.where(low, n, 0.0)
        v = v * inverse * tile_gain(head_gains, is_key)
        return (v * c + swap_halves(v) * n).astype(BF)

    product(QW, KVW)
    for h in range(HH):
        kv_src[h] = rope(QW // 128 + h, True)
    kv_own = {d: at[d] for d in KV_DIMS}
    puts = [pltpu.make_async_copy(kv_src.at[h], pick(kvg.at[h], KV_DIMS, kv_own, ()), ksem.at[h]) for h in range(HH)]
    for c in puts:
        c.start()
    for c in puts:
        c.wait()
    every(kvs, "start")
    every(rest, "pass_on")
    product(0, 384)
    every(kvs, "pass_on")
    every(rest, "finish", "start")
    product(384, 384)
    every(kvs, "finish", "start")
    for t in range(QW // 128):
        query[:, t * 128 : (t + 1) * 128] = rope(t, False)
    every(kvs, "pass_on")
    every(kvs, "finish", "start")
    every(rest[:3], "pass_on")
    every(kvs, "pass_on")
    every(rest[3:], "pass_on")
    every(kvs, "finish")
    every(rest, "finish")
    arrived(6)
    keep.wait()
    for c in remote + total.sent:
        c.wait_send()
    for s in ones + rest + kvs:
        s.wait_sent()


def front(shards, x, dy, gains, cosine, sine, cid):
    anywhere = pl.BlockSpec(memory_space=pl.ANY)
    vmem = pl.BlockSpec(memory_space=pltpu.VMEM)
    full = [jax.ShapeDtypeStruct((2, 4, 4, 2, 32, s.shape[-1]), BF) for s in shards]
    n = len(GATHER)
    return pl.pallas_call(
        front_kernel,
        out_shape=full
        + [
            jax.ShapeDtypeStruct((2,) + x.shape, BF),
            jax.ShapeDtypeStruct((2,) + dy.shape, BF),
            jax.ShapeDtypeStruct(gains.shape, F32),
            jax.ShapeDtypeStruct((2 * TOK, QW + KVW), F32),
            jax.ShapeDtypeStruct((2 * TOK, D), BF),
            jax.ShapeDtypeStruct((2 * TOK, QW), BF),
            jax.ShapeDtypeStruct((HH, 2, 4, 4, 2 * TOK, 2 * HD), BF),
        ],
        in_specs=[anywhere] * 7 + [vmem] * 3,
        out_specs=[anywhere] * 5 + [vmem, anywhere] + [vmem] * 4 + [anywhere],
        scratch_shapes=[
            pltpu.VMEM((2, 4, 4, 2, 32, QW + KVW), BF),
            pltpu.VMEM((HH, 2 * TOK, 2 * HD), BF),
            pltpu.VMEM((4, 4) + gains.shape, F32),
            pltpu.SemaphoreType.DMA((7, 2)),
            pltpu.SemaphoreType.DMA((8,)),
            pltpu.SemaphoreType.DMA((4, 4)),
            pltpu.SemaphoreType.DMA((4, 4)),
            pltpu.SemaphoreType.DMA((3, 3, 4)),
            pltpu.SemaphoreType.DMA((3, 3, 4)),
            pltpu.SemaphoreType.DMA((n, 3, 4)),
            pltpu.SemaphoreType.DMA((n, 3, 4)),
            pltpu.SemaphoreType.DMA((HH, 3, 4)),
            pltpu.SemaphoreType.DMA((HH, 3, 4)),
            pltpu.SemaphoreType.DMA((HH,)),
        ],
        compiler_params=pltpu.CompilerParams(
            collective_id=cid, has_side_effects=True, vmem_limit_bytes=32 * 1024 * 1024
        ),
        name="front",
    )(*shards, x, dy, gains, cosine, sine)


def rope_back_kernel(joined, dq, dkv, gains, cosine, sine, out, terms):
    head_gains = gains[32:33]

    def tile(t, is_key, grad):
        v = joined[:, t * 128 : (t + 1) * 128]
        low = lane_of(v.shape) < HD
        back = grad * cosine[...] - swap_halves(grad) * sine[...]
        inverse = lax.rsqrt(head_sums(v * v) * (1.0 / HD) + EPSILON)
        scaled = back * tile_gain(head_gains, is_key)
        inner = head_sums(scaled * v) * (1.0 / HD)
        result = inverse * scaled - v * (inverse * inverse * inverse) * inner
        if is_key:
            result = jnp.where(low, result, grad)
        out[:, t * 128 : (t + 1) * 128] = result.astype(BF)
        return jnp.sum(back * v * inverse, axis=0, keepdims=True)

    q_terms = sum(tile(t, False, dq[:, t * 128 : (t + 1) * 128]) for t in range(QW // 128))
    k_terms = sum(tile(QW // 128 + h, True, dkv[h]) for h in range(HH))
    low = lane_of(q_terms.shape) < HD
    q_terms = q_terms + pltpu.roll(q_terms, HD, 1)
    terms[...] = jnp.where(low, q_terms, pltpu.roll(k_terms, HD, 1))


def rope_back(joined, dq, dkv, gains, cosine, sine):
    vmem = pl.BlockSpec(memory_space=pltpu.VMEM)
    return pl.pallas_call(
        rope_back_kernel,
        out_shape=[jax.ShapeDtypeStruct((2 * TOK, QW + KVW), BF), jax.ShapeDtypeStruct((1, 128), F32)],
        in_specs=[vmem] * 6,
        out_specs=[vmem] * 2,
        compiler_params=pltpu.CompilerParams(vmem_limit_bytes=32 * 1024 * 1024),
        name="rope_back",
    )(joined, dq, dkv, gains, cosine, sine)


def lead_shape(dims):
    full = {"h": 2, "x": 4, "y": 4, "l": 2}
    return tuple(full[d] for d in dims)


def without(dims, axis):
    gone = ("h", "l") if axis == "z" else (axis,)
    return tuple(d for d in dims if d not in gone)


class Summing:
    def __init__(self, source, dims, at, order, rows, cols, buffers, ssem, rsem, lsem):
        self.ref, self.dims, self.at, self.order = source, dims, at, order
        self.cols, self.buffers, self.rows = cols, buffers, rows
        self.ssem, self.rsem, self.lsem = ssem, rsem, lsem
        self.phase, self.sent = 0, []

    def part(self, coordinate, rows):
        return pick(self.ref, self.dims, labels(self.axis, coordinate), (rows, self.cols))

    def send(self, n, src, dst, by):
        c = send(src, dst, self.ssem.at[self.phase, n], self.rsem.at[self.phase, n], moved(self.at, self.axis, by))
        self.sent.append(c)
        return c

    def start(self):
        self.axis = self.order[self.phase]
        self.rest = without(self.dims, self.axis)
        self.lead = lead_shape(self.rest)
        half = self.rows // 2
        first, second, every = pl.ds(0, half), pl.ds(half, half), pl.ds(0, self.rows)
        i = self.at[self.axis]
        buf = self.buffers[self.phase]
        self.local = []
        if SIZES[self.axis] == 2:
            self.direct = (self.send(0, self.part(1 - i, every), buf["got"].at[0], 1),)
        else:
            up, down, far = lax.rem(i + 1, 4), lax.rem(i + 3, 4), lax.rem(i + 2, 4)
            self.relay = (
                self.send(0, self.part(far, first), buf["relay"].at[0], 1),
                self.send(1, self.part(far, second), buf["relay"].at[1], 3),
            )
            self.direct = (
                self.send(2, self.part(up, second), buf["got"].at[1, 1], 1),
                self.send(3, self.part(down, first), buf["got"].at[0, 1], 3),
            )
            self.near = (up, down)
        if self.phase == 0:
            todo = [(self.part(i, every), buf["mine"])]
            if SIZES[self.axis] == 4:
                todo.append((self.part(up, first), buf["own"].at[0]))
                todo.append((self.part(down, second), buf["own"].at[1]))
            for n, (src, dst) in enumerate(todo):
                c = pltpu.make_async_copy(src, dst, self.lsem.at[n])
                c.start()
                self.local.append(c)

    def over_lead(self, add):
        rest = self.lead[1:]
        spots = [()]
        for n in rest:
            spots = [s + (j,) for s in spots for j in range(n)]
        if not self.lead:
            add(())
            return

        def go(j, carry):
            for s in spots:
                add((j,) + s)
            return carry

        lax.fori_loop(0, self.lead[0], go, 0)

    def pass_on(self):
        if SIZES[self.axis] == 2:
            return
        buf = self.buffers[self.phase]
        half = self.rows // 2
        for n, by in ((0, 1), (1, 3)):
            self.relay[n].wait_recv()
            if self.phase == 0:
                self.local[1 + n].wait()
                own = buf["own"].at[n]
            else:
                own = self.part(self.near[n], pl.ds(n * half, half))

            def add(spot):
                here_ = spot + (slice(None), slice(None))
                both = buf["relay"][(n,) + here_].astype(F32) + own[here_].astype(F32)
                buf["relay"][(n,) + here_] = both.astype(BF)

            self.over_lead(add)
            c = self.send(4 + n, buf["relay"].at[n], buf["got"].at[n, 0], by)
            self.direct = self.direct + (c,)

    def finish(self):
        buf = self.buffers[self.phase]
        half = self.rows // 2
        if self.local:
            self.local[0].wait()
        for c in self.direct:
            c.wait_recv()
        own = buf["mine"] if self.phase == 0 else self.part(self.at[self.axis], pl.ds(0, self.rows))
        out = buf["mine"] if self.phase == 0 else buf["sum"]

        def add(spot):
            if SIZES[self.axis] == 2:
                here_ = spot + (slice(None), slice(None))
                out[here_] = (own[here_].astype(F32) + buf["got"][(0,) + here_].astype(F32)).astype(out.dtype)
                return
            for n in range(2):
                rows = spot + (pl.ds(n * half, half), slice(None))
                all_ = spot + (slice(None), slice(None))
                total = own[rows].astype(F32) + buf["got"][(n, 0) + all_].astype(F32)
                total = total + buf["got"][(n, 1) + all_].astype(F32)
                out[rows] = total.astype(out.dtype)

        self.over_lead(add)
        self.ref, self.dims, self.cols = out, self.rest, slice(None)
        self.phase += 1


class Total:
    def __init__(self, value, at, buf, ssem, rsem):
        self.value, self.at, self.buf, self.ssem, self.rsem = value, at, buf, ssem, rsem
        self.phase, self.sent = 0, []
        self.start()

    def start(self):
        n, axis = self.phase, ("core", "z", "y", "x")[self.phase]
        self.buf[n, 0] = self.value
        self.copies = []
        for i in (1, 3, 2) if axis != "core" else (1,):
            self.copies.append(
                send(self.buf.at[n, 0], self.buf.at[n, i], self.ssem.at[n, i], self.rsem.at[n, i], moved(self.at, axis, i))
            )

    def step(self):
        n, buf = self.phase, self.buf
        if n == 4:
            return
        for c in self.copies:
            c.wait_recv()
            self.sent.append(c)
        if n == 0:
            self.value = buf[n, 0] + buf[n, 1]
        else:
            self.value = (buf[n, 0] + buf[n, 2]) + (buf[n, 1] + buf[n, 3])
        self.phase += 1
        if self.phase < 4:
            self.start()


def run_sums(streams, total=None):
    for s in streams:
        s.start()
    for phase in range(3):
        for s in streams:
            s.pass_on()
        if total is not None:
            total.step()
        for s in streams:
            s.finish()
            if phase < 2:
                s.start()
        if total is not None:
            total.step()
    for s in streams:
        for c in s.sent:
            c.wait_send()


def sum_scratch(order, dims, rows, width):
    buffers = []
    for phase, axis in enumerate(order):
        rest = without(dims, axis)
        lead = lead_shape(rest)
        buf = {}
        if SIZES[axis] == 2:
            buf["got"] = pltpu.VMEM((1,) + lead + (rows, width), BF)
        else:
            buf["got"] = pltpu.VMEM((2, 2) + lead + (rows // 2, width), BF)
            buf["relay"] = pltpu.VMEM((2,) + lead + (rows // 2, width), BF)
        if phase == 0:
            buf["mine"] = pltpu.VMEM(lead + (rows, width), BF)
            if SIZES[axis] == 4:
                buf["own"] = pltpu.VMEM((2,) + lead + (rows // 2, width), BF)
        else:
            buf["sum"] = pltpu.VMEM(lead + (rows, width), BF if phase < 2 else F32)
        buffers.append(buf)
        dims = rest
    return buffers


def kv_sum_kernel(src, out, buffers, ssem, rsem, lsem):
    at = here()
    greet(neighbours(at, ("h", "x", "y")))
    streams = [
        Summing(src.at[h], KV_DIMS, at, KV_SUM_ORDERS[h], 2 * TOK, slice(None), buffers[h], ssem.at[h], rsem.at[h], lsem.at[h])
        for h in range(HH)
    ]
    run_sums(streams)
    for h in range(HH):
        out[h] = buffers[h][2]["sum"][...]


def sum_kv(grads, cid):
    return pl.pallas_call(
        kv_sum_kernel,
        out_shape=jax.ShapeDtypeStruct((HH, 2 * TOK, 2 * HD), F32),
        in_specs=[pl.BlockSpec(memory_space=pl.ANY)],
        out_specs=pl.BlockSpec(memory_space=pltpu.VMEM),
        scratch_shapes=[
            [sum_scratch(KV_SUM_ORDERS[h], KV_DIMS, 2 * TOK, 2 * HD) for h in range(HH)],
            pltpu.SemaphoreType.DMA((HH, 3, 6)),
            pltpu.SemaphoreType.DMA((HH, 3, 6)),
            pltpu.SemaphoreType.DMA((HH, 3)),
        ],
        compiler_params=pltpu.CompilerParams(
            collective_id=cid, has_side_effects=True, vmem_limit_bytes=48 * 1024 * 1024
        ),
        name="sum_kv",
    )(grads)


def weight_sum_kernel(pieces, n, *refs):
    ins, small, outs, small_out = refs[:n], refs[n], refs[n + 1 : 2 * n + 1], refs[2 * n + 1]
    buffers, stages, swapped, small_buf, ssem, rsem, lsem, csem, tssem, trsem = refs[2 * n + 2 :]
    at = here()
    core = at["core"]
    sibling = moved(at, "core", 1)
    greet([sibling] + sum_peers(at, ("x", "y", "z")))
    streams = [
        Summing(ins[a], W_DIMS, at, order, 32, pl.ds(start, width), buffers[k], ssem.at[k], rsem.at[k], lsem.at[k])
        for k, (a, start, width, order) in enumerate(pieces)
    ]
    total = Total(small[...], at, small_buf, tssem, trsem)
    run_sums(streams, total)
    small_out[...] = total.value
    for k, (a, start, width, order) in enumerate(pieces):
        stages[a][:, start : start + width] = buffers[k][2]["sum"][...]
    other = pl.ds(pl.multiple_of((1 - core) * 16, 16), 16)
    own = pl.ds(pl.multiple_of(core * 16, 16), 16)
    copies = [send(stages[a].at[other], swapped[a], csem.at[a, 0], csem.at[a, 1], sibling) for a in range(n)]
    for a in range(n):
        outs[a][core] = stages[a][own, :]
        copies[a].wait_recv()
        outs[a][1 - core] = swapped[a][...]
    for c in copies + total.sent:
        c.wait_send()


def sum_weights(grads, small, pieces, cid, limit):
    n, k = len(grads), len(pieces)
    anywhere = pl.BlockSpec(memory_space=pl.ANY)
    vmem = pl.BlockSpec(memory_space=pltpu.VMEM)
    widths = [g.shape[-1] for g in grads]
    return pl.pallas_call(
        functools.partial(weight_sum_kernel, pieces, n),
        out_shape=[jax.ShapeDtypeStruct((2, 16, w), F32) for w in widths] + [jax.ShapeDtypeStruct(small.shape, F32)],
        in_specs=[anywhere] * n + [vmem],
        out_specs=[vmem] * (n + 1),
        scratch_shapes=[
            [sum_scratch(order, W_DIMS, 32, width) for a, start, width, order in pieces],
            [pltpu.VMEM((32, w), F32) for w in widths],
            [pltpu.VMEM((16, w), F32) for w in widths],
            pltpu.VMEM((4, 4) + small.shape, F32),
            pltpu.SemaphoreType.DMA((k, 3, 6)),
            pltpu.SemaphoreType.DMA((k, 3, 6)),
            pltpu.SemaphoreType.DMA((k, 3)),
            pltpu.SemaphoreType.DMA((n, 2)),
            pltpu.SemaphoreType.DMA((4, 4)),
            pltpu.SemaphoreType.DMA((4, 4)),
        ],
        compiler_params=pltpu.CompilerParams(collective_id=cid, has_side_effects=True, vmem_limit_bytes=limit),
        name="sum_weights",
    )(*[g.reshape(2, 4, 4, 2, 32, g.shape[-1]) for g in grads], small)


def sum_peers(at, axes):
    out = []
    for a in axes:
        for i in (1, 3, 2) if SIZES[a] == 4 else (1,):
            out.append(moved(at, a, i))
    return out


def fetch_keys(tab, kvg, kv, sems):
    for s in range(2):
        for h in range(HH):

            def go(p, carry):
                slot = tab[s, p]
                row = lax.rem(slot, 2) * SPAN + s * TOK
                pltpu.make_async_copy(
                    kvg.at[h, lax.div(slot, 2), pl.ds(pl.multiple_of(row, SPAN), SPAN)],
                    kv.at[s, h, pl.ds(pl.multiple_of(p * SPAN, SPAN), SPAN)],
                    sems.at[s, h],
                ).start()
                return carry

            lax.fori_loop(0, 2 * N_CTX, go, 0)


def step_of(t, low_steps):
    half = jnp.where(t < low_steps, 0, 1)
    return half, jnp.where(t < low_steps, t, t - low_steps)


def heads_at(ref, s, h, half, width=HD):
    rows = slice(s * TOK + half * SPAN, s * TOK + (half + 1) * SPAN)
    return jnp.concatenate([ref[rows, (h * GROUP + g) * HD : (h * GROUP + g + 1) * HD] for g in range(GROUP)], axis=0)


def put_heads(ref, s, h, half, value):
    rows = slice(s * TOK + half * SPAN, s * TOK + (half + 1) * SPAN)
    for g in range(0, GROUP, 2):
        both = jnp.concatenate([value[g * SPAN : (g + 1) * SPAN], value[(g + 1) * SPAN : (g + 2) * SPAN]], axis=1)
        ref[rows, (h * GROUP + g) * HD : (h * GROUP + g + 2) * HD] = both.astype(ref.dtype)


def attend_kernel(tab, qr, kvg, o_ref, low_ref, l_ref, kv, q_ref, acc, total, sems):
    fetch_keys(tab, kvg, kv, sems)
    rate = LOG2E * HD**-0.5
    blank = jnp.zeros((QROWS, HD), BF)
    for s in range(2):
        for h in range(HH):
            for half in range(2):
                q_ref[s, h, half] = jnp.concatenate([heads_at(qr, s, h, half), blank], axis=1)
    for s in range(2):
        span = tab[s, 2 * N_CTX]
        low_steps = lax.div(span, SPANS_STEP)
        for h in range(HH):
            pltpu.make_async_copy(kv.at[s, h], kv.at[s, h], sems.at[s, h]).wait()
            acc[...] = jnp.zeros_like(acc)
            total[...] = jnp.zeros_like(total)

            def step(half, block, limit):
                keys = kv[s, h, pl.ds(pl.multiple_of(block * KEYS, KEYS), KEYS), :]
                scores = lax.dot_general(keys, q_ref[s, h, half], NT, preferred_element_type=F32)
                prob = jnp.exp2(scores * rate)
                if limit is not None:
                    row = lax.broadcasted_iota(jnp.int32, prob.shape, 0)
                    col = lax.rem(lax.broadcasted_iota(jnp.int32, prob.shape, 1), SPAN)
                    prob = jnp.where(row <= col + limit, prob, 0.0)
                total[half] += jnp.sum(prob, axis=0, keepdims=True)
                acc[half] += lax.dot_general(keys, prob.astype(BF), TN, preferred_element_type=F32)

            def full(t, carry):
                half, block = step_of(t, low_steps)
                step(half, block, None)
                return carry

            lax.fori_loop(0, FULL_STEPS, full, 0)
            for half, first in ((0, span), (1, 2 * N_CTX - 1 - span)):
                step(half, lax.div(first, SPANS_STEP), lax.rem(first, SPANS_STEP) * SPAN)
                out = (acc[half, HD:, :] / total[half]).T
                put_heads(o_ref, s, h, half, out)
                put_heads(low_ref, s, h, half, out)
                l_ref[s, h, half] = jnp.log2(total[half])


def attend(tab, query, kvg):
    vmem = pl.BlockSpec(memory_space=pltpu.VMEM)
    return pl.pallas_call(
        attend_kernel,
        out_shape=[
            jax.ShapeDtypeStruct((2 * TOK, QW), F32),
            jax.ShapeDtypeStruct((2 * TOK, QW), BF),
            jax.ShapeDtypeStruct((2, HH, 2, 1, QROWS), F32),
        ],
        in_specs=[pl.BlockSpec(memory_space=pltpu.SMEM), vmem, pl.BlockSpec(memory_space=pl.ANY)],
        out_specs=[vmem, vmem, vmem],
        scratch_shapes=[
            pltpu.VMEM((2, HH, N_CTX * TOK, 2 * HD), BF),
            pltpu.VMEM((2, HH, 2, QROWS, 2 * HD), BF),
            pltpu.VMEM((2, 2 * HD, QROWS), F32),
            pltpu.VMEM((2, 1, QROWS), F32),
            pltpu.SemaphoreType.DMA((2, HH)),
        ],
        compiler_params=pltpu.CompilerParams(vmem_limit_bytes=32 * 1024 * 1024),
        name="attend",
    )(tab, query, kvg)


def attend_back_kernel(
    tab, qr, da, attn, l_ref, kvg, dq_ref, dkv_ref, kv, qd_ref, delta_ref, stage, acc, dq_acc, sems, osems
):
    fetch_keys(tab, kvg, kv, sems)
    blank = jnp.zeros((QROWS, HD), BF)
    for s in range(2):
        for h in range(HH):
            for half in range(2):
                grads = heads_at(da, s, h, half)
                qd_ref[s, h, half, :QROWS] = jnp.concatenate([heads_at(qr, s, h, half), blank], axis=1)
                qd_ref[s, h, half, QROWS:] = jnp.concatenate([blank, grads], axis=1)
                inner = (grads.astype(F32) * heads_at(attn, s, h, half)).T
                delta_ref[s, h, half] = jnp.sum(inner, axis=0, keepdims=True)
    rate = LOG2E * HD**-0.5
    lanes = lax.broadcasted_iota(jnp.int32, (1, 2 * HD), 1)
    factor = jnp.where(lanes < HD, HD**-0.5, 1.0)
    for s in range(2):
        span = tab[s, 2 * N_CTX]
        low_steps = lax.div(span, SPANS_STEP)
        for h in range(HH):
            pltpu.make_async_copy(kv.at[s, h], kv.at[s, h], sems.at[s, h]).wait()
            dq_acc[...] = jnp.zeros_like(dq_acc)
            acc[...] = jnp.zeros_like(acc)

            def step(half, block, limit):
                rows = pl.ds(pl.multiple_of(block * KEYS, KEYS), KEYS)
                keys = kv[s, h, rows, :]
                both = lax.dot_general(keys, qd_ref[s, h, half], NT, preferred_element_type=F32)
                prob = jnp.exp2(both[:, :QROWS] * rate - l_ref[s, h, half])
                if limit is not None:
                    row = lax.broadcasted_iota(jnp.int32, prob.shape, 0)
                    col = lax.rem(lax.broadcasted_iota(jnp.int32, prob.shape, 1), SPAN)
                    prob = jnp.where(row <= col + limit, prob, 0.0)
                grad = (prob * (both[:, QROWS:] - delta_ref[s, h, half])).astype(BF)
                pair = jnp.concatenate([grad, prob.astype(BF)], axis=1)
                acc[rows, :] += lax.dot_general(pair, qd_ref[s, h, half], NN, preferred_element_type=F32)
                dq_acc[half] += lax.dot_general(keys, grad, TN, preferred_element_type=F32)

            def full(t, carry):
                half, block = step_of(t, low_steps)
                step(half, block, None)
                return carry

            lax.fori_loop(0, FULL_STEPS, full, 0)
            for half, first in ((0, span), (1, 2 * N_CTX - 1 - span)):
                step(half, lax.div(first, SPANS_STEP), lax.rem(first, SPANS_STEP) * SPAN)
                put_heads(dq_ref, s, h, half, (dq_acc[half, :HD, :] * HD**-0.5).T)

            def cast(b, carry):
                rows = pl.ds(pl.multiple_of(b * KEYS, KEYS), KEYS)
                stage[s, h, rows, :] = (acc[rows, :] * factor).astype(BF)
                return carry

            lax.fori_loop(0, N_CTX * TOK // KEYS, cast, 0)

            def put(p, carry):
                slot = tab[s, p]
                row = lax.rem(slot, 2) * SPAN + s * TOK
                pltpu.make_async_copy(
                    stage.at[s, h, pl.ds(pl.multiple_of(p * SPAN, SPAN), SPAN)],
                    dkv_ref.at[h, lax.div(slot, 2), pl.ds(pl.multiple_of(row, SPAN), SPAN)],
                    osems.at[s, h],
                ).start()
                return carry

            lax.fori_loop(0, 2 * N_CTX, put, 0)
    for s in range(2):
        for h in range(HH):
            pltpu.make_async_copy(stage.at[s, h], stage.at[s, h], osems.at[s, h]).wait()


def attend_back(tab, query, grad_attn, attn, log_sum, kvg):
    vmem = pl.BlockSpec(memory_space=pltpu.VMEM)
    anywhere = pl.BlockSpec(memory_space=pl.ANY)
    return pl.pallas_call(
        attend_back_kernel,
        out_shape=[
            jax.ShapeDtypeStruct((2 * TOK, QW), F32),
            jax.ShapeDtypeStruct((HH, N_CTX, 2 * TOK, 2 * HD), BF),
        ],
        in_specs=[pl.BlockSpec(memory_space=pltpu.SMEM), vmem, vmem, vmem, vmem, anywhere],
        out_specs=[vmem, anywhere],
        scratch_shapes=[
            pltpu.VMEM((2, HH, N_CTX * TOK, 2 * HD), BF),
            pltpu.VMEM((2, HH, 2, 2 * QROWS, 2 * HD), BF),
            pltpu.VMEM((2, HH, 2, 1, QROWS), F32),
            pltpu.VMEM((2, HH, N_CTX * TOK, 2 * HD), BF),
            pltpu.VMEM((N_CTX * TOK, 2 * HD), F32),
            pltpu.VMEM((2, 2 * HD, QROWS), F32),
            pltpu.SemaphoreType.DMA((2, HH)),
            pltpu.SemaphoreType.DMA((2, HH)),
        ],
        compiler_params=pltpu.CompilerParams(vmem_limit_bytes=40 * 1024 * 1024),
        name="attend_back",
    )(tab, query, grad_attn, attn, log_sum, kvg)


def permutation(axis, by):
    pairs = []
    for c in range(N_CTX):
        for f in range(4):
            h, x, y = c // 16, (c // 4) % 4, c % 4
            z, core = h * 2 + f // 2, f % 2
            if axis == "x":
                x = (x + by) % 4
            elif axis == "y":
                y = (y + by) % 4
            elif axis == "z":
                z = (z + by) % 4
            else:
                core = 1 - core
            pairs.append((c * 4 + f, ((z // 2) * 16 + x * 4 + y) * 4 + (z % 2) * 2 + core))
    return pairs


def shift(value, axis, by=1):
    return lax.ppermute(value, ("ctx", "fsdp"), permutation(axis, by))


def norm_rows(value_in, gain_row):
    inverse = lax.rsqrt(jnp.mean(value_in * value_in, axis=-1, keepdims=True) + EPSILON)
    return (value_in * inverse * gain_row, inverse)


def norm_back(value_in, inverse, gain_row, upstream):
    scaled = upstream * gain_row
    backward = inverse * scaled - value_in * inverse**3 * jnp.mean(scaled * value_in, axis=-1, keepdims=True)
    return (backward, upstream * value_in * inverse)


def body(layer_input, w_qkv, w_out, w_gate_up, w_down, norm_gains, span_map, cotangent):
    at = here()
    core, low = at["core"], at["l"]
    w_q = w_qkv[:, : HQ * HD].reshape(16, 2, QW).transpose(1, 0, 2)
    w_k = w_qkv[:, HQ * HD : (HQ + HK) * HD].reshape(16, 2, HH, HD)
    w_v = w_qkv[:, (HQ + HK) * HD :].reshape(16, 2, HH, HD)
    w_kv = jnp.concatenate([w_k, w_v], axis=3).reshape(16, 2, KVW).transpose(1, 0, 2)
    shard_one = jnp.concatenate([w_q, w_kv], axis=2)
    shard_gate = w_gate_up[:, :FF].reshape(16, 2, FH).transpose(1, 0, 2)
    shard_up = w_gate_up[:, FF:].reshape(16, 2, FH).transpose(1, 0, 2)
    shard_down = w_down.reshape(16, 2, FH).transpose(1, 0, 2)
    shard_out = w_out.reshape(16, 2, QW).transpose(1, 0, 2)
    share = norm_gains.shape[0]
    device = lax.axis_index(("ctx", "fsdp"))
    own_gain = lax.dynamic_update_slice_in_dim(jnp.zeros((40 * 128,), F32), norm_gains.astype(F32), device * share, 0)

    ctx_index = lax.axis_index("ctx")
    maps = lax.dynamic_slice_in_dim(span_map, low * 2, 2, 0)
    own_span = lax.dynamic_slice_in_dim(maps, ctx_index, 1, 1)
    spans = jnp.concatenate([own_span, 2 * N_CTX - 1 - own_span], axis=1)
    positions = (spans[:, :, None] * SPAN + jnp.arange(SPAN, dtype=jnp.int32)).reshape(2 * TOK)
    match = maps[:, None, :] == jnp.arange(N_CTX, dtype=jnp.int32)[None, :, None]
    inverse_map = jnp.sum(jnp.where(match, jnp.arange(N_CTX, dtype=jnp.int32), 0), axis=2)
    tab = jnp.concatenate([inverse_map * 2, inverse_map[:, ::-1] * 2 + 1, own_span], axis=1)
    half_dim = HD // 2
    frequencies = ROPE_BASE ** (-(jnp.arange(half_dim, dtype=F32) * 2.0 / HD))
    angles = positions.astype(F32)[:, None] * frequencies[None, :]
    cosine, sine = jnp.cos(angles), jnp.sin(angles)
    cosine = jnp.concatenate([cosine] * 4, axis=1)
    sine = jnp.concatenate([-sine, sine] * 2, axis=1)

    weights = [shard_one, shard_gate, shard_up, shard_down, shard_out]
    (w_joined, w_gate, w_up, w_back, w_proj, x_pair, dy_pair, gains, joined, normed_one, query, kvg) = front(
        weights, layer_input[0], cotangent[0], own_gain.reshape(40, 128), cosine, sine, 1
    )
    w_joined, w_gate, w_up, w_back, w_proj = (w.reshape(D, -1) for w in (w_joined, w_gate, w_up, w_back, w_proj))
    kvg = kvg.reshape(HH, N_CTX, 2 * TOK, 2 * HD)
    gain_one, gain_two = gains[:16].reshape(D), gains[16:32].reshape(D)
    stream_in = x_pair.reshape(2 * TOK, D).astype(F32)
    dy = dy_pair.reshape(2 * TOK, D)
    attn_f32, attn_low, log_sum = attend(tab, query, kvg)

    partial_a = lax.dot_general(attn_low, w_proj, NT, preferred_element_type=F32)
    branch_a = partial_a + shift(partial_a, "core")
    middle = stream_in + branch_a
    normed_two, inverse_two = norm_rows(middle, gain_two)
    normed_two = normed_two.astype(BF)
    gate_part = jnp.dot(normed_two, w_gate, preferred_element_type=F32)
    up_part = jnp.dot(normed_two, w_up, preferred_element_type=F32)
    sigmoid_gate = jax.nn.sigmoid(gate_part)
    silu_gate = gate_part * sigmoid_gate
    hidden = (silu_gate * up_part).astype(BF)
    partial_f = lax.dot_general(hidden, w_back, NT, preferred_element_type=F32)
    grad_hidden = jnp.dot(dy, w_back, preferred_element_type=F32)
    grad_gate = (grad_hidden * up_part * sigmoid_gate * (1.0 + gate_part * (1.0 - sigmoid_gate))).astype(BF)
    grad_up = (grad_hidden * silu_gate).astype(BF)
    partial_n = lax.dot_general(grad_gate, w_gate, NT, preferred_element_type=F32)
    partial_n = partial_n + lax.dot_general(grad_up, w_up, NT, preferred_element_type=F32)

    def own_rows(value):
        return lax.dynamic_slice_in_dim(value, core * TOK, TOK, 0)

    def other_rows(value):
        return lax.dynamic_slice_in_dim(value, (1 - core) * TOK, TOK, 0)

    branch_f = own_rows(partial_f) + shift(other_rows(partial_f), "core")
    result = own_rows(middle) + branch_f
    grad_normed_two = partial_n + shift(partial_n, "core")
    back_two, gain_two_terms = norm_back(middle, inverse_two, gain_two, grad_normed_two)
    grad_middle = dy.astype(F32) + back_two
    grad_branch = grad_middle.astype(BF)

    def outer(left, right):
        return lax.dot_general(left, right, TN, preferred_element_type=F32).astype(BF)

    early = [outer(normed_two, grad_gate), outer(normed_two, grad_up), outer(dy, hidden), outer(grad_branch, attn_low)]

    grad_attn = jnp.dot(grad_branch, w_proj, preferred_element_type=F32).astype(BF)
    dq, dkv = attend_back(tab, query, grad_attn, attn_f32, log_sum, kvg)
    grad_kv = sum_kv(dkv.reshape(HH, 2, 4, 4, 2 * TOK, 2 * HD), 4)
    grad_joined, head_terms = rope_back(joined, dq, grad_kv, gains, cosine, sine)
    partial_one = lax.dot_general(grad_joined, w_joined, NT, preferred_element_type=F32)
    grad_normed_one = own_rows(partial_one) + shift(other_rows(partial_one), "core")
    own_in = layer_input[0].astype(F32)
    inverse_one = lax.rsqrt(jnp.mean(own_in * own_in, axis=-1, keepdims=True) + EPSILON)
    back_one, gain_one_terms = norm_back(own_in, inverse_one, gain_one, grad_normed_one)
    grad_input = own_rows(grad_middle) + back_one

    def mean_root(stream):
        return jnp.sum(jnp.sqrt(jnp.mean(stream * stream, axis=-1)))

    stats = jnp.stack([mean_root(s) for s in (own_in, own_rows(branch_a), own_rows(middle))] + [mean_root(branch_f)])
    sums = jnp.concatenate(
        [
            jnp.sum(gain_one_terms, axis=0),
            jnp.sum(own_rows(gain_two_terms), axis=0),
            head_terms[0],
            stats,
        ]
    )
    sums = jnp.pad(sums, (0, 40 * 128 - sums.shape[0])).reshape(40, 128)
    own_gate, own_up, own_down, own_out, own_qkv, sums = sum_weights(
        early + [outer(normed_one, grad_joined)], sums, SUMS, 5, 62 * 1024 * 1024
    )
    sums = sums.reshape(-1)
    grad_mlp = jnp.concatenate([own_gate[0], own_gate[1], own_up[0], own_up[1]], axis=1)
    grad_down = jnp.concatenate([own_down[0], own_down[1]], axis=1)
    kv_cols = own_qkv[:, :, QW:].reshape(2, 16, HH, 2, HD)
    grad_qkv = jnp.concatenate(
        [
            own_qkv[0, :, :QW],
            own_qkv[1, :, :QW],
            *(kv_cols[half, :, :, kind].reshape(16, HH * HD) for kind in range(2) for half in range(2)),
        ],
        axis=1,
    )
    grad_proj = jnp.concatenate([own_out[0], own_out[1]], axis=1)

    own_gains = lax.dynamic_slice_in_dim(sums, device * share, share, 0)
    stream_rms = sums[4224:4228] / (TOK * N_CTX * 4)
    return (
        result[None].astype(BF),
        grad_input[None].astype(BF),
        grad_qkv,
        grad_proj,
        grad_mlp,
        grad_down,
        own_gains,
        stream_rms,
    )


def solution(mesh):
    rows = P(("ctx", "fsdp"), None)
    tokens = P("fsdp", "ctx", None)
    return jax.shard_map(
        body,
        mesh=mesh,
        in_specs=(tokens, rows, rows, rows, rows, P(("ctx", "fsdp")), P(), tokens),
        out_specs=(tokens, tokens, rows, rows, rows, rows, P(("ctx", "fsdp")), P()),
        check_vma=False,
    )
```

time: 864 us -> 591 us (0.68)
  waiting for transfers between devices: 76.4 us -> 0.01 us
  starting transfers between devices: 57.8 us -> 5.18 us
  local copies, waits for them, and re-layouts: 84 us -> 31.6 us
  Pallas kernels: 502 us -> 454 us
  other arithmetic: 64.7 us -> 18.2 us
    ppermute x34 -> x4, waiting for transfers between devices: 76.4 us -> 0.01 us  [shift(): return lax.ppermute(value, ('ctx', 'fsdp'), permutation(axis, by))]
    ppermute x34 -> x4, starting transfers between devices: 57.8 us -> 5.18 us  [shift(): return lax.ppermute(value, ('ctx', 'fsdp'), permutation(axis, by))]
    pallas_call x8 -> x6, Pallas kernels: 502 us -> 454 us  [the longest x1 182 us: front(): pl.pallas_call(front_kernel, out_shape=full + [jax.ShapeDtypeStruct((2,)...]
    reshape x15 -> x0, local copies, waits for them, and re-layouts: 21.6 us -> none  [the longest x6 9.36 us: product(): return out.reshape(lead_shape(rest) + (32, right.shape[1]))]
    add x9 -> x0, other arithmetic: 19.9 us -> none  [the longest x6 17.6 us: block(): total = sum((take(g, dims, axis, target).astype(F32) for g in gathered))]
    mul x11 -> x1, local copies, waits for them, and re-layouts: 12.8 us -> 0.72 us  [norm_back(): scaled = upstream * gain_row]
    dot_general x1, matrix products: 5.31 us -> 14.8 us  [body(): partial_f = lax.dot_general(hidden, w_back, NT, preferred_element_type=F32)]
    dot_general x15 -> x5, matrix products: 26.7 us -> 21.2 us  [outer(): lax.dot_general(left, right, TN, preferred_element_type=F32).astype(BF)]
  transfers between devices with their start and end apart: 34 -> 4, of which waited for: 7 -> 0; matrix products, arithmetic and copies ran while one was open for 15% -> 10% of each run, Pallas kernels for 28% -> 16%
where the time goes in v2:
time: 591 us; the launch traced here: 581 us
  Pallas kernels  454 us (77%)
  matrix products  70 us (12%)
  local copies, waits for them, and re-layouts  31.6 us (5%)
  other arithmetic  18.2 us (3%)
    pallas_call x1, Pallas kernels, front(): pl.pallas_call(front_kernel, out_shape=full + [jax.ShapeDtypeStruct((2,)...  182 us
    pallas_call x1, Pallas kernels, sum_weights(): pl.pallas_call(functools.partial(weight_sum_kernel, pieces, n), out_shape...  138 us
    pallas_call x1, Pallas kernels, attend_back(): pl.pallas_call(attend_back_kernel, out_shape=[jax.ShapeDtypeStruct((2 * T...  50.6 us
    pallas_call x1, Pallas kernels, sum_kv(): pl.pallas_call(kv_sum_kernel, out_shape=jax.ShapeDtypeStruct((HH, 2 * TOK...  42.8 us
    pallas_call x1, Pallas kernels, attend(): pl.pallas_call(attend_kernel, out_shape=[jax.ShapeDtypeStruct((2 * TOK, Q...  38.8 us
    dot_general x5, matrix products, outer(): lax.dot_general(left, right, TN, preferred_element_type=F32).astype(BF)  21.2 us
    dot_general x1, matrix products, body(): partial_f = lax.dot_general(hidden, w_back, NT, preferred_element_type=F32)  14.8 us
    unnamed x94, local copies, waits for them, and re-layouts  12.1 us
  transfers between devices with their start and end apart: 4, of which 0 were waited for; matrix products, arithmetic and copies ran while one was open for 10% of the time, Pallas kernels for 16%

profile of v2, /device:TPU:1, one launch (start us, length us, event | category | flops | bytes accessed | tf_op | source)
XLA Modules:
  0.0 580.9 jit_solution(15137406951967780295)
XLA Ops:
  4.4 1.4 copy.50
  11.4 181.7 %front.1 = (bf16[2,4,4,2,32,1152]{5,4,3,2,1,0:T(8,128)(2,1)S(1)}, bf16[2,4,4,2,32,2176]{5,4,3,2,1,0:T(8,128)(2,1)}, bf16[2,4,4,2,32,2176]{5,4,3,2,1,0:T(8,128)(2...) custom-call(bf16[2,16,1152]{2,1,0:T(8,128)(2,1)S(1)} %pad_maximum_fu, ...), custom_call_target="tpu_custom_call" | custom-call | tf_op jit(solution)/shard_map/front/pallas_call | solution.py:333
  197.2 2.2 copy-done.25
  199.4 38.8 %attend.1 = (f32[256,768]{1,0:T(8,128)S(1)}, bf16[256,768]{1,0:T(8,128)(2,1)S(1)}, f32[2,3,2,1,256]{4,3,2,1,0:T(1,128)S(1)}) custom-call(s32[2,65]{1,0:T(2,128)S(1)} %pad_add_fusion.tab, bf16[256,768]{1,0:T(8,128)(2,1)S(1)} %get-tuple-element.34.qr, bf16[3,32,256,128]{3,2,1,0:T(8,128)(2,1)S(1)} %bitcast.121), custom_call_target="tpu_custom_call" | custom-call | tf_op jit(solution)/shard_map/attend/pallas_call | solution.py:769
  238.3 2.4 fusion.18
  241.2 1.2 fusion.1
  244.3 7.9 %fusion.21 = f32[256,2176]{1,0:T(8,128)} fusion(bf16[256,2048]{1,0:T(8,128)(2,1)} %bitcast.127, bf16[2048,2176]{1,0:T(8,128)(2,1)} %bitcast.149), kind=kOutput, calls=%fused_computation.104 | convolution fusion | flops 2281701376 | bytes 12189696 | tf_op jit(solution)/shard_map/dot_general | solution.py:973
  252.2 2.8 multiply_reduce_fusion.1
  255.3 4.0 fusion.19
  259.3 5.4 multiply_convert_fusion
  264.7 7.5 %fusion.22 = f32[256,2048]{1,0:T(8,128)} fusion(bf16[256,2176]{1,0:T(8,128)(2,1)S(1)} %get-tuple-element.75, bf16[2048,2176]{1,0:T(8,128)(2,1)} %bitcast.155), kind=kOutput, calls=%fused_computation.105 | convolution fusion | flops 2281701376 | bytes 12124160 | tf_op jit(solution)/shard_map/dot_general | solution.py:976
  272.2 4.2 convolution_add_fusion
  276.5 14.8 %fusion.20 = f32[256,2048]{1,0:T(8,128)S(1)} fusion(bf16[256,2176]{1,0:T(8,128)(2,1)S(1)} %get-tuple-element.76, bf16[2048,2176]{1,0:T(8,128)(2,1)} %bitcast.150), kind=kOutput, calls=%fused_computation.103 | convolution fusion | flops 2281701376 | bytes 12124160 | tf_op jit(solution)/shard_map/dot_general | solution.py:972
  291.4 1.2 constant_dynamic-slice_fusion.1
  293.6 4.9 convolution_convert_fusion.1
  298.5 4.9 convolution_convert_fusion.2
  303.4 4.9 convolution_convert_fusion
  312.0 50.6 %attend_back.1 = (f32[256,768]{1,0:T(8,128)S(1)}, bf16[3,32,256,128]{3,2,1,0:T(8,128)(2,1)S(1)}) custom-call(s32[2,65]{1,0:T(2,128)S(1)} %pad_add_fusion.tab, bf16[256,768]{1,0:T(8,128)(2,1)S(1)} %get-tuple-element.34.qr, bf16[256,768]{1,0:T(8,128)(2,1)S(1)} %convolution_convert_fusion.5.da, f32[256,768]{1,0:T(8,128)S(1)} %copy-done.19, ...), custom_call_target="tpu_custom_call" | custom-call | tf_op jit(solution)/shard_map/attend_back/pallas_call | solution.py:864
  362.5 2.7 copy-done.3
  365.2 42.8 %sum_kv.1.dkv = f32[3,256,128]{2,1,0:T(8,128)S(1)} custom-call(bf16[3,2,4,4,256,128]{5,4,3,2,1,0:T(8,128)(2,1)} %bitcast.126), custom_call_target="tpu_custom_call" | custom-call | tf_op jit(solution)/shard_map/sum_kv/pallas_call | solution.py:612
  408.1 2.2 rope_back.1
  410.3 1.6 fusion.23
  412.0 4.4 collective-permute-start.3
  416.4 2.3 multiply_reduce_fusion.2
  419.9 2.7 convolution_convert_fusion.4
  422.6 3.8 convolution_convert_fusion.3
  426.8 2.7 concatenate.43
  430.1 138.1 %sum_weights.1 = (f32[2,16,2176]{2,1,0:T(8,128)}, f32[2,16,2176]{2,1,0:T(8,128)}, f32[2,16,2176]{2,1,0:T(8,128)}, f32[2,16,768]{2,1,0:T(8,128)}, f32[2,16,1152]{2,1,0:T(8,128)}, /*index=5*/f32[40,128]{1,0:T(8,128)}) custom-call(bf16[2,4,4,2,32,2176]{5,4,3,2,1,0:T(8,128)(2,1)} %bitcast.138, bf16[2,4,4,2,32,2176]{5,4,3,2,1,0:T(8,128)(2,1)} %bitcast.137, ...), custom_call_target="tpu_custom_call" | custom-call | tf_op jit(solution)/shard_map/sum_weights/pallas_call | solution.py:662
  568.2 1.3 dynamic_slice.44
  569.5 1.2 slice_multiply_fusion
  574.0 1.1 slice_bitcast_fusion.5
  577.6 1.3 fusion.12
  (160 shorter events, 30.3 us)
Async XLA Ops:
  0.6 8.6 %copy-start.38 = (bf16[33]{0:T(256)(128)(2,1)S(1)}, bf16[33]{0:T(256)(128)(2,1)}, u32[]{:S(2)}) copy-start(bf16[33]{0:T(256)(128)(2,1)} %param.13) | copy-start | bytes 202
  9.6 228.6 %copy-start.10 = (f32[256,128]{1,0:T(8,128)}, f32[256,128]{1,0:T(8,128)S(1)}, u32[]{:S(2)}) copy-start(f32[256,128]{1,0:T(8,128)S(1)} %get-tuple-element.105.cosine) | copy-start | bytes 393220
  9.6 228.6 %copy-start.12 = (f32[256,128]{1,0:T(8,128)}, f32[256,128]{1,0:T(8,128)S(1)}, u32[]{:S(2)}) copy-start(f32[256,128]{1,0:T(8,128)S(1)} %get-tuple-element.106.sine) | copy-start | bytes 393220
  199.4 38.9 %copy-start = (bf16[3,2,4,4,256,128]{5,4,3,2,1,0:T(8,128)(2,1)}, bf16[3,2,4,4,256,128]{5,4,3,2,1,0:T(8,128)(2,1)S(1)}, u32[]{:S(2)}) copy-start(bf16[3,2,4,4,256,128]{5,4,3,2,1,0:T(8,128)(2,1)S(1)} %get-tuple-element.35) | copy-start | bytes 18874372
  199.4 38.9 %copy-start.23 = (f32[40,128]{1,0:T(8,128)}, f32[40,128]{1,0:T(8,128)S(1)}, u32[]{:S(2)}) copy-start(f32[40,128]{1,0:T(8,128)S(1)} %get-tuple-element.38.gains) | copy-start | bytes 61444
  240.7 11.5 %collective-permute-start = (f32[256,2048]{1,0:T(8,128)}, f32[256,2048]{1,0:T(8,128)}, u32[]{:S(2)}, u32[]{:S(2)}) collective-permute-start(f32[256,2048]{1,0:T(8,128)} %fusion.18), channel_id=1, source_target_pairs={{0,1},{1,0},{2,3},{3,2},{4,5},{5,4},{6,7},{7,6},{8,9},{9,8},{10,11... | collective-permute-start | bytes 6291464 | tf_op jit(solution)/shard_map/ppermute | solution.py:906
  243.5 182.8 %copy-start.35 = (f32[128]{0:T(128)}, f32[128]{0:T(128)S(1)}, u32[]{:S(2)}) copy-start(f32[128]{0:T(128)S(1)} %get-tuple-element.104) | copy-start | bytes 1540
  244.3 182.1 %copy-start.33 = (f32[2048]{0:T(1024)}, f32[2048]{0:T(1024)S(1)}, u32[]{:S(2)}) copy-start(f32[2048]{0:T(1024)S(1)} %get-tuple-element.95) | copy-start | bytes 24580
  244.3 7.9 %copy-start.17 = (bf16[2,128,2048]{2,1,0:T(8,128)(2,1)S(1)}, bf16[2,128,2048]{2,1,0:T(8,128)(2,1)}, u32[]{:S(2)}) copy-start(bf16[2,128,2048]{2,1,0:T(8,128)(2,1)} %copy-done.16) | copy-start | bytes 3145732
  244.3 11.0 %slice-start.2 = ((s8[8912896]{0:T(1024)(128)(4,1)}), s8[4194304]{0:T(1024)(128)(4,1)S(1)}, s32[]{:S(2)}) async-start(s8[8912896]{0:T(1024)(128)(4,1)} %bitcast.151), calls=%async_computation.2 | async-start | bytes 8388608
  244.3 11.0 %slice-start.3 = ((s8[8912896]{0:T(1024)(128)(4,1)}), s8[4194304]{0:T(1024)(128)(4,1)S(1)}, s32[]{:S(2)}) async-start(s8[8912896]{0:T(1024)(128)(4,1)} %bitcast.151), calls=%async_computation.3 | async-start | bytes 8388608
  255.0 4.3 slice-start.5
  255.3 4.0 slice-start.6
  276.4 31.9 %collective-permute-start.2 = (f32[256,2048]{1,0:T(8,128)S(1)}, f32[256,2048]{1,0:T(8,128)S(1)}, u32[]{:S(2)}, u32[]{:S(2)}) collective-permute-start(f32[256,2048]{1,0:T(8,128)S(1)} %convolution_add_fusion), channel_id=1, source_target_pairs={{0,1},{1,0},{2,3},{3,2},{4,5},{5,4},{6,7},{7,6},{8,9},{9,8},{10,11... | collective-permute-start | bytes 6291464 | tf_op jit(solution)/shard_map/ppermute | solution.py:906
  291.3 7.2 %copy-start.30 = (f32[256,2048]{1,0:T(8,128)}, f32[256,2048]{1,0:T(8,128)S(1)}, u32[]{:S(2)}) copy-start(f32[256,2048]{1,0:T(8,128)S(1)} %fusion.20) | copy-start | bytes 6291460
  292.6 123.8 %collective-permute-start.1 = (f32[128,2048]{1,0:T(8,128)}, f32[128,2048]{1,0:T(8,128)}, u32[]{:S(2)}, u32[]{:S(2)}) collective-permute-start(f32[128,2048]{1,0:T(8,128)} %constant_dynamic-slice_fusion.1), channel_id=1, source_target_pairs={{0,1},{1,0},{2,3},{3,2},{4,5},{5,4},{6,7},{7,6},{8,9},{9,8},{10,11... | collective-permute-start | bytes 3145736 | tf_op jit(solution)/shard_map/ppermute | solution.py:906
  298.5 4.9 copy-start.5
  310.3 109.6 %copy-start.26 = (f32[256,2048]{1,0:T(8,128)}, f32[256,2048]{1,0:T(8,128)S(1)}, u32[]{:S(2)}) copy-start(f32[256,2048]{1,0:T(8,128)S(1)} %subtract_add_fusion) | copy-start | bytes 6291460
  312.0 98.3 %slice-start = ((s8[4718592]{0:T(1024)(128)(4,1)}), s8[4194304]{0:T(1024)(128)(4,1)S(1)}, s32[]{:S(2)}) async-start(s8[4718592]{0:T(1024)(128)(4,1)} %bitcast.134), calls=%async_computation | async-start | bytes 8388608
  365.2 42.8 %copy-start.11 = (f32[256,128]{1,0:T(8,128)S(1)}, f32[256,128]{1,0:T(8,128)}, u32[]{:S(2)}) copy-start(f32[256,128]{1,0:T(8,128)} %copy-done.10) | copy-start | bytes 393220
  365.2 42.8 %copy-start.13 = (f32[256,128]{1,0:T(8,128)S(1)}, f32[256,128]{1,0:T(8,128)}, u32[]{:S(2)}) copy-start(f32[256,128]{1,0:T(8,128)} %copy-done.12) | copy-start | bytes 393220
  365.2 42.8 %copy-start.15 = (f32[256,1152]{1,0:T(8,128)S(1)}, f32[256,1152]{1,0:T(8,128)}, u32[]{:S(2)}) copy-start(f32[256,1152]{1,0:T(8,128)} %copy-done.14) | copy-start | bytes 3538948
  365.2 42.8 %copy-start.24 = (f32[40,128]{1,0:T(8,128)S(1)}, f32[40,128]{1,0:T(8,128)}, u32[]{:S(2)}) copy-start(f32[40,128]{1,0:T(8,128)} %copy-done.23) | copy-start | bytes 61444
  365.2 45.0 %slice-start.1 = ((s8[4718592]{0:T(1024)(128)(4,1)}), s8[524288]{0:T(1024)(128)(4,1)S(1)}, s32[]{:S(2)}) async-start(s8[4718592]{0:T(1024)(128)(4,1)} %bitcast.134), calls=%async_computation.1 | async-start | bytes 1048576
  410.3 6.1 %copy-start.31 = (f32[256,2048]{1,0:T(8,128)S(1)}, f32[256,2048]{1,0:T(8,128)}, u32[]{:S(2)}) copy-start(f32[256,2048]{1,0:T(8,128)} %copy-done.30) | copy-start | bytes 6291460
  411.9 4.5 copy-start.29
  412.0 7.9 %copy-start.9 = (bf16[256,768]{1,0:T(8,128)(2,1)S(1)}, bf16[256,768]{1,0:T(8,128)(2,1)}, u32[]{:S(2)}) copy-start(bf16[256,768]{1,0:T(8,128)(2,1)} %copy-done.8) | copy-start | bytes 1179652
  412.0 14.4 %collective-permute-start.3 = (f32[128,2048]{1,0:T(8,128)S(1)}, f32[128,2048]{1,0:T(8,128)S(1)}, u32[]{:S(2)}, u32[]{:S(2)}) collective-permute-start(f32[128,2048]{1,0:T(8,128)S(1)} %constant_dynamic-slice_fusion), channel_id=1, source_target_pairs={{0,1},{1,0},{2,3},{3,2},{4,5},{5,4},{6,7},{7,6},{8,9},{9,8},{10,11... | collective-permute-start | bytes 3145736 | tf_op jit(solution)/shard_map/ppermute | solution.py:906
  568.2 8.0 %copy-start.32 = (f32[2,16,2176]{2,1,0:T(8,128)S(1)}, f32[2,16,2176]{2,1,0:T(8,128)}, u32[]{:S(2)}) copy-start(f32[2,16,2176]{2,1,0:T(8,128)} %get-tuple-element.56) | copy-start | bytes 835588
  568.2 9.4 %copy-start.34 = (f32[2048]{0:T(1024)S(1)}, f32[2048]{0:T(1024)}, u32[]{:S(2)}) copy-start(f32[2048]{0:T(1024)} %copy-done.33) | copy-start | bytes 24580
  568.2 9.4 %copy-start.36 = (f32[128]{0:T(128)S(1)}, f32[128]{0:T(128)}, u32[]{:S(2)}) copy-start(f32[128]{0:T(128)} %copy-done.35) | copy-start | bytes 1540
  568.2 9.3 %copy-start.37 = (f32[128]{0:T(128)S(1)}, f32[128]{0:T(128)}, u32[]{:S(2)}) copy-start(f32[128]{0:T(128)} %get-tuple-element.103) | copy-start | bytes 1540
  (19 other events, 39.8 us)

commit v3 on v2

--- a/solution.py
+++ b/solution.py
@@ -24,12 +24,14 @@
 FH = FF // 2
 KEYS = 512
 SPANS_STEP = KEYS // SPAN
-FULL_STEPS = 7
+KEY_BLOCKS = 8
 QROWS = GROUP * SPAN
 
 EPSILON = 1e-06
 ROPE_BASE = 10000.0
 LOG2E = 1.4426950408889634
+AT_H, AT_X, AT_Y, AT_HALF = 0, 64, 128, 192
+AT_STEP_HALF, AT_STEP_BLOCK, AT_MARK, AT_EDGE, AT_LIMIT, AT_MAP = 256, 259, 262, 266, 268, 270
 MESH = pl.DeviceIdType.MESH
 BF = jnp.bfloat16
 F32 = jnp.float32
@@ -48,13 +50,14 @@
     (0, 1152, 1024, ORDERS[0]),
     (1, 1152, 1024, ORDERS[1]),
     (2, 1152, 1024, ORDERS[2]),
+    (3, 0, 256, ORDERS[0]),
+    (3, 256, 256, ORDERS[1]),
+    (3, 512, 256, ORDERS[2]),
     (4, 0, 384, ORDERS[0]),
     (4, 384, 384, ORDERS[1]),
     (4, 768, 384, ORDERS[2]),
-    (3, 0, 256, ORDERS[0]),
-    (3, 256, 256, ORDERS[1]),
-    (3, 512, 256, ORDERS[2]),
 )
+N_EARLY = 9
 SIZES = {"x": 4, "y": 4, "z": 4, "h": 2}
 
 
@@ -200,9 +203,9 @@
 
 
 def front_kernel(
-    shard_one, shard_gate, shard_up, shard_down, shard_out, x, dy, gains, cosine, sine,
-    w_one, w_gate, w_up, w_down, w_out, x_pair, dy_pair, gain_all, joined, normed, query, kvg,
-    one, kv_src, small_buf, psem, lsem, tssem, trsem, ossem, orsem, gssem, grsem, kssem, krsem, ksem,
+    tab, shard_one, shard_gate, shard_up, shard_down, shard_out, x, dy, gains, cosine, sine,
+    w_one, w_gate, w_up, w_down, w_out, x_pair, dy_pair, gain_all, joined, normed, query, kv_out, o_ref, low_ref, l_ref,
+    one, kv_src, kvg, kvs, q_ref, acc, sum_ref, small_buf, psem, lsem, tssem, trsem, ossem, orsem, gssem, grsem, kssem, krsem, ksem,
 ):
     at = here()
     core = at["core"]
@@ -233,8 +236,8 @@
         Gathering(pairs[1 + a][1], W_DIMS, at, order, 32, pl.ds(start, width), gssem.at[k], grsem.at[k])
         for k, (a, start, width, order) in enumerate(GATHER)
     ]
-    kvs = [
-        Gathering(kvg.at[h], KV_DIMS, at, KV_ORDERS[h], 2 * TOK, slice(None), kssem.at[h], krsem.at[h]) for h in range(HH)
+    keys = [
+        Gathering(kvg.at[h], KV_DIMS, at, KV_ORDERS[h], 4, slice(None), kssem.at[h], krsem.at[h]) for h in range(HH)
     ]
 
     def every(streams, *steps):
@@ -294,38 +297,60 @@
 
     product(QW, KVW)
     for h in range(HH):
-        kv_src[h] = rope(QW // 128 + h, True)
+        kv_src[h] = rope(QW // 128 + h, True).reshape(4, SPAN, 2 * HD)
     kv_own = {d: at[d] for d in KV_DIMS}
     puts = [pltpu.make_async_copy(kv_src.at[h], pick(kvg.at[h], KV_DIMS, kv_own, ()), ksem.at[h]) for h in range(HH)]
     for c in puts:
         c.start()
     for c in puts:
         c.wait()
-    every(kvs, "start")
+    every(keys, "start")
     every(rest, "pass_on")
     product(0, 384)
-    every(kvs, "pass_on")
-    every(rest, "finish", "start")
+    every(keys, "pass_on")
+    every(rest, "finish")
+    every(keys, "finish", "start")
     product(384, 384)
-    every(kvs, "finish", "start")
+    every(keys, "pass_on")
     for t in range(QW // 128):
         query[:, t * 128 : (t + 1) * 128] = rope(t, False)
-    every(kvs, "pass_on")
-    every(kvs, "finish", "start")
+    every(keys, "finish", "start")
+    every(rest[:3], "start")
+    blank = jnp.zeros((QROWS, HD), BF)
+    for s in range(2):
+        for h in range(HH):
+            for half in range(2):
+                q_ref[s, h, half] = jnp.concatenate([heads_at(query, s, h, half), blank], axis=1)
+    every(keys, "pass_on")
+    every(rest[3:], "start")
+    every(keys, "finish")
+
+    def sort(p, carry):
+        for s in range(2):
+            place = tuple(tab[s, column + p] for column in (AT_H, AT_X, AT_Y))
+            half = tab[s, AT_HALF + p]
+            for h in range(HH):
+                kvs[s, h, lax.div(p, SPANS_STEP), lax.rem(p, SPANS_STEP)] = kvg[(h,) + place + (s * 2 + half,)]
+        return carry
+
+    lax.fori_loop(0, 2 * N_CTX, sort, 0)
+    keep_keys = pltpu.make_async_copy(kvs, kv_out, ksem.at[HH])
+    keep_keys.start()
+    attend_heads(tab, 0, q_ref, kvs, o_ref, low_ref, l_ref, acc, sum_ref)
     every(rest[:3], "pass_on")
-    every(kvs, "pass_on")
+    attend_heads(tab, 1, q_ref, kvs, o_ref, low_ref, l_ref, acc, sum_ref)
     every(rest[3:], "pass_on")
-    every(kvs, "finish")
     every(rest, "finish")
+    keep_keys.wait()
     arrived(6)
     keep.wait()
     for c in remote + total.sent:
         c.wait_send()
-    for s in ones + rest + kvs:
+    for s in ones + rest + keys:
         s.wait_sent()
 
 
-def front(shards, x, dy, gains, cosine, sine, cid):
+def front(tab, shards, x, dy, gains, cosine, sine, cid):
     anywhere = pl.BlockSpec(memory_space=pl.ANY)
     vmem = pl.BlockSpec(memory_space=pltpu.VMEM)
     full = [jax.ShapeDtypeStruct((2, 4, 4, 2, 32, s.shape[-1]), BF) for s in shards]
@@ -340,13 +365,21 @@
             jax.ShapeDtypeStruct((2 * TOK, QW + KVW), F32),
             jax.ShapeDtypeStruct((2 * TOK, D), BF),
             jax.ShapeDtypeStruct((2 * TOK, QW), BF),
-            jax.ShapeDtypeStruct((HH, 2, 4, 4, 2 * TOK, 2 * HD), BF),
+            jax.ShapeDtypeStruct((2, HH, KEY_BLOCKS, SPANS_STEP, SPAN, 2 * HD), BF),
+            jax.ShapeDtypeStruct((2 * TOK, QW), F32),
+            jax.ShapeDtypeStruct((2 * TOK, QW), BF),
+            jax.ShapeDtypeStruct((2, HH, 2, 1, QROWS), F32),
         ],
-        in_specs=[anywhere] * 7 + [vmem] * 3,
-        out_specs=[anywhere] * 5 + [vmem, anywhere] + [vmem] * 4 + [anywhere],
+        in_specs=[pl.BlockSpec(memory_space=pltpu.SMEM)] + [anywhere] * 7 + [vmem] * 3,
+        out_specs=[anywhere] * 5 + [vmem, anywhere] + [vmem] * 4 + [anywhere] + [vmem] * 3,
         scratch_shapes=[
             pltpu.VMEM((2, 4, 4, 2, 32, QW + KVW), BF),
-            pltpu.VMEM((HH, 2 * TOK, 2 * HD), BF),
+            pltpu.VMEM((HH, 4, SPAN, 2 * HD), BF),
+            pltpu.VMEM((HH, 2, 4, 4, 4, SPAN, 2 * HD), BF),
+            pltpu.VMEM((2, HH, KEY_BLOCKS, SPANS_STEP, SPAN, 2 * HD), BF),
+            pltpu.VMEM((2, HH, 2, QROWS, 2 * HD), BF),
+            pltpu.VMEM((2, 2 * HD, QROWS), F32),
+            pltpu.VMEM((2, 1, QROWS), F32),
             pltpu.VMEM((4, 4) + gains.shape, F32),
             pltpu.SemaphoreType.DMA((7, 2)),
             pltpu.SemaphoreType.DMA((8,)),
@@ -358,13 +391,13 @@
             pltpu.SemaphoreType.DMA((n, 3, 4)),
             pltpu.SemaphoreType.DMA((HH, 3, 4)),
             pltpu.SemaphoreType.DMA((HH, 3, 4)),
-            pltpu.SemaphoreType.DMA((HH,)),
+            pltpu.SemaphoreType.DMA((HH + 1,)),
         ],
         compiler_params=pltpu.CompilerParams(
-            collective_id=cid, has_side_effects=True, vmem_limit_bytes=32 * 1024 * 1024
+            collective_id=cid, has_side_effects=True, vmem_limit_bytes=48 * 1024 * 1024
         ),
         name="front",
-    )(*shards, x, dy, gains, cosine, sine)
+    )(tab, *shards, x, dy, gains, cosine, sine)
 
 
 def rope_back_kernel(joined, dq, dkv, gains, cosine, sine, out, terms):
@@ -413,8 +446,8 @@
 
 
 class Summing:
-    def __init__(self, source, dims, at, order, rows, cols, buffers, ssem, rsem, lsem):
-        self.ref, self.dims, self.at, self.order = source, dims, at, order
+    def __init__(self, source, dims, at, order, rows, cols, buffers, ssem, rsem, lsem, begun=None):
+        self.ref, self.dims, self.at, self.order, self.begun = source, dims, at, order, begun
         self.cols, self.buffers, self.rows = cols, buffers, rows
         self.ssem, self.rsem, self.lsem = ssem, rsem, lsem
         self.phase, self.sent = 0, []
@@ -440,6 +473,10 @@
             self.direct = (self.send(0, self.part(1 - i, every), buf["got"].at[0], 1),)
         else:
             up, down, far = lax.rem(i + 1, 4), lax.rem(i + 3, 4), lax.rem(i + 2, 4)
+            self.near = (up, down)
+        if self.phase == 0 and self.begun is not None:
+            self.relay, self.direct = (), ()
+        elif SIZES[self.axis] == 4:
             self.relay = (
                 self.send(0, self.part(far, first), buf["relay"].at[0], 1),
                 self.send(1, self.part(far, second), buf["relay"].at[1], 3),
@@ -448,12 +485,15 @@
                 self.send(2, self.part(up, second), buf["got"].at[1, 1], 1),
                 self.send(3, self.part(down, first), buf["got"].at[0, 1], 3),
             )
-            self.near = (up, down)
         if self.phase == 0:
             todo = [(self.part(i, every), buf["mine"])]
             if SIZES[self.axis] == 4:
                 todo.append((self.part(up, first), buf["own"].at[0]))
                 todo.append((self.part(down, second), buf["own"].at[1]))
+            if self.begun is not None:
+                todo.append((self.begun[0], buf["relay"]))
+                todo.append((self.begun[1].at[0], buf["got"].at[0, 1]))
+                todo.append((self.begun[1].at[1], buf["got"].at[1, 1]))
             for n, (src, dst) in enumerate(todo):
                 c = pltpu.make_async_copy(src, dst, self.lsem.at[n])
                 c.start()
@@ -481,7 +521,10 @@
         buf = self.buffers[self.phase]
         half = self.rows // 2
         for n, by in ((0, 1), (1, 3)):
-            self.relay[n].wait_recv()
+            if self.relay:
+                self.relay[n].wait_recv()
+            elif n == 0:
+                self.local[3].wait()
             if self.phase == 0:
                 self.local[1 + n].wait()
                 own = buf["own"].at[n]
@@ -502,6 +545,8 @@
         half = self.rows // 2
         if self.local:
             self.local[0].wait()
+        for c in self.local[4:]:
+            c.wait()
         for c in self.direct:
             c.wait_recv()
         own = buf["mine"] if self.phase == 0 else self.part(self.at[self.axis], pl.ds(0, self.rows))
@@ -596,46 +641,19 @@
     return buffers
 
 
-def kv_sum_kernel(src, out, buffers, ssem, rsem, lsem):
-    at = here()
-    greet(neighbours(at, ("h", "x", "y")))
-    streams = [
-        Summing(src.at[h], KV_DIMS, at, KV_SUM_ORDERS[h], 2 * TOK, slice(None), buffers[h], ssem.at[h], rsem.at[h], lsem.at[h])
-        for h in range(HH)
-    ]
-    run_sums(streams)
-    for h in range(HH):
-        out[h] = buffers[h][2]["sum"][...]
-
-
-def sum_kv(grads, cid):
-    return pl.pallas_call(
-        kv_sum_kernel,
-        out_shape=jax.ShapeDtypeStruct((HH, 2 * TOK, 2 * HD), F32),
-        in_specs=[pl.BlockSpec(memory_space=pl.ANY)],
-        out_specs=pl.BlockSpec(memory_space=pltpu.VMEM),
-        scratch_shapes=[
-            [sum_scratch(KV_SUM_ORDERS[h], KV_DIMS, 2 * TOK, 2 * HD) for h in range(HH)],
-            pltpu.SemaphoreType.DMA((HH, 3, 6)),
-            pltpu.SemaphoreType.DMA((HH, 3, 6)),
-            pltpu.SemaphoreType.DMA((HH, 3)),
-        ],
-        compiler_params=pltpu.CompilerParams(
-            collective_id=cid, has_side_effects=True, vmem_limit_bytes=48 * 1024 * 1024
-        ),
-        name="sum_kv",
-    )(grads)
-
-
 def weight_sum_kernel(pieces, n, *refs):
-    ins, small, outs, small_out = refs[:n], refs[n], refs[n + 1 : 2 * n + 1], refs[2 * n + 1]
-    buffers, stages, swapped, small_buf, ssem, rsem, lsem, csem, tssem, trsem = refs[2 * n + 2 :]
+    ins, small, begun, refs = refs[:n], refs[n], refs[n + 1 : n + 1 + 2 * N_EARLY], refs[n + 1 + 2 * N_EARLY :]
+    outs, small_out = refs[:n], refs[n]
+    buffers, stages, swapped, small_buf, ssem, rsem, lsem, csem, tssem, trsem = refs[n + 1 :]
     at = here()
     core = at["core"]
     sibling = moved(at, "core", 1)
     greet([sibling] + sum_peers(at, ("x", "y", "z")))
     streams = [
-        Summing(ins[a], W_DIMS, at, order, 32, pl.ds(start, width), buffers[k], ssem.at[k], rsem.at[k], lsem.at[k])
+        Summing(
+            ins[a], W_DIMS, at, order, 32, pl.ds(start, width), buffers[k], ssem.at[k], rsem.at[k], lsem.at[k],
+            (begun[2 * k], begun[2 * k + 1]) if k < N_EARLY else None,
+        )
         for k, (a, start, width, order) in enumerate(pieces)
     ]
     total = Total(small[...], at, small_buf, tssem, trsem)
@@ -654,7 +672,7 @@
         c.wait_send()
 
 
-def sum_weights(grads, small, pieces, cid, limit):
+def sum_weights(grads, small, begun, pieces, cid, limit):
     n, k = len(grads), len(pieces)
     anywhere = pl.BlockSpec(memory_space=pl.ANY)
     vmem = pl.BlockSpec(memory_space=pltpu.VMEM)
@@ -662,7 +680,7 @@
     return pl.pallas_call(
         functools.partial(weight_sum_kernel, pieces, n),
         out_shape=[jax.ShapeDtypeStruct((2, 16, w), F32) for w in widths] + [jax.ShapeDtypeStruct(small.shape, F32)],
-        in_specs=[anywhere] * n + [vmem],
+        in_specs=[anywhere] * n + [vmem] + [anywhere] * len(begun),
         out_specs=[vmem] * (n + 1),
         scratch_shapes=[
             [sum_scratch(order, W_DIMS, 32, width) for a, start, width, order in pieces],
@@ -671,14 +689,14 @@
             pltpu.VMEM((4, 4) + small.shape, F32),
             pltpu.SemaphoreType.DMA((k, 3, 6)),
             pltpu.SemaphoreType.DMA((k, 3, 6)),
-            pltpu.SemaphoreType.DMA((k, 3)),
+            pltpu.SemaphoreType.DMA((k, 6)),
             pltpu.SemaphoreType.DMA((n, 2)),
             pltpu.SemaphoreType.DMA((4, 4)),
             pltpu.SemaphoreType.DMA((4, 4)),
         ],
         compiler_params=pltpu.CompilerParams(collective_id=cid, has_side_effects=True, vmem_limit_bytes=limit),
         name="sum_weights",
-    )(*[g.reshape(2, 4, 4, 2, 32, g.shape[-1]) for g in grads], small)
+    )(*[g.reshape(2, 4, 4, 2, 32, g.shape[-1]) for g in grads], small, *begun)
 
 
 def sum_peers(at, axes):
@@ -689,199 +707,243 @@
     return out
 
 
-def fetch_keys(tab, kvg, kv, sems):
-    for s in range(2):
-        for h in range(HH):
-
-            def go(p, carry):
-                slot = tab[s, p]
-                row = lax.rem(slot, 2) * SPAN + s * TOK
-                pltpu.make_async_copy(
-                    kvg.at[h, lax.div(slot, 2), pl.ds(pl.multiple_of(row, SPAN), SPAN)],
-                    kv.at[s, h, pl.ds(pl.multiple_of(p * SPAN, SPAN), SPAN)],
-                    sems.at[s, h],
-                ).start()
-                return carry
-
-            lax.fori_loop(0, 2 * N_CTX, go, 0)
-
-
-def step_of(t, low_steps):
-    half = jnp.where(t < low_steps, 0, 1)
-    return half, jnp.where(t < low_steps, t, t - low_steps)
-
-
-def heads_at(ref, s, h, half, width=HD):
+def heads_at(ref, s, h, half):
     rows = slice(s * TOK + half * SPAN, s * TOK + (half + 1) * SPAN)
     return jnp.concatenate([ref[rows, (h * GROUP + g) * HD : (h * GROUP + g + 1) * HD] for g in range(GROUP)], axis=0)
 
 
 def put_heads(ref, s, h, half, value):
-    rows = slice(s * TOK + half * SPAN, s * TOK + (half + 1) * SPAN)
+    rows = pl.ds(pl.multiple_of(s * TOK + half * SPAN, SPAN), SPAN)
     for g in range(0, GROUP, 2):
         both = jnp.concatenate([value[g * SPAN : (g + 1) * SPAN], value[(g + 1) * SPAN : (g + 2) * SPAN]], axis=1)
-        ref[rows, (h * GROUP + g) * HD : (h * GROUP + g + 2) * HD] = both.astype(ref.dtype)
-
-
-def attend_kernel(tab, qr, kvg, o_ref, low_ref, l_ref, kv, q_ref, acc, total, sems):
-    fetch_keys(tab, kvg, kv, sems)
+        ref[rows, pl.ds(pl.multiple_of((h * GROUP + g) * HD, 2 * HD), 2 * HD)] = both.astype(ref.dtype)
+
+
+def masked(prob, limit):
+    if limit is None:
+        return prob
+    row = lax.broadcasted_iota(jnp.int32, prob.shape, 0)
+    col = lax.rem(lax.broadcasted_iota(jnp.int32, prob.shape, 1), SPAN)
+    return jnp.where(row <= col + limit, prob, 0.0)
+
+
+def attend_heads(tab, s, q_ref, kvs, o_ref, low_ref, l_ref, acc, total):
     rate = LOG2E * HD**-0.5
+
+    def head(h, carry):
+        acc[...] = jnp.zeros_like(acc)
+        total[...] = jnp.zeros_like(total)
+
+        def scored(half, block, limit):
+            keys = kvs[s, h, block].reshape(KEYS, 2 * HD)
+            scores = lax.dot_general(keys, q_ref[s, h, half], NT, preferred_element_type=F32)
+            prob = masked(jnp.exp2(scores * rate), limit)
+            return (
+                jnp.sum(prob, axis=0, keepdims=True),
+                lax.dot_general(keys, prob.astype(BF), TN, preferred_element_type=F32),
+            )
+
+        def high(k, c):
+            t, o = scored(1, k, None)
+            total[1] += t
+            acc[1] += o
+            return c
+
+        def either(k, c):
+            half = tab[s, AT_STEP_HALF + k]
+            t, o = scored(half, tab[s, AT_STEP_BLOCK + k], None)
+            up = half.astype(F32)
+            total[0] += t * (1.0 - up)
+            total[1] += t * up
+            acc[0] += o * (1.0 - up)
+            acc[1] += o * up
+            return c
+
+        lax.fori_loop(0, 4, high, 0)
+        lax.fori_loop(0, 3, either, 0)
+        for half in range(2):
+            t, o = scored(half, tab[s, AT_EDGE + half], tab[s, AT_LIMIT + half])
+            t, o = total[half] + t, acc[half] + o
+            out = (o[HD:, :] / t).T
+            put_heads(o_ref, s, h, half, out)
+            put_heads(low_ref, s, h, half, out)
+            l_ref[s, h, half] = jnp.log2(t)
+        return carry
+
+    lax.fori_loop(0, HH, head, 0)
+
+
+class Early:
+    def __init__(self, source, at, order, cols, relay, direct, ssem, rsem):
+        axis = order[0]
+        i = at[axis]
+        up, down, far = lax.rem(i + 1, 4), lax.rem(i + 3, 4), lax.rem(i + 2, 4)
+        self.copies = []
+        plan = ((far, 0, relay, 0, 1), (far, 1, relay, 1, 3), (up, 1, direct, 1, 1), (down, 0, direct, 0, 3))
+        for n, (coordinate, half, dst, slot, by) in enumerate(plan):
+            src = pick(source, W_DIMS, labels(axis, coordinate), (pl.ds(half * 16, 16), cols))
+            self.copies.append(send(src, dst.at[slot], ssem.at[n], rsem.at[n], moved(at, axis, by)))
+
+    def wait(self):
+        for c in self.copies:
+            c.wait_recv()
+        for c in self.copies:
+            c.wait_send()
+
+
+def early_shapes():
+    shapes = []
+    for a, start, width, order in SUMS[:N_EARLY]:
+        lead = lead_shape(without(W_DIMS, order[0]))
+        shapes += [jax.ShapeDtypeStruct((2,) + lead + (16, width), BF)] * 2
+    return shapes
+
+
+def attend_back_kernel(*refs):
+    tab, qr, da, attn, l_ref, kv_sorted = refs[:6]
+    grads, refs = refs[6:10], refs[10:]
+    dq_ref, dkv_out = refs[:2]
+    begun, refs = refs[2 : 2 + 2 * N_EARLY], refs[2 + 2 * N_EARLY :]
+    kvs, qd_ref, delta_ref, stage, acc, dq_acc, buffers, essem, ersem, ssem, rsem, lsem, sems = refs
+    at = here()
+    greet(neighbours(at, ("x", "y", "z", "h")))
+    early = [
+        Early(grads[a], at, order, pl.ds(start, width), begun[2 * k], begun[2 * k + 1], essem.at[k], ersem.at[k])
+        for k, (a, start, width, order) in enumerate(SUMS[:N_EARLY])
+    ]
+    loads = []
+    for h in range(HH):
+        for s in range(2):
+            loads.append(pltpu.make_async_copy(kv_sorted.at[s, h], kvs.at[s, h], sems.at[s, h]))
+            loads[-1].start()
+    rate = LOG2E * HD**-0.5
+    factor = jnp.where(lax.broadcasted_iota(jnp.int32, (1, 2 * HD), 1) < HD, HD**-0.5, 1.0)
     blank = jnp.zeros((QROWS, HD), BF)
     for s in range(2):
         for h in range(HH):
             for half in range(2):
-                q_ref[s, h, half] = jnp.concatenate([heads_at(qr, s, h, half), blank], axis=1)
-    for s in range(2):
-        span = tab[s, 2 * N_CTX]
-        low_steps = lax.div(span, SPANS_STEP)
-        for h in range(HH):
-            pltpu.make_async_copy(kv.at[s, h], kv.at[s, h], sems.at[s, h]).wait()
-            acc[...] = jnp.zeros_like(acc)
-            total[...] = jnp.zeros_like(total)
-
-            def step(half, block, limit):
-                keys = kv[s, h, pl.ds(pl.multiple_of(block * KEYS, KEYS), KEYS), :]
-                scores = lax.dot_general(keys, q_ref[s, h, half], NT, preferred_element_type=F32)
-                prob = jnp.exp2(scores * rate)
-                if limit is not None:
-                    row = lax.broadcasted_iota(jnp.int32, prob.shape, 0)
-                    col = lax.rem(lax.broadcasted_iota(jnp.int32, prob.shape, 1), SPAN)
-                    prob = jnp.where(row <= col + limit, prob, 0.0)
-                total[half] += jnp.sum(prob, axis=0, keepdims=True)
-                acc[half] += lax.dot_general(keys, prob.astype(BF), TN, preferred_element_type=F32)
-
-            def full(t, carry):
-                half, block = step_of(t, low_steps)
-                step(half, block, None)
-                return carry
-
-            lax.fori_loop(0, FULL_STEPS, full, 0)
-            for half, first in ((0, span), (1, 2 * N_CTX - 1 - span)):
-                step(half, lax.div(first, SPANS_STEP), lax.rem(first, SPANS_STEP) * SPAN)
-                out = (acc[half, HD:, :] / total[half]).T
-                put_heads(o_ref, s, h, half, out)
-                put_heads(low_ref, s, h, half, out)
-                l_ref[s, h, half] = jnp.log2(total[half])
-
-
-def attend(tab, query, kvg):
-    vmem = pl.BlockSpec(memory_space=pltpu.VMEM)
-    return pl.pallas_call(
-        attend_kernel,
-        out_shape=[
-            jax.ShapeDtypeStruct((2 * TOK, QW), F32),
-            jax.ShapeDtypeStruct((2 * TOK, QW), BF),
-            jax.ShapeDtypeStruct((2, HH, 2, 1, QROWS), F32),
-        ],
-        in_specs=[pl.BlockSpec(memory_space=pltpu.SMEM), vmem, pl.BlockSpec(memory_space=pl.ANY)],
-        out_specs=[vmem, vmem, vmem],
-        scratch_shapes=[
-            pltpu.VMEM((2, HH, N_CTX * TOK, 2 * HD), BF),
-            pltpu.VMEM((2, HH, 2, QROWS, 2 * HD), BF),
-            pltpu.VMEM((2, 2 * HD, QROWS), F32),
-            pltpu.VMEM((2, 1, QROWS), F32),
-            pltpu.SemaphoreType.DMA((2, HH)),
-        ],
-        compiler_params=pltpu.CompilerParams(vmem_limit_bytes=32 * 1024 * 1024),
-        name="attend",
-    )(tab, query, kvg)
-
-
-def attend_back_kernel(
-    tab, qr, da, attn, l_ref, kvg, dq_ref, dkv_ref, kv, qd_ref, delta_ref, stage, acc, dq_acc, sems, osems
-):
-    fetch_keys(tab, kvg, kv, sems)
-    blank = jnp.zeros((QROWS, HD), BF)
-    for s in range(2):
-        for h in range(HH):
-            for half in range(2):
-                grads = heads_at(da, s, h, half)
+                up = heads_at(da, s, h, half)
                 qd_ref[s, h, half, :QROWS] = jnp.concatenate([heads_at(qr, s, h, half), blank], axis=1)
-                qd_ref[s, h, half, QROWS:] = jnp.concatenate([blank, grads], axis=1)
-                inner = (grads.astype(F32) * heads_at(attn, s, h, half)).T
+                qd_ref[s, h, half, QROWS:] = jnp.concatenate([blank, up], axis=1)
+                inner = (up.astype(F32) * heads_at(attn, s, h, half)).T
                 delta_ref[s, h, half] = jnp.sum(inner, axis=0, keepdims=True)
-    rate = LOG2E * HD**-0.5
-    lanes = lax.broadcasted_iota(jnp.int32, (1, 2 * HD), 1)
-    factor = jnp.where(lanes < HD, HD**-0.5, 1.0)
-    for s in range(2):
-        span = tab[s, 2 * N_CTX]
-        low_steps = lax.div(span, SPANS_STEP)
-        for h in range(HH):
-            pltpu.make_async_copy(kv.at[s, h], kv.at[s, h], sems.at[s, h]).wait()
+    for c in loads:
+        c.wait()
+    streams = [
+        Summing(stage.at[h], KV_DIMS, at, KV_SUM_ORDERS[h], 2 * TOK, slice(None), buffers[h], ssem.at[h], rsem.at[h], lsem.at[h])
+        for h in range(HH)
+    ]
+    todo = [["pass_on", "finish", "start", "pass_on", "finish", "start", "pass_on", "finish"] for h in range(HH)]
+    for h in range(HH):
+
+        def sequence(s, carry):
             dq_acc[...] = jnp.zeros_like(dq_acc)
             acc[...] = jnp.zeros_like(acc)
 
-            def step(half, block, limit):
-                rows = pl.ds(pl.multiple_of(block * KEYS, KEYS), KEYS)
-                keys = kv[s, h, rows, :]
+            def backward(half, block, limit):
+                keys = kvs[s, h, block].reshape(KEYS, 2 * HD)
                 both = lax.dot_general(keys, qd_ref[s, h, half], NT, preferred_element_type=F32)
-                prob = jnp.exp2(both[:, :QROWS] * rate - l_ref[s, h, half])
-                if limit is not None:
-                    row = lax.broadcasted_iota(jnp.int32, prob.shape, 0)
-                    col = lax.rem(lax.broadcasted_iota(jnp.int32, prob.shape, 1), SPAN)
-                    prob = jnp.where(row <= col + limit, prob, 0.0)
+                prob = masked(jnp.exp2(both[:, :QROWS] * rate - l_ref[s, h, half]), limit)
                 grad = (prob * (both[:, QROWS:] - delta_ref[s, h, half])).astype(BF)
                 pair = jnp.concatenate([grad, prob.astype(BF)], axis=1)
-                acc[rows, :] += lax.dot_general(pair, qd_ref[s, h, half], NN, preferred_element_type=F32)
-                dq_acc[half] += lax.dot_general(keys, grad, TN, preferred_element_type=F32)
-
-            def full(t, carry):
-                half, block = step_of(t, low_steps)
-                step(half, block, None)
-                return carry
-
-            lax.fori_loop(0, FULL_STEPS, full, 0)
-            for half, first in ((0, span), (1, 2 * N_CTX - 1 - span)):
-                step(half, lax.div(first, SPANS_STEP), lax.rem(first, SPANS_STEP) * SPAN)
-                put_heads(dq_ref, s, h, half, (dq_acc[half, :HD, :] * HD**-0.5).T)
-
-            def cast(b, carry):
-                rows = pl.ds(pl.multiple_of(b * KEYS, KEYS), KEYS)
-                stage[s, h, rows, :] = (acc[rows, :] * factor).astype(BF)
-                return carry
-
-            lax.fori_loop(0, N_CTX * TOK // KEYS, cast, 0)
-
-            def put(p, carry):
-                slot = tab[s, p]
-                row = lax.rem(slot, 2) * SPAN + s * TOK
-                pltpu.make_async_copy(
-                    stage.at[s, h, pl.ds(pl.multiple_of(p * SPAN, SPAN), SPAN)],
-                    dkv_ref.at[h, lax.div(slot, 2), pl.ds(pl.multiple_of(row, SPAN), SPAN)],
-                    osems.at[s, h],
-                ).start()
-                return carry
-
-            lax.fori_loop(0, 2 * N_CTX, put, 0)
-    for s in range(2):
-        for h in range(HH):
-            pltpu.make_async_copy(stage.at[s, h], stage.at[s, h], osems.at[s, h]).wait()
-
-
-def attend_back(tab, query, grad_attn, attn, log_sum, kvg):
+                kv = lax.dot_general(pair, qd_ref[s, h, half], NN, preferred_element_type=F32)
+                return (
+                    kv.reshape(SPANS_STEP, SPAN, 2 * HD),
+                    lax.dot_general(keys, grad, TN, preferred_element_type=F32),
+                )
+
+            def spans(block):
+                return pl.ds(block * SPANS_STEP, SPANS_STEP)
+
+            def high(k, c):
+                kv, q = backward(1, k, None)
+                acc[spans(k)] += kv
+                dq_acc[1] += q
+                return c
+
+            def either(k, c):
+                half = tab[s, AT_STEP_HALF + k]
+                kv, q = backward(half, tab[s, AT_STEP_BLOCK + k], None)
+                up = half.astype(F32)
+                acc[spans(k)] += kv * (1.0 - up)
+                acc[spans(6 - k)] += kv * up
+                dq_acc[0] += q * (1.0 - up)
+                dq_acc[1] += q * up
+                return c
+
+            lax.fori_loop(0, 4, high, 0)
+            lax.fori_loop(0, 3, either, 0)
+            for half in range(2):
+                kv, q = backward(half, tab[s, AT_EDGE + half], tab[s, AT_LIMIT + half])
+                for k in range(4):
+                    acc[spans(k if half == 0 else 7 - k)] += kv * tab[s, AT_MARK + k].astype(F32)
+                q = dq_acc[half] + q
+                put_heads(dq_ref, s, h, half, (q[:HD, :] * HD**-0.5).T)
+
+            def put(j, c):
+                for half in range(2):
+                    v = acc[tab[s, AT_MAP + half * N_CTX + j]] * factor
+                    rows = pl.ds(pl.multiple_of(s * TOK + half * SPAN, SPAN), SPAN)
+                    stage[h, lax.div(j, 16), lax.rem(lax.div(j, 4), 4), lax.rem(j, 4), rows, :] = v.astype(BF)
+                return c
+
+            lax.fori_loop(0, N_CTX, put, 0)
+            return carry
+
+        lax.fori_loop(0, 2, sequence, 0)
+        for k in range(h):
+            for step in range(1 if k == h - 1 else 2):
+                getattr(streams[k], todo[k].pop(0))()
+        streams[h].start()
+    while any(todo):
+        for k in range(HH):
+            if todo[k]:
+                name = todo[k].pop(0)
+                getattr(streams[k], name)()
+                if name == "finish" and todo[k]:
+                    getattr(streams[k], todo[k].pop(0))()
+    for h in range(HH):
+        dkv_out[h] = buffers[h][2]["sum"][...]
+    for e in early:
+        e.wait()
+    for st in streams:
+        for c in st.sent:
+            c.wait_send()
+
+
+def attend_back(tab, query, grad_attn, attn, log_sum, kv_sorted, grads, cid):
     vmem = pl.BlockSpec(memory_space=pltpu.VMEM)
     anywhere = pl.BlockSpec(memory_space=pl.ANY)
-    return pl.pallas_call(
+    out = pl.pallas_call(
         attend_back_kernel,
         out_shape=[
             jax.ShapeDtypeStruct((2 * TOK, QW), F32),
-            jax.ShapeDtypeStruct((HH, N_CTX, 2 * TOK, 2 * HD), BF),
-        ],
-        in_specs=[pl.BlockSpec(memory_space=pltpu.SMEM), vmem, vmem, vmem, vmem, anywhere],
-        out_specs=[vmem, anywhere],
+            jax.ShapeDtypeStruct((HH, 2 * TOK, 2 * HD), F32),
+        ]
+        + early_shapes(),
+        in_specs=[pl.BlockSpec(memory_space=pltpu.SMEM)] + [vmem] * 4 + [anywhere] * 5,
+        out_specs=[vmem, vmem] + [anywhere] * (2 * N_EARLY),
         scratch_shapes=[
-            pltpu.VMEM((2, HH, N_CTX * TOK, 2 * HD), BF),
+            pltpu.VMEM((2, HH, KEY_BLOCKS, SPANS_STEP, SPAN, 2 * HD), BF),
             pltpu.VMEM((2, HH, 2, 2 * QROWS, 2 * HD), BF),
             pltpu.VMEM((2, HH, 2, 1, QROWS), F32),
-            pltpu.VMEM((2, HH, N_CTX * TOK, 2 * HD), BF),
-            pltpu.VMEM((N_CTX * TOK, 2 * HD), F32),
+            pltpu.VMEM((HH, 2, 4, 4, 2 * TOK, 2 * HD), BF),
+            pltpu.VMEM((2 * N_CTX, SPAN, 2 * HD), F32),
             pltpu.VMEM((2, 2 * HD, QROWS), F32),
-            pltpu.SemaphoreType.DMA((2, HH)),
+            [sum_scratch(KV_SUM_ORDERS[h], KV_DIMS, 2 * TOK, 2 * HD) for h in range(HH)],
+            pltpu.SemaphoreType.DMA((N_EARLY, 4)),
+            pltpu.SemaphoreType.DMA((N_EARLY, 4)),
+            pltpu.SemaphoreType.DMA((HH, 3, 6)),
+            pltpu.SemaphoreType.DMA((HH, 3, 6)),
+            pltpu.SemaphoreType.DMA((HH, 3)),
             pltpu.SemaphoreType.DMA((2, HH)),
         ],
-        compiler_params=pltpu.CompilerParams(vmem_limit_bytes=40 * 1024 * 1024),
+        compiler_params=pltpu.CompilerParams(
+            collective_id=cid, has_side_effects=True, vmem_limit_bytes=48 * 1024 * 1024
+        ),
         name="attend_back",
-    )(tab, query, grad_attn, attn, log_sum, kvg)
+    )(tab, query, grad_attn, attn, log_sum, kv_sorted, *[g.reshape(2, 4, 4, 2, 32, g.shape[-1]) for g in grads])
+    return out[0], out[1], out[2:]
 
 
 def permutation(axis, by):
@@ -940,7 +1002,30 @@
     positions = (spans[:, :, None] * SPAN + jnp.arange(SPAN, dtype=jnp.int32)).reshape(2 * TOK)
     match = maps[:, None, :] == jnp.arange(N_CTX, dtype=jnp.int32)[None, :, None]
     inverse_map = jnp.sum(jnp.where(match, jnp.arange(N_CTX, dtype=jnp.int32), 0), axis=2)
-    tab = jnp.concatenate([inverse_map * 2, inverse_map[:, ::-1] * 2 + 1, own_span], axis=1)
+    holder = jnp.concatenate([inverse_map, inverse_map[:, ::-1]], axis=1)
+    upper = (jnp.arange(2 * N_CTX, dtype=jnp.int32) >= N_CTX).astype(jnp.int32)[None, :] + jnp.zeros_like(holder)
+    low_block = own_span // SPANS_STEP
+    low_limit = own_span % SPANS_STEP * SPAN
+    three = jnp.arange(3, dtype=jnp.int32)[None, :]
+    step_half = (three >= low_block).astype(jnp.int32)
+    tab = jnp.concatenate(
+        [
+            holder // 16,
+            holder // 4 % 4,
+            holder % 4,
+            upper,
+            step_half,
+            jnp.where(step_half == 0, three, 6 - three),
+            (jnp.arange(4, dtype=jnp.int32)[None, :] == low_block).astype(jnp.int32),
+            low_block,
+            KEY_BLOCKS - 1 - low_block,
+            low_limit,
+            KEYS - SPAN - low_limit,
+            maps,
+            2 * N_CTX - 1 - maps,
+        ],
+        axis=1,
+    )
     half_dim = HD // 2
     frequencies = ROPE_BASE ** (-(jnp.arange(half_dim, dtype=F32) * 2.0 / HD))
     angles = positions.astype(F32)[:, None] * frequencies[None, :]
@@ -949,15 +1034,13 @@
     sine = jnp.concatenate([-sine, sine] * 2, axis=1)
 
     weights = [shard_one, shard_gate, shard_up, shard_down, shard_out]
-    (w_joined, w_gate, w_up, w_back, w_proj, x_pair, dy_pair, gains, joined, normed_one, query, kvg) = front(
-        weights, layer_input[0], cotangent[0], own_gain.reshape(40, 128), cosine, sine, 1
+    (w_joined, w_gate, w_up, w_back, w_proj, x_pair, dy_pair, gains, joined, normed_one, query, keys, attn_f32, attn_low, log_sum) = front(
+        tab, weights, layer_input[0], cotangent[0], own_gain.reshape(40, 128), cosine, sine, 1
     )
     w_joined, w_gate, w_up, w_back, w_proj = (w.reshape(D, -1) for w in (w_joined, w_gate, w_up, w_back, w_proj))
-    kvg = kvg.reshape(HH, N_CTX, 2 * TOK, 2 * HD)
     gain_one, gain_two = gains[:16].reshape(D), gains[16:32].reshape(D)
     stream_in = x_pair.reshape(2 * TOK, D).astype(F32)
     dy = dy_pair.reshape(2 * TOK, D)
-    attn_f32, attn_low, log_sum = attend(tab, query, kvg)
 
     partial_a = lax.dot_general(attn_low, w_proj, NT, preferred_element_type=F32)
     branch_a = partial_a + shift(partial_a, "core")
@@ -995,8 +1078,7 @@
     early = [outer(normed_two, grad_gate), outer(normed_two, grad_up), outer(dy, hidden), outer(grad_branch, attn_low)]
 
     grad_attn = jnp.dot(grad_branch, w_proj, preferred_element_type=F32).astype(BF)
-    dq, dkv = attend_back(tab, query, grad_attn, attn_f32, log_sum, kvg)
-    grad_kv = sum_kv(dkv.reshape(HH, 2, 4, 4, 2 * TOK, 2 * HD), 4)
+    dq, grad_kv, begun = attend_back(tab, query, grad_attn, attn_f32, log_sum, keys, early, 4)
     grad_joined, head_terms = rope_back(joined, dq, grad_kv, gains, cosine, sine)
     partial_one = lax.dot_general(grad_joined, w_joined, NT, preferred_element_type=F32)
     grad_normed_one = own_rows(partial_one) + shift(other_rows(partial_one), "core")
@@ -1019,7 +1101,7 @@
     )
     sums = jnp.pad(sums, (0, 40 * 128 - sums.shape[0])).reshape(40, 128)
     own_gate, own_up, own_down, own_out, own_qkv, sums = sum_weights(
-        early + [outer(normed_one, grad_joined)], sums, SUMS, 5, 62 * 1024 * 1024
+        early + [outer(normed_one, grad_joined)], sums, begun, SUMS, 5, 62 * 1024 * 1024
     )
     sums = sums.reshape(-1)
     grad_mlp = jnp.concatenate([own_gate[0], own_gate[1], own_up[0], own_up[1]], axis=1)

time: 591 us -> 508 us (0.86)
  Pallas kernels: 454 us -> 383 us
  matrix products: 70 us -> 56.3 us
    pallas_call x2 -> x0, Pallas kernels: 81.6 us -> none  [the longest x1 42.8 us: sum_kv(): pl.pallas_call(kv_sum_kernel, out_shape=jax.ShapeDtypeStruct((HH, 2 * TOK...]
    pallas_call x1, Pallas kernels: 50.6 us -> 112 us  [attend_back(): pl.pallas_call(attend_back_kernel, out_shape=[jax.ShapeDtypeStruct((2 * T...]
    pallas_call x1, Pallas kernels: 138 us -> 85.1 us  [sum_weights(): pl.pallas_call(functools.partial(weight_sum_kernel, pieces, n), out_shape...]
    dot_general x1, matrix products: 14.8 us -> 5.14 us  [body(): partial_f = lax.dot_general(hidden, w_back, NT, preferred_element_type=F32)]
    unnamed x94 -> x84, local copies, waits for them, and re-layouts: 12.1 us -> 8.08 us
  transfers between devices with their start and end apart: 4 -> 4, of which waited for: 0 -> 0; matrix products, arithmetic and copies ran while one was open for 10% -> 9% of each run, Pallas kernels for 16% -> 23%
where the time goes in v3:
time: 508 us; the launch traced here: 499 us
  Pallas kernels  383 us (75%)
  matrix products  56.3 us (11%)
  local copies, waits for them, and re-layouts  28.4 us (6%)
  other arithmetic  23 us (5%)
  starting transfers between devices  6.65 us (1%)
    pallas_call x1, Pallas kernels, front(): pl.pallas_call(front_kernel, out_shape=full + [jax.ShapeDtypeStruct((2,)...  183 us
    pallas_call x1, Pallas kernels, attend_back(): pl.pallas_call(attend_back_kernel, out_shape=[jax.ShapeDtypeStruct((2 * T...  112 us
    pallas_call x1, Pallas kernels, sum_weights(): pl.pallas_call(functools.partial(weight_sum_kernel, pieces, n), out_shape...  85.1 us
    dot_general x5, matrix products, outer(): lax.dot_general(left, right, TN, preferred_element_type=F32).astype(BF)  21.4 us
  transfers between devices with their start and end apart: 4, of which 0 were waited for; matrix products, arithmetic and copies ran while one was open for 9% of the time, Pallas kernels for 23%

profile of v3, /device:TPU:1, one launch (start us, length us, event | category | flops | bytes accessed | tf_op | source)
XLA Modules:
  0.0 498.7 jit_solution(7761237002107024534)
XLA Ops:
  6.8 1.6 bitcast_bitcast_fusion
  13.3 183.4 %front.1 = (bf16[2,4,4,2,32,1152]{5,4,3,2,1,0:T(8,128)(2,1)}, bf16[2,4,4,2,32,2176]{5,4,3,2,1,0:T(8,128)(2,1)}, bf16[2,4,4,2,32,2176]{5,4,3,2,1,0:T(8,128)(2,1)}...) custom-call(s32[2,334]{1,0:T(2,128)S(1)} %concatenate.41.tab.refs_0_, ...), custom_call_target="tpu_custom_call" | custom-call | tf_op jit(solution)/shard_map/front/pallas_call | solution.py:358
  196.8 4.6 fusion.21
  201.4 1.6 collective-permute-start
  203.9 6.3 %fusion.24 = f32[256,2176]{1,0:T(8,128)S(1)} fusion(bf16[256,2048]{1,0:T(8,128)(2,1)S(1)} %bitcast.120, bf16[2048,2176]{1,0:T(8,128)(2,1)} %bitcast.145), kind=kOutput, calls=%fused_computation.133 | convolution fusion | flops 2281701376 | bytes 12189696 | tf_op jit(solution)/shard_map/dot_general | solution.py:1056
  210.3 4.0 multiply_reduce_fusion.1
  214.6 2.6 fusion.22
  217.2 1.3 slice-done.4
  218.5 3.5 multiply_convert_fusion
  222.0 5.1 %fusion.25 = f32[256,2048]{1,0:T(8,128)S(1)} fusion(bf16[256,2176]{1,0:T(8,128)(2,1)S(1)} %get-tuple-element.117, bf16[2048,2176]{1,0:T(8,128)(2,1)} %bitcast.151), kind=kOutput, calls=%fused_computation.134 | convolution fusion | flops 2281701376 | bytes 12124160 | tf_op jit(solution)/shard_map/dot_general | solution.py:1059
  227.1 5.2 %convolution_add_fusion = f32[256,2048]{1,0:T(8,128)S(1)} fusion(f32[256,2048]{1,0:T(8,128)S(1)} %fusion.25, bf16[256,2176]{1,0:T(8,128)(2,1)S(1)} %get-tuple-element.116, bf16[2048,2176]{1,0:T(8,128)(2,1)} %bitcast.147), kind=kOutput, calls=%fused_computation.5 | convolution fusion | flops 2282225664 | bytes 14221312 | tf_op jit(solution)/shard_map/dot_general | solution.py:1060
  232.4 5.1 %fusion.23 = f32[256,2048]{1,0:T(8,128)S(1)} fusion(bf16[256,2176]{1,0:T(8,128)(2,1)S(1)} %get-tuple-element.118, bf16[2048,2176]{1,0:T(8,128)(2,1)} %bitcast.146), kind=kOutput, calls=%fused_computation.132 | convolution fusion | flops 2281701376 | bytes 12124160 | tf_op jit(solution)/shard_map/dot_general | solution.py:1055
  237.5 1.2 constant_dynamic-slice_fusion.1
  239.4 4.9 convolution_convert_fusion.1
  244.3 5.0 convolution_convert_fusion.2
  249.3 5.0 convolution_convert_fusion
  256.2 1.4 copy-done.27
  258.9 2.7 convolution_convert_fusion.4
  261.6 111.8 %attend_back.1 = (f32[256,768]{1,0:T(8,128)S(1)}, f32[3,256,128]{2,1,0:T(8,128)S(1)}, bf16[2,2,4,2,16,1152]{5,4,3,2,1,0:T(8,128)(2,1)}, bf16[2,2,4,2,16,1152]{5,...) custom-call(s32[2,334]{1,0:T(2,128)S(1)} %concatenate.41.tab.refs_0_, ...), custom_call_target="tpu_custom_call" | custom-call | tf_op jit(solution)/shard_map/attend_back/pallas_call | solution.py:917
  373.5 2.3 rope_back.1
  375.8 1.5 fusion.26
  379.1 4.3 collective-permute-start.3
  384.1 1.4 multiply_reduce_fusion.4
  386.1 3.0 multiply_reduce_fusion.2
  390.3 3.8 convolution_convert_fusion.3
  394.2 2.5 fusion.8
  396.6 2.7 concatenate.47
  399.9 85.1 %sum_weights.1 = (f32[2,16,2176]{2,1,0:T(8,128)}, f32[2,16,2176]{2,1,0:T(8,128)}, f32[2,16,2176]{2,1,0:T(8,128)}, f32[2,16,768]{2,1,0:T(8,128)}, f32[2,16,1152]{2,1,0:T(8,128)}, /*index=5*/f32[40,128]{1,0:T(8,128)}) custom-call(bf16[2,4,4,2,32,2176]{5,4,3,2,1,0:T(8,128)(2,1)} %bitcast.130, bf16[2,4,4,2,32,2176]{5,4,3,2,1,0:T(8,128)(2,1)} %bitcast.128, ...), custom_call_target="tpu_custom_call" | custom-call | tf_op jit(solution)/shard_map/sum_weights/pallas_call | solution.py:680
  485.0 1.4 dynamic_slice.44
  486.5 1.2 slice_multiply_fusion
  490.9 1.1 slice_bitcast_fusion.5
  495.4 1.3 fusion.12
  (156 shorter events, 29.1 us)
Async XLA Ops:
  0.6 8.4 %copy-start.33 = (bf16[33]{0:T(256)(128)(2,1)S(1)}, bf16[33]{0:T(256)(128)(2,1)}, u32[]{:S(2)}) copy-start(bf16[33]{0:T(256)(128)(2,1)} %param.13) | copy-start | bytes 202
  0.6 9.1 %copy-start = (bf16[1,128,2048]{2,1,0:T(8,128)(2,1)S(1)}, bf16[1,128,2048]{2,1,0:T(8,128)(2,1)}, u32[]{:S(2)}) copy-start(bf16[1,128,2048]{2,1,0:T(8,128)(2,1)} %param.8) | copy-start | bytes 1572868
  196.7 4.7 copy-start.3
  196.7 4.7 copy-start.8
  196.7 4.7 copy-start.18
  196.8 4.7 copy-start.20
  201.4 8.8 %collective-permute-start = (f32[256,2048]{1,0:T(8,128)}, f32[256,2048]{1,0:T(8,128)}, u32[]{:S(2)}, u32[]{:S(2)}) collective-permute-start(f32[256,2048]{1,0:T(8,128)} %fusion.21), channel_id=1, source_target_pairs={{0,1},{1,0},{2,3},{3,2},{4,5},{5,4},{6,7},{7,6},{8,9},{9,8},{10,11... | collective-permute-start | bytes 6291464 | tf_op jit(solution)/shard_map/ppermute | solution.py:968
  203.9 10.6 %slice-start = ((s8[8912896]{0:T(1024)(128)(4,1)}), s8[4194304]{0:T(1024)(128)(4,1)S(1)}, s32[]{:S(2)}) async-start(s8[8912896]{0:T(1024)(128)(4,1)} %bitcast.148), calls=%async_computation | async-start | bytes 8388608
  203.9 10.6 %slice-start.1 = ((s8[8912896]{0:T(1024)(128)(4,1)}), s8[4194304]{0:T(1024)(128)(4,1)S(1)}, s32[]{:S(2)}) async-start(s8[8912896]{0:T(1024)(128)(4,1)} %bitcast.148), calls=%async_computation.1 | async-start | bytes 8388608
  210.2 4.3 slice-start.2
  214.3 40.7 %copy-start.22 = (f32[256,2048]{1,0:T(8,128)}, f32[256,2048]{1,0:T(8,128)S(1)}, u32[]{:S(2)}) copy-start(f32[256,2048]{1,0:T(8,128)S(1)} %get-tuple-element.106) | copy-start | bytes 6291460
  214.6 3.9 slice-start.4
  214.6 3.9 slice-start.5
  232.3 22.0 %collective-permute-start.2 = (f32[256,2048]{1,0:T(8,128)S(1)}, f32[256,2048]{1,0:T(8,128)S(1)}, u32[]{:S(2)}, u32[]{:S(2)}) collective-permute-start(f32[256,2048]{1,0:T(8,128)S(1)} %convolution_add_fusion), channel_id=1, source_target_pairs={{0,1},{1,0},{2,3},{3,2},{4,5},{5,4},{6,7},{7,6},{8,9},{9,8},{10,11... | collective-permute-start | bytes 6291464 | tf_op jit(solution)/shard_map/ppermute | solution.py:968
  237.5 6.8 %copy-start.32 = (f32[256,2048]{1,0:T(8,128)}, f32[256,2048]{1,0:T(8,128)S(1)}, u32[]{:S(2)}) copy-start(f32[256,2048]{1,0:T(8,128)S(1)} %fusion.23) | copy-start | bytes 6291460
  238.8 147.3 %collective-permute-start.1 = (f32[128,2048]{1,0:T(8,128)}, f32[128,2048]{1,0:T(8,128)}, u32[]{:S(2)}, u32[]{:S(2)}) collective-permute-start(f32[128,2048]{1,0:T(8,128)} %constant_dynamic-slice_fusion.1), channel_id=1, source_target_pairs={{0,1},{1,0},{2,3},{3,2},{4,5},{5,4},{6,7},{7,6},{8,9},{9,8},{10,11... | collective-permute-start | bytes 3145736 | tf_op jit(solution)/shard_map/ppermute | solution.py:968
  261.6 114.2 %slice-start.6 = ((s8[4718592]{0:T(1024)(128)(4,1)}), s8[4194304]{0:T(1024)(128)(4,1)S(1)}, s32[]{:S(2)}) async-start(s8[4718592]{0:T(1024)(128)(4,1)} %bitcast.155), calls=%async_computation.6 | async-start | bytes 8388608
  261.6 111.9 %copy-start.1 = (f32[256,1152]{1,0:T(8,128)S(1)}, f32[256,1152]{1,0:T(8,128)}, u32[]{:S(2)}) copy-start(f32[256,1152]{1,0:T(8,128)} %get-tuple-element.59.joined) | copy-start | bytes 3538948
  261.6 111.9 %copy-start.19 = (f32[40,128]{1,0:T(8,128)S(1)}, f32[40,128]{1,0:T(8,128)}, u32[]{:S(2)}) copy-start(f32[40,128]{1,0:T(8,128)} %copy-done.18) | copy-start | bytes 61444
  261.6 114.2 %slice-start.7 = ((s8[4718592]{0:T(1024)(128)(4,1)}), s8[524288]{0:T(1024)(128)(4,1)S(1)}, s32[]{:S(2)}) async-start(s8[4718592]{0:T(1024)(128)(4,1)} %bitcast.155), calls=%async_computation.7 | async-start | bytes 1048576
  373.4 4.0 copy-start.2
  373.4 4.0 copy-start.10
  373.4 4.0 copy-start.11
  373.4 4.0 copy-start.12
  373.4 4.0 copy-start.13
  373.4 4.0 copy-start.14
  373.5 4.0 copy-start.15
  377.4 8.7 %copy-start.23 = (f32[256,2048]{1,0:T(8,128)S(1)}, f32[256,2048]{1,0:T(8,128)}, u32[]{:S(2)}) copy-start(f32[256,2048]{1,0:T(8,128)} %copy-done.22) | copy-start | bytes 6291460
  379.1 15.1 %collective-permute-start.3 = (f32[128,2048]{1,0:T(8,128)}, f32[128,2048]{1,0:T(8,128)}, u32[]{:S(2)}, u32[]{:S(2)}) collective-permute-start(f32[128,2048]{1,0:T(8,128)} %constant_dynamic-slice_fusion), channel_id=1, source_target_pairs={{0,1},{1,0},{2,3},{3,2},{4,5},{5,4},{6,7},{7,6},{8,9},{9,8},{10,11... | collective-permute-start | bytes 3145736 | tf_op jit(solution)/shard_map/ppermute | solution.py:968
  386.1 4.3 copy-start.29
  485.0 10.3 %copy-start.25 = (f32[256,2048]{1,0:T(8,128)S(1)}, f32[256,2048]{1,0:T(8,128)}, u32[]{:S(2)}) copy-start(f32[256,2048]{1,0:T(8,128)} %copy-done.24) | copy-start | bytes 6291460
  490.9 4.5 copy-start.28
  (14 other events, 26.0 us)

commit v4 on v3

--- a/solution.py
+++ b/solution.py
@@ -42,7 +42,7 @@
 KV_DIMS = ("h", "x", "y")
 ORDERS = (("x", "y", "z"), ("y", "z", "x"), ("z", "x", "y"))
 KV_ORDERS = (("h", "x", "y"), ("x", "y", "h"), ("y", "h", "x"))
-KV_SUM_ORDERS = (("y", "x", "h"), ("h", "y", "x"), ("x", "h", "y"))
+KV_PARTS = ((0, 96, ("y", "x", "h")), (96, 96, ("x", "y", "h")), (192, 64, ("h", "x", "y")))
 SUMS = (
     (0, 0, 1152, ORDERS[0]),
     (1, 0, 1152, ORDERS[1]),
@@ -203,7 +203,7 @@
 
 
 def front_kernel(
-    tab, shard_one, shard_gate, shard_up, shard_down, shard_out, x, dy, gains, cosine, sine,
+    tab, shard_one, gate_up, down, out, x, dy, gains, cosine, sine,
     w_one, w_gate, w_up, w_down, w_out, x_pair, dy_pair, gain_all, joined, normed, query, kv_out, o_ref, low_ref, l_ref,
     one, kv_src, kvg, kvs, q_ref, acc, sum_ref, small_buf, psem, lsem, tssem, trsem, ossem, orsem, gssem, grsem, kssem, krsem, ksem,
 ):
@@ -214,11 +214,21 @@
     own = {d: at[d] for d in W_DIMS}
     total = Total(gains[...], at, small_buf, tssem, trsem)
     remote, local = [], []
-    pairs = [(shard_one, one), (shard_gate, w_gate), (shard_up, w_up), (shard_down, w_down), (shard_out, w_out)]
+
+    def half_of(src, start, width, which):
+        return src.at[:, pl.ds(pl.multiple_of(start + which * width, 128), width)]
+
+    pairs = [
+        (lambda c: shard_one.at[c], one),
+        (lambda c: half_of(gate_up, 0, FH, c), w_gate),
+        (lambda c: half_of(gate_up, FF, FH, c), w_up),
+        (lambda c: half_of(down, 0, FH, c), w_down),
+        (lambda c: half_of(out, 0, QW, c), w_out),
+    ]
     for i, (src, ref) in enumerate(pairs):
         dst = pick(ref, W_DIMS, own, (pl.ds(core * 16, 16), slice(None)))
-        remote.append(send(src.at[1 - core], dst, psem.at[i, 0], psem.at[i, 1], sibling))
-        local.append(pltpu.make_async_copy(src.at[core], dst, lsem.at[i]))
+        remote.append(send(src(1 - core), dst, psem.at[i, 0], psem.at[i, 1], sibling))
+        local.append(pltpu.make_async_copy(src(core), dst, lsem.at[i]))
         local[-1].start()
     for i, (src, ref) in ((5, (x, x_pair)), (6, (dy, dy_pair))):
         remote.append(send(src, ref.at[core], psem.at[i, 0], psem.at[i, 1], sibling))
@@ -308,14 +318,14 @@
     every(rest, "pass_on")
     product(0, 384)
     every(keys, "pass_on")
-    every(rest, "finish")
+    every(rest[:3], "finish", "start")
     every(keys, "finish", "start")
     product(384, 384)
     every(keys, "pass_on")
     for t in range(QW // 128):
         query[:, t * 128 : (t + 1) * 128] = rope(t, False)
     every(keys, "finish", "start")
-    every(rest[:3], "start")
+    every(rest[3:], "finish")
     blank = jnp.zeros((QROWS, HD), BF)
     for s in range(2):
         for h in range(HH):
@@ -353,7 +363,7 @@
 def front(tab, shards, x, dy, gains, cosine, sine, cid):
     anywhere = pl.BlockSpec(memory_space=pl.ANY)
     vmem = pl.BlockSpec(memory_space=pltpu.VMEM)
-    full = [jax.ShapeDtypeStruct((2, 4, 4, 2, 32, s.shape[-1]), BF) for s in shards]
+    full = [jax.ShapeDtypeStruct((2, 4, 4, 2, 32, w), BF) for w in (QW + KVW, FH, FH, FH, QW)]
     n = len(GATHER)
     return pl.pallas_call(
         front_kernel,
@@ -370,7 +380,7 @@
             jax.ShapeDtypeStruct((2 * TOK, QW), BF),
             jax.ShapeDtypeStruct((2, HH, 2, 1, QROWS), F32),
         ],
-        in_specs=[pl.BlockSpec(memory_space=pltpu.SMEM)] + [anywhere] * 7 + [vmem] * 3,
+        in_specs=[pl.BlockSpec(memory_space=pltpu.SMEM)] + [anywhere] * 6 + [vmem] * 3,
         out_specs=[anywhere] * 5 + [vmem, anywhere] + [vmem] * 4 + [anywhere] + [vmem] * 3,
         scratch_shapes=[
             pltpu.VMEM((2, 4, 4, 2, 32, QW + KVW), BF),
@@ -400,41 +410,6 @@
     )(tab, *shards, x, dy, gains, cosine, sine)
 
 
-def rope_back_kernel(joined, dq, dkv, gains, cosine, sine, out, terms):
-    head_gains = gains[32:33]
-
-    def tile(t, is_key, grad):
-        v = joined[:, t * 128 : (t + 1) * 128]
-        low = lane_of(v.shape) < HD
-        back = grad * cosine[...] - swap_halves(grad) * sine[...]
-        inverse = lax.rsqrt(head_sums(v * v) * (1.0 / HD) + EPSILON)
-        scaled = back * tile_gain(head_gains, is_key)
-        inner = head_sums(scaled * v) * (1.0 / HD)
-        result = inverse * scaled - v * (inverse * inverse * inverse) * inner
-        if is_key:
-            result = jnp.where(low, result, grad)
-        out[:, t * 128 : (t + 1) * 128] = result.astype(BF)
-        return jnp.sum(back * v * inverse, axis=0, keepdims=True)
-
-    q_terms = sum(tile(t, False, dq[:, t * 128 : (t + 1) * 128]) for t in range(QW // 128))
-    k_terms = sum(tile(QW // 128 + h, True, dkv[h]) for h in range(HH))
-    low = lane_of(q_terms.shape) < HD
-    q_terms = q_terms + pltpu.roll(q_terms, HD, 1)
-    terms[...] = jnp.where(low, q_terms, pltpu.roll(k_terms, HD, 1))
-
-
-def rope_back(joined, dq, dkv, gains, cosine, sine):
-    vmem = pl.BlockSpec(memory_space=pltpu.VMEM)
-    return pl.pallas_call(
-        rope_back_kernel,
-        out_shape=[jax.ShapeDtypeStruct((2 * TOK, QW + KVW), BF), jax.ShapeDtypeStruct((1, 128), F32)],
-        in_specs=[vmem] * 6,
-        out_specs=[vmem] * 2,
-        compiler_params=pltpu.CompilerParams(vmem_limit_bytes=32 * 1024 * 1024),
-        name="rope_back",
-    )(joined, dq, dkv, gains, cosine, sine)
-
-
 def lead_shape(dims):
     full = {"h": 2, "x": 4, "y": 4, "l": 2}
     return tuple(full[d] for d in dims)
@@ -446,13 +421,15 @@
 
 
 class Summing:
-    def __init__(self, source, dims, at, order, rows, cols, buffers, ssem, rsem, lsem, begun=None):
+    def __init__(self, source, dims, at, order, rows, cols, buffers, ssem, rsem, lsem, begun=None, base=None):
         self.ref, self.dims, self.at, self.order, self.begun = source, dims, at, order, begun
         self.cols, self.buffers, self.rows = cols, buffers, rows
         self.ssem, self.rsem, self.lsem = ssem, rsem, lsem
-        self.phase, self.sent = 0, []
-
-    def part(self, coordinate, rows):
+        self.phase, self.sent, self.base = 0, [], base
+        self.resident = base is not None
+
+    def part(self, coordinate, start, length):
+        rows = pl.ds(start + (self.base or 0), length)
         return pick(self.ref, self.dims, labels(self.axis, coordinate), (rows, self.cols))
 
     def send(self, n, src, dst, by):
@@ -465,12 +442,12 @@
         self.rest = without(self.dims, self.axis)
         self.lead = lead_shape(self.rest)
         half = self.rows // 2
-        first, second, every = pl.ds(0, half), pl.ds(half, half), pl.ds(0, self.rows)
+        first, second, every = (0, half), (half, half), (0, self.rows)
         i = self.at[self.axis]
         buf = self.buffers[self.phase]
         self.local = []
         if SIZES[self.axis] == 2:
-            self.direct = (self.send(0, self.part(1 - i, every), buf["got"].at[0], 1),)
+            self.direct = (self.send(0, self.part(1 - i, *every), buf["got"].at[0], 1),)
         else:
             up, down, far = lax.rem(i + 1, 4), lax.rem(i + 3, 4), lax.rem(i + 2, 4)
             self.near = (up, down)
@@ -478,22 +455,22 @@
             self.relay, self.direct = (), ()
         elif SIZES[self.axis] == 4:
             self.relay = (
-                self.send(0, self.part(far, first), buf["relay"].at[0], 1),
-                self.send(1, self.part(far, second), buf["relay"].at[1], 3),
+                self.send(0, self.part(far, *first), buf["relay"].at[0], 1),
+                self.send(1, self.part(far, *second), buf["relay"].at[1], 3),
             )
             self.direct = (
-                self.send(2, self.part(up, second), buf["got"].at[1, 1], 1),
-                self.send(3, self.part(down, first), buf["got"].at[0, 1], 3),
+                self.send(2, self.part(up, *second), buf["got"].at[1, 1], 1),
+                self.send(3, self.part(down, *first), buf["got"].at[0, 1], 3),
             )
-        if self.phase == 0:
-            todo = [(self.part(i, every), buf["mine"])]
-            if SIZES[self.axis] == 4:
-                todo.append((self.part(up, first), buf["own"].at[0]))
-                todo.append((self.part(down, second), buf["own"].at[1]))
+        if self.phase == 0 and not self.resident:
+            todo = [(self.part(i, *every), buf["mine"])]
             if self.begun is not None:
-                todo.append((self.begun[0], buf["relay"]))
-                todo.append((self.begun[1].at[0], buf["got"].at[0, 1]))
-                todo.append((self.begun[1].at[1], buf["got"].at[1, 1]))
+                passed, direct = self.begun[1], self.begun[0]
+                todo += [(passed.at[n], buf["got"].at[n, 0]) for n in range(2)]
+                todo += [(direct.at[n], buf["got"].at[n, 1]) for n in range(2)]
+            elif SIZES[self.axis] == 4:
+                todo.append((self.part(up, *first), buf["own"].at[0]))
+                todo.append((self.part(down, *second), buf["own"].at[1]))
             for n, (src, dst) in enumerate(todo):
                 c = pltpu.make_async_copy(src, dst, self.lsem.at[n])
                 c.start()
@@ -516,20 +493,17 @@
         lax.fori_loop(0, self.lead[0], go, 0)
 
     def pass_on(self):
-        if SIZES[self.axis] == 2:
+        if SIZES[self.axis] == 2 or (self.phase == 0 and self.begun is not None):
             return
         buf = self.buffers[self.phase]
         half = self.rows // 2
         for n, by in ((0, 1), (1, 3)):
-            if self.relay:
-                self.relay[n].wait_recv()
-            elif n == 0:
-                self.local[3].wait()
-            if self.phase == 0:
+            self.relay[n].wait_recv()
+            if self.phase == 0 and not self.resident:
                 self.local[1 + n].wait()
                 own = buf["own"].at[n]
             else:
-                own = self.part(self.near[n], pl.ds(n * half, half))
+                own = self.part(self.near[n], n * half, half)
 
             def add(spot):
                 here_ = spot + (slice(None), slice(None))
@@ -545,12 +519,14 @@
         half = self.rows // 2
         if self.local:
             self.local[0].wait()
-        for c in self.local[4:]:
-            c.wait()
+        if self.begun is not None:
+            for c in self.local[1:]:
+                c.wait()
         for c in self.direct:
             c.wait_recv()
-        own = buf["mine"] if self.phase == 0 else self.part(self.at[self.axis], pl.ds(0, self.rows))
-        out = buf["mine"] if self.phase == 0 else buf["sum"]
+        copied = self.phase == 0 and not self.resident
+        own = buf["mine"] if copied else self.part(self.at[self.axis], 0, self.rows)
+        out = buf["mine"] if copied else buf["sum"]
 
         def add(spot):
             if SIZES[self.axis] == 2:
@@ -567,6 +543,7 @@
         self.over_lead(add)
         self.ref, self.dims, self.cols = out, self.rest, slice(None)
         self.phase += 1
+        self.base = 0
 
 
 class Total:
@@ -600,26 +577,24 @@
             self.start()
 
 
-def run_sums(streams, total=None):
+def run_sums(streams, total):
+    todo = []
     for s in streams:
         s.start()
-    for phase in range(3):
-        for s in streams:
-            s.pass_on()
-        if total is not None:
-            total.step()
-        for s in streams:
-            s.finish()
-            if phase < 2:
-                s.start()
-        if total is not None:
-            total.step()
+        steps = [("pass_on",), ("finish", "start"), ("pass_on",), ("finish", "start"), ("pass_on",), ("finish",)]
+        todo.append(steps[1:] if s.begun is not None else steps)
+    while any(todo):
+        for s, steps in zip(streams, todo):
+            if steps:
+                for name in steps.pop(0):
+                    getattr(s, name)()
+        total.step()
     for s in streams:
         for c in s.sent:
             c.wait_send()
 
 
-def sum_scratch(order, dims, rows, width):
+def sum_scratch(order, dims, rows, width, begun=False, resident=False):
     buffers = []
     for phase, axis in enumerate(order):
         rest = without(dims, axis)
@@ -629,10 +604,11 @@
             buf["got"] = pltpu.VMEM((1,) + lead + (rows, width), BF)
         else:
             buf["got"] = pltpu.VMEM((2, 2) + lead + (rows // 2, width), BF)
-            buf["relay"] = pltpu.VMEM((2,) + lead + (rows // 2, width), BF)
-        if phase == 0:
+            if phase or not begun:
+                buf["relay"] = pltpu.VMEM((2,) + lead + (rows // 2, width), BF)
+        if phase == 0 and not resident:
             buf["mine"] = pltpu.VMEM(lead + (rows, width), BF)
-            if SIZES[axis] == 4:
+            if SIZES[axis] == 4 and not begun:
                 buf["own"] = pltpu.VMEM((2,) + lead + (rows // 2, width), BF)
         else:
             buf["sum"] = pltpu.VMEM(lead + (rows, width), BF if phase < 2 else F32)
@@ -643,8 +619,8 @@
 
 def weight_sum_kernel(pieces, n, *refs):
     ins, small, begun, refs = refs[:n], refs[n], refs[n + 1 : n + 1 + 2 * N_EARLY], refs[n + 1 + 2 * N_EARLY :]
-    outs, small_out = refs[:n], refs[n]
-    buffers, stages, swapped, small_buf, ssem, rsem, lsem, csem, tssem, trsem = refs[n + 1 :]
+    outs, small_out = refs[: n - 1], refs[n - 1]
+    buffers, stages, swapped, small_buf, ssem, rsem, lsem, csem, tssem, trsem = refs[n:]
     at = here()
     core = at["core"]
     sibling = moved(at, "core", 1)
@@ -664,39 +640,47 @@
     other = pl.ds(pl.multiple_of((1 - core) * 16, 16), 16)
     own = pl.ds(pl.multiple_of(core * 16, 16), 16)
     copies = [send(stages[a].at[other], swapped[a], csem.at[a, 0], csem.at[a, 1], sibling) for a in range(n)]
+
+    def put(a, half, value):
+        width = value.shape[1]
+        ref, start = ((outs[0], 0), (outs[0], FF), (outs[1], 0), (outs[2], 0), (outs[3], 0))[a]
+        ref[:, pl.ds(pl.multiple_of(start + half * width, 128), width)] = value
+
     for a in range(n):
-        outs[a][core] = stages[a][own, :]
+        put(a, core, stages[a][own, :])
+    for a in range(n):
         copies[a].wait_recv()
-        outs[a][1 - core] = swapped[a][...]
+        put(a, 1 - core, swapped[a][...])
     for c in copies + total.sent:
         c.wait_send()
 
 
 def sum_weights(grads, small, begun, pieces, cid, limit):
-    n, k = len(grads), len(pieces)
+    n, count = len(grads), len(pieces)
     anywhere = pl.BlockSpec(memory_space=pl.ANY)
     vmem = pl.BlockSpec(memory_space=pltpu.VMEM)
     widths = [g.shape[-1] for g in grads]
     return pl.pallas_call(
         functools.partial(weight_sum_kernel, pieces, n),
-        out_shape=[jax.ShapeDtypeStruct((2, 16, w), F32) for w in widths] + [jax.ShapeDtypeStruct(small.shape, F32)],
+        out_shape=[jax.ShapeDtypeStruct((16, w), F32) for w in (2 * FF, FF, HQ * HD, 2 * (QW + KVW))]
+        + [jax.ShapeDtypeStruct(small.shape, F32)],
         in_specs=[anywhere] * n + [vmem] + [anywhere] * len(begun),
-        out_specs=[vmem] * (n + 1),
+        out_specs=[vmem] * n,
         scratch_shapes=[
-            [sum_scratch(order, W_DIMS, 32, width) for a, start, width, order in pieces],
+            [sum_scratch(order, W_DIMS, 32, width, k < N_EARLY) for k, (a, start, width, order) in enumerate(pieces)],
             [pltpu.VMEM((32, w), F32) for w in widths],
             [pltpu.VMEM((16, w), F32) for w in widths],
             pltpu.VMEM((4, 4) + small.shape, F32),
-            pltpu.SemaphoreType.DMA((k, 3, 6)),
-            pltpu.SemaphoreType.DMA((k, 3, 6)),
-            pltpu.SemaphoreType.DMA((k, 6)),
+            pltpu.SemaphoreType.DMA((count, 3, 6)),
+            pltpu.SemaphoreType.DMA((count, 3, 6)),
+            pltpu.SemaphoreType.DMA((count, 6)),
             pltpu.SemaphoreType.DMA((n, 2)),
             pltpu.SemaphoreType.DMA((4, 4)),
             pltpu.SemaphoreType.DMA((4, 4)),
         ],
         compiler_params=pltpu.CompilerParams(collective_id=cid, has_side_effects=True, vmem_limit_bytes=limit),
         name="sum_weights",
-    )(*[g.reshape(2, 4, 4, 2, 32, g.shape[-1]) for g in grads], small, *begun)
+    )(*grads, small, *begun)
 
 
 def sum_peers(at, axes):
@@ -774,21 +758,56 @@
 
 
 class Early:
-    def __init__(self, source, at, order, cols, relay, direct, ssem, rsem):
-        axis = order[0]
-        i = at[axis]
-        up, down, far = lax.rem(i + 1, 4), lax.rem(i + 3, 4), lax.rem(i + 2, 4)
+    def __init__(self, source, at, order, cols, width, relay, direct, passed, ssem, rsem):
+        self.source, self.at, self.axis, self.cols, self.width = source, at, order[0], cols, width
+        self.relay, self.passed, self.ssem, self.rsem, self.views = relay, passed, ssem, rsem, {}
+        i = at[self.axis]
+        self.near = (lax.rem(i + 1, 4), lax.rem(i + 3, 4))
+        far = lax.rem(i + 2, 4)
+        plan = (
+            (far, 0, relay, 0, 1),
+            (far, 1, relay, 1, 3),
+            (self.near[0], 1, direct, 1, 1),
+            (self.near[1], 0, direct, 0, 3),
+        )
         self.copies = []
-        plan = ((far, 0, relay, 0, 1), (far, 1, relay, 1, 3), (up, 1, direct, 1, 1), (down, 0, direct, 0, 3))
         for n, (coordinate, half, dst, slot, by) in enumerate(plan):
-            src = pick(source, W_DIMS, labels(axis, coordinate), (pl.ds(half * 16, 16), cols))
-            self.copies.append(send(src, dst.at[slot], ssem.at[n], rsem.at[n], moved(at, axis, by)))
+            self.copies.append(self.send(n, self.part(coordinate, half), dst.at[slot], by))
+
+    def part(self, coordinate, half):
+        return pick(self.source, W_DIMS, labels(self.axis, coordinate), (pl.ds(half * 16, 16), self.cols))
+
+    def send(self, n, src, dst, by):
+        return send(src, dst, self.ssem.at[n], self.rsem.at[n], moved(self.at, self.axis, by))
+
+    def load(self, n, own, sem):
+        lead = lead_shape(without(W_DIMS, self.axis))
+        view = own.at[(slice(None),) * (len(lead) + 1) + (pl.ds(0, self.width),)]
+        self.views[n] = view
+        copy = pltpu.make_async_copy(self.part(self.near[n], n), view, sem)
+        copy.start()
+        return copy
+
+    def add(self, n):
+        self.copies[n].wait_recv()
+        came, own = self.relay.at[n], self.views[n]
+        lead = lead_shape(without(W_DIMS, self.axis))
+        spots = [()]
+        for size in lead[1:]:
+            spots = [s + (j,) for s in spots for j in range(size)]
+
+        def go(j, carry):
+            for s in spots:
+                at = (j,) + s + (slice(None), slice(None))
+                came[at] = (came[at].astype(F32) + own[at].astype(F32)).astype(BF)
+            return carry
+
+        lax.fori_loop(0, lead[0], go, 0)
+        self.copies.append(self.send(4 + n, came, self.passed.at[n], 1 if n == 0 else 3))
 
     def wait(self):
-        for c in self.copies:
+        for c in self.copies[2:]:
             c.wait_recv()
-        for c in self.copies:
-            c.wait_send()
 
 
 def early_shapes():
@@ -800,22 +819,78 @@
 
 
 def attend_back_kernel(*refs):
-    tab, qr, da, attn, l_ref, kv_sorted = refs[:6]
-    grads, refs = refs[6:10], refs[10:]
-    dq_ref, dkv_out = refs[:2]
-    begun, refs = refs[2 : 2 + 2 * N_EARLY], refs[2 + 2 * N_EARLY :]
-    kvs, qd_ref, delta_ref, stage, acc, dq_acc, buffers, essem, ersem, ssem, rsem, lsem, sems = refs
+    tab, qr, da, attn, attn_low, l_ref, kv_sorted, normed, dy, low_mid, hid, dgate, dup = refs[:13]
+    joined, normed_one, w_one, gains, cosine, sine, grad_mid, own_x = refs[13:21]
+    input_grad, terms, head_terms = refs[21:24]
+    grads, refs = refs[24:29], refs[29:]
+    begun, refs = refs[: 2 * N_EARLY], refs[2 * N_EARLY :]
+    held, qd_ref, delta_ref, stage, acc, dq_acc, dq_ref, buffers, refs = refs[:8] + (refs[8:],)
+    tiles, mix, mix_z, relays, w_ref, d_joined, part, got = refs[:8]
+    essem, ersem, ssem, rsem, sems, tsem, msem, psem = refs[8:]
     at = here()
-    greet(neighbours(at, ("x", "y", "z", "h")))
-    early = [
-        Early(grads[a], at, order, pl.ds(start, width), begun[2 * k], begun[2 * k + 1], essem.at[k], ersem.at[k])
-        for k, (a, start, width, order) in enumerate(SUMS[:N_EARLY])
-    ]
-    loads = []
-    for h in range(HH):
-        for s in range(2):
-            loads.append(pltpu.make_async_copy(kv_sorted.at[s, h], kvs.at[s, h], sems.at[s, h]))
-            loads[-1].start()
+    core = at["core"]
+    sibling = moved(at, "core", 1)
+    def load_keys(h):
+        return [pltpu.make_async_copy(kv_sorted.at[s, h], held[h % 2].at[s], sems.at[s, h]) for s in range(2)]
+
+    for c in load_keys(0):
+        c.start()
+
+    def load_w(c):
+        return pltpu.make_async_copy(w_one.at[c], w_ref, psem.at[0])
+
+    load_w(0).start()
+    greet([sibling] + neighbours(at, ("x", "y", "z", "h")))
+    sides = ((normed, dgate), (normed, dup), (dy, hid), (low_mid, attn_low), (normed_one, d_joined))
+
+    def tile_copy(n, i, slot, parity):
+        a, start, width = n
+        half = lax.rem(i, 2)
+        return pltpu.make_async_copy(
+            tiles.at[parity, slot, :, :, :, :, pl.ds(0, width)],
+            grads[a].at[lax.div(i, 2), pl.ds(half * 2, 2), :, :, :, pl.ds(start, width)],
+            tsem.at[parity, slot],
+        )
+
+    def outer(n, parity):
+        a, start, width = n
+        left, right = sides[a]
+
+        def go(i, carry):
+            slot = lax.rem(i, 2)
+
+            @pl.when(i > 1)
+            def _():
+                tile_copy(n, i, slot, parity).wait()
+
+            rows = pl.ds(pl.multiple_of(i * 512, 512), 512)
+            value = lax.dot_general(left[:, rows], right[:, start : start + width], TN, preferred_element_type=F32)
+            tiles[parity, slot, :, :, :, :, :width] = value.astype(BF).reshape(2, 4, 2, 32, width)
+            tile_copy(n, i, slot, parity).start()
+            return carry
+
+        lax.fori_loop(0, 4, go, 0)
+
+    def drain(n, parity):
+        for slot in range(2):
+            tile_copy(n, slot, slot, parity).wait()
+
+    early = []
+
+    def begin(k):
+        a, start, width, order = SUMS[k]
+        drain((a, start, width), k % 2)
+        early.append(
+            Early(
+                grads[a], at, order, pl.ds(start, width), width, relays[k], begun[2 * k], begun[2 * k + 1],
+                essem.at[k], ersem.at[k],
+            )
+        )
+
+    for k in range(N_EARLY):
+        outer(SUMS[k][:3], k % 2)
+        if k:
+            begin(k - 1)
     rate = LOG2E * HD**-0.5
     factor = jnp.where(lax.broadcasted_iota(jnp.int32, (1, 2 * HD), 1) < HD, HD**-0.5, 1.0)
     blank = jnp.zeros((QROWS, HD), BF)
@@ -827,21 +902,58 @@
                 qd_ref[s, h, half, QROWS:] = jnp.concatenate([blank, up], axis=1)
                 inner = (up.astype(F32) * heads_at(attn, s, h, half)).T
                 delta_ref[s, h, half] = jnp.sum(inner, axis=0, keepdims=True)
-    for c in loads:
-        c.wait()
+    begin(N_EARLY - 1)
     streams = [
-        Summing(stage.at[h], KV_DIMS, at, KV_SUM_ORDERS[h], 2 * TOK, slice(None), buffers[h], ssem.at[h], rsem.at[h], lsem.at[h])
+        [
+            Summing(
+                stage.at[h], KV_DIMS, at, order, rows, slice(None), buffers[h][j],
+                ssem.at[h, j], rsem.at[h, j], None, None, start,
+            )
+            for j, (start, rows, order) in enumerate(KV_PARTS)
+        ]
         for h in range(HH)
     ]
-    todo = [["pass_on", "finish", "start", "pass_on", "finish", "start", "pass_on", "finish"] for h in range(HH)]
+    todo = [[("pass_on",), ("finish", "start"), ("pass_on",), ("finish", "start"), ("pass_on",), ("finish",)] for h in range(HH)]
+
+    def move(h):
+        for name_of in todo[h].pop(0) if todo[h] else ():
+            for st in streams[h]:
+                getattr(st, name_of)()
+
+    units = [(k, n) for k in range(N_EARLY) for n in range(2)]
+    used, flying, ahead = {}, [], [0]
+
+    def fetch():
+        k, n = units[ahead[0]]
+        pool, slots, first = (mix_z, 2, 3) if early[k].axis == "z" else (mix, 3, 0)
+        slot = used.get(slots, 0) % slots
+        used[slots] = used.get(slots, 0) + 1
+        flying.append((k, n, early[k].load(n, pool.at[slot], msem.at[first + slot])))
+        ahead[0] += 1
+
+    def advance(count):
+        for _ in range(count):
+            while ahead[0] < len(units) and len(flying) < 2:
+                fetch()
+            if flying:
+                k, n, copy = flying.pop(0)
+                copy.wait()
+                early[k].add(n)
+
     for h in range(HH):
-
-        def sequence(s, carry):
+        for c in load_keys(h):
+            c.wait()
+        if h + 1 < HH:
+            for c in load_keys(h + 1):
+                c.start()
+        kvs = held[h % 2]
+
+        def sequence(s, carry, h=h, kvs=kvs):
             dq_acc[...] = jnp.zeros_like(dq_acc)
             acc[...] = jnp.zeros_like(acc)
 
             def backward(half, block, limit):
-                keys = kvs[s, h, block].reshape(KEYS, 2 * HD)
+                keys = kvs[s, block].reshape(KEYS, 2 * HD)
                 both = lax.dot_general(keys, qd_ref[s, h, half], NT, preferred_element_type=F32)
                 prob = masked(jnp.exp2(both[:, :QROWS] * rate - l_ref[s, h, half]), limit)
                 grad = (prob * (both[:, QROWS:] - delta_ref[s, h, half])).astype(BF)
@@ -892,91 +1004,276 @@
 
         lax.fori_loop(0, 2, sequence, 0)
         for k in range(h):
-            for step in range(1 if k == h - 1 else 2):
-                getattr(streams[k], todo[k].pop(0))()
-        streams[h].start()
+            move(k)
+        for st in streams[h]:
+            st.start()
+        advance((4, 6, 2)[h])
     while any(todo):
-        for k in range(HH):
-            if todo[k]:
-                name = todo[k].pop(0)
-                getattr(streams[k], name)()
-                if name == "finish" and todo[k]:
-                    getattr(streams[k], todo[k].pop(0))()
+        for h in range(HH):
+            move(h)
+        advance(1)
+
+    head_gains = gains[32:33]
+
+    def tile(t, is_key, grad):
+        v = joined[:, t * 128 : (t + 1) * 128]
+        low = lane_of(v.shape) < HD
+        back = grad * cosine[...] - swap_halves(grad) * sine[...]
+        inverse = lax.rsqrt(head_sums(v * v) * (1.0 / HD) + EPSILON)
+        scaled = back * tile_gain(head_gains, is_key)
+        inner = head_sums(scaled * v) * (1.0 / HD)
+        result = inverse * scaled - v * (inverse * inverse * inverse) * inner
+        if is_key:
+            result = jnp.where(low, result, grad)
+        d_joined[:, t * 128 : (t + 1) * 128] = result.astype(BF)
+        return jnp.sum(back * v * inverse, axis=0, keepdims=True)
+
+    q_terms = sum(tile(t, False, dq_ref[:, t * 128 : (t + 1) * 128]) for t in range(QW // 128))
+    k_terms = 0.0
     for h in range(HH):
-        dkv_out[h] = buffers[h][2]["sum"][...]
+        grad = jnp.concatenate([buffers[h][j][2]["sum"][...] for j in range(len(KV_PARTS))], axis=0)
+        k_terms = k_terms + tile(QW // 128 + h, True, grad)
+    q_terms = q_terms + pltpu.roll(q_terms, HD, 1)
+    head_terms[...] = jnp.where(lane_of(q_terms.shape) < HD, q_terms, pltpu.roll(k_terms, HD, 1))
+    other = pl.ds(pl.multiple_of((1 - core) * TOK, TOK), TOK)
+    swaps = []
+    for c in range(2):
+        load_w(c).wait()
+        w = w_ref[...].reshape(D // 2, QW + KVW)
+        part[c] = lax.dot_general(d_joined[...], w, NT, preferred_element_type=F32)
+        if c == 0:
+            load_w(1).start()
+        swaps.append(send(part.at[c, other], got.at[c], psem.at[1 + c], psem.at[3 + c], sibling))
+    advance(4)
+    outer((4, 0, QW + KVW), 0)
+    advance(4)
+    gain_row = jnp.concatenate([gains[j : j + 1] for j in range(D // 128)], axis=1)
+    for c in swaps:
+        c.wait_recv()
+
+    def last(r, carry):
+        rows = rows_at(r)
+        own = pl.ds(pl.multiple_of(core * TOK + r * 32, 32), 32)
+        e = jnp.concatenate([part[c, own, :] + got[c, rows, :] for c in range(2)], axis=1)
+        v = own_x[rows, :].astype(F32)
+        inverse = lax.rsqrt(jnp.sum(v * v, axis=1, keepdims=True) * (1.0 / D) + EPSILON)
+        scaled = e * gain_row
+        inner = jnp.sum(scaled * v, axis=1, keepdims=True) * (1.0 / D)
+        total = grad_mid[rows, :] + inverse * scaled - v * (inverse * inverse * inverse) * inner
+        input_grad[rows, :] = total.astype(BF)
+        return carry + jnp.sum(e * v * inverse, axis=0, keepdims=True)
+
+    terms[...] = lax.fori_loop(0, TOK // 32, last, jnp.zeros((1, D), F32))
+    advance(len(units))
+    drain((4, 0, QW + KVW), 0)
     for e in early:
         e.wait()
-    for st in streams:
-        for c in st.sent:
-            c.wait_send()
-
-
-def attend_back(tab, query, grad_attn, attn, log_sum, kv_sorted, grads, cid):
+    pending = [c for e in early for c in e.copies] + swaps + [c for group in streams for st in group for c in st.sent]
+    for c in pending:
+        c.wait_send()
+
+
+def attend_back(operands, cid):
     vmem = pl.BlockSpec(memory_space=pltpu.VMEM)
     anywhere = pl.BlockSpec(memory_space=pl.ANY)
+    tokens = 2 * TOK
+    widths = (FH, FH, FH, QW, QW + KVW)
     out = pl.pallas_call(
         attend_back_kernel,
         out_shape=[
-            jax.ShapeDtypeStruct((2 * TOK, QW), F32),
-            jax.ShapeDtypeStruct((HH, 2 * TOK, 2 * HD), F32),
+            jax.ShapeDtypeStruct((TOK, D), BF),
+            jax.ShapeDtypeStruct((1, D), F32),
+            jax.ShapeDtypeStruct((1, 128), F32),
         ]
+        + [jax.ShapeDtypeStruct((2, 4, 4, 2, 32, w), BF) for w in widths]
         + early_shapes(),
-        in_specs=[pl.BlockSpec(memory_space=pltpu.SMEM)] + [vmem] * 4 + [anywhere] * 5,
-        out_specs=[vmem, vmem] + [anywhere] * (2 * N_EARLY),
+        in_specs=[pl.BlockSpec(memory_space=pltpu.SMEM)]
+        + [vmem] * 5
+        + [anywhere]
+        + [vmem] * 8
+        + [anywhere]
+        + [vmem] * 5,
+        out_specs=[vmem] * 3 + [anywhere] * (5 + 2 * N_EARLY),
         scratch_shapes=[
-            pltpu.VMEM((2, HH, KEY_BLOCKS, SPANS_STEP, SPAN, 2 * HD), BF),
+            [pltpu.VMEM((2, KEY_BLOCKS, SPANS_STEP, SPAN, 2 * HD), BF)] * 2,
             pltpu.VMEM((2, HH, 2, 2 * QROWS, 2 * HD), BF),
             pltpu.VMEM((2, HH, 2, 1, QROWS), F32),
-            pltpu.VMEM((HH, 2, 4, 4, 2 * TOK, 2 * HD), BF),
+            pltpu.VMEM((HH, 2, 4, 4, tokens, 2 * HD), BF),
             pltpu.VMEM((2 * N_CTX, SPAN, 2 * HD), F32),
             pltpu.VMEM((2, 2 * HD, QROWS), F32),
-            [sum_scratch(KV_SUM_ORDERS[h], KV_DIMS, 2 * TOK, 2 * HD) for h in range(HH)],
-            pltpu.SemaphoreType.DMA((N_EARLY, 4)),
-            pltpu.SemaphoreType.DMA((N_EARLY, 4)),
-            pltpu.SemaphoreType.DMA((HH, 3, 6)),
-            pltpu.SemaphoreType.DMA((HH, 3, 6)),
-            pltpu.SemaphoreType.DMA((HH, 3)),
+            pltpu.VMEM((tokens, QW), F32),
+            [
+                [sum_scratch(order, KV_DIMS, rows, 2 * HD, False, True) for start, rows, order in KV_PARTS]
+                for h in range(HH)
+            ],
+            pltpu.VMEM((2, 2, 2, 4, 2, 32, 1152), BF),
+            pltpu.VMEM((3, 2, 4, 2, 16, 1152), BF),
+            pltpu.VMEM((2, 4, 4, 16, 1152), BF),
+            [
+                pltpu.VMEM((2,) + lead_shape(without(W_DIMS, order[0])) + (16, width), BF)
+                for a, start, width, order in SUMS[:N_EARLY]
+            ],
+            pltpu.VMEM((4, 4, 2, 32, QW + KVW), BF),
+            pltpu.VMEM((tokens, QW + KVW), BF),
+            pltpu.VMEM((2, tokens, D // 2), F32),
+            pltpu.VMEM((2, TOK, D // 2), F32),
+            pltpu.SemaphoreType.DMA((N_EARLY, 6)),
+            pltpu.SemaphoreType.DMA((N_EARLY, 6)),
+            pltpu.SemaphoreType.DMA((HH, 3, 3, 6)),
+            pltpu.SemaphoreType.DMA((HH, 3, 3, 6)),
             pltpu.SemaphoreType.DMA((2, HH)),
+            pltpu.SemaphoreType.DMA((2, 2)),
+            pltpu.SemaphoreType.DMA((5,)),
+            pltpu.SemaphoreType.DMA((5,)),
         ],
         compiler_params=pltpu.CompilerParams(
-            collective_id=cid, has_side_effects=True, vmem_limit_bytes=48 * 1024 * 1024
+            collective_id=cid, has_side_effects=True, vmem_limit_bytes=63 * 1024 * 1024
         ),
         name="attend_back",
-    )(tab, query, grad_attn, attn, log_sum, kv_sorted, *[g.reshape(2, 4, 4, 2, 32, g.shape[-1]) for g in grads])
-    return out[0], out[1], out[2:]
-
-
-def permutation(axis, by):
-    pairs = []
-    for c in range(N_CTX):
-        for f in range(4):
-            h, x, y = c // 16, (c // 4) % 4, c % 4
-            z, core = h * 2 + f // 2, f % 2
-            if axis == "x":
-                x = (x + by) % 4
-            elif axis == "y":
-                y = (y + by) % 4
-            elif axis == "z":
-                z = (z + by) % 4
-            else:
-                core = 1 - core
-            pairs.append((c * 4 + f, ((z // 2) * 16 + x * 4 + y) * 4 + (z % 2) * 2 + core))
-    return pairs
-
-
-def shift(value, axis, by=1):
-    return lax.ppermute(value, ("ctx", "fsdp"), permutation(axis, by))
-
-
-def norm_rows(value_in, gain_row):
-    inverse = lax.rsqrt(jnp.mean(value_in * value_in, axis=-1, keepdims=True) + EPSILON)
-    return (value_in * inverse * gain_row, inverse)
-
-
-def norm_back(value_in, inverse, gain_row, upstream):
-    scaled = upstream * gain_row
-    backward = inverse * scaled - value_in * inverse**3 * jnp.mean(scaled * value_in, axis=-1, keepdims=True)
-    return (backward, upstream * value_in * inverse)
+    )(*operands)
+    return out[0], out[1], out[2], out[3:8], out[8:]
+
+
+CHUNKS = ((0, 768), (768, 768), (1536, 640))
+
+
+def rows_at(r, n=32):
+    return pl.ds(pl.multiple_of(r * n, n), n)
+
+
+def feed_kernel(
+    attn, x, dy, gains, wo_h, wg_h, wu_h, wd_h,
+    result, grad_mid, grad_attn, normed, hid, dgate, dup, low_mid, stats, terms,
+    wo, wg, wu, wd, mid, part, got, part_f, got_f, wsem, psem,
+):
+    at = here()
+    core = at["core"]
+    sibling = moved(at, "core", 1)
+    loads = []
+    for i, (src, dst) in enumerate(((wo_h, wo), (wg_h, wg), (wu_h, wu), (wd_h, wd))):
+        loads.append(pltpu.make_async_copy(src, dst, wsem.at[i]))
+        loads[-1].start()
+    greet([sibling])
+    gain_row = jnp.concatenate([gains[16 + j : 17 + j] for j in range(D // 128)], axis=1)
+    sent = []
+    loads[0].wait()
+    for c in range(2):
+        cols = slice(c * 1024, (c + 1) * 1024)
+        part[0, c] = lax.dot_general(attn[...], wo[cols, :], NT, preferred_element_type=F32)
+        sent.append(send(part.at[0, c], got.at[0, c], psem.at[c, 0], psem.at[c, 1], sibling))
+    for c in sent:
+        c.wait_recv()
+
+    def root(v):
+        return jnp.sum(jnp.sqrt(jnp.sum(v * v, axis=1, keepdims=True) * (1.0 / D)), axis=0, keepdims=True)
+
+    def middle(r, carry):
+        rows = rows_at(r)
+        branch = jnp.concatenate([part[0, c, rows, :] + got[0, c, rows, :] for c in range(2)], axis=1)
+        v = x[rows, :].astype(F32)
+        m = v + branch
+        mid[rows, :] = m
+        inverse = lax.rsqrt(jnp.sum(m * m, axis=1, keepdims=True) * (1.0 / D) + EPSILON)
+        normed[rows, :] = (m * inverse * gain_row).astype(BF)
+        own = jnp.where(lax.div(r, TOK // 32) == core, 1.0, 0.0)
+        return tuple(t + own * root(u) for t, u in zip(carry, (v, branch, m)))
+
+    zero = jnp.zeros((1, 1), F32)
+    roots = lax.fori_loop(0, 2 * TOK // 32, middle, (zero, zero, zero))
+    for c in loads[1:]:
+        c.wait()
+    for start, width in CHUNKS:
+        cols = slice(start, start + width)
+        gate = jnp.dot(normed[...], wg[:, cols], preferred_element_type=F32)
+        up = jnp.dot(normed[...], wu[:, cols], preferred_element_type=F32)
+        back = jnp.dot(dy[...], wd[:, cols], preferred_element_type=F32)
+        sigmoid = lax.logistic(gate)
+        silu = gate * sigmoid
+        hid[:, cols] = (silu * up).astype(BF)
+        dup[:, cols] = (back * silu).astype(BF)
+        dgate[:, cols] = (back * up * sigmoid * (1.0 + gate * (1.0 - sigmoid))).astype(BF)
+    late = []
+    for c in range(2):
+        cols = slice(c * 1024, (c + 1) * 1024)
+        one = lax.dot_general(dgate[...], wg[cols, :], NT, preferred_element_type=F32)
+        part[1, c] = one + lax.dot_general(dup[...], wu[cols, :], NT, preferred_element_type=F32)
+        late.append(send(part.at[1, c], got.at[1, c], psem.at[2 + c, 0], psem.at[2 + c, 1], sibling))
+    part_f[...] = lax.dot_general(hid[...], wd[...], NT, preferred_element_type=F32)
+    other = pl.ds(pl.multiple_of((1 - core) * TOK, TOK), TOK)
+    last = send(part_f.at[other], got_f, psem.at[4, 0], psem.at[4, 1], sibling)
+
+    for c in late:
+        c.wait_recv()
+
+    def backward(r, carry):
+        rows = rows_at(r)
+        e = jnp.concatenate([part[1, c, rows, :] + got[1, c, rows, :] for c in range(2)], axis=1)
+        v = mid[rows, :]
+        inverse = lax.rsqrt(jnp.sum(v * v, axis=1, keepdims=True) * (1.0 / D) + EPSILON)
+        scaled = e * gain_row
+        inner = jnp.sum(scaled * v, axis=1, keepdims=True) * (1.0 / D)
+        total = dy[rows, :].astype(F32) + inverse * scaled - v * (inverse * inverse * inverse) * inner
+        low_mid[rows, :] = total.astype(BF)
+        mid[rows, :] = total
+        own = jnp.where(lax.div(r, TOK // 32) == core, 1.0, 0.0)
+        return carry + own * jnp.sum(e * v * inverse, axis=0, keepdims=True)
+
+    def finish(r, carry):
+        rows = rows_at(r)
+        own = pl.ds(pl.multiple_of(core * TOK + r * 32, 32), 32)
+        branch = part_f[own, :] + got_f[rows, :]
+        result[rows, :] = (mid[own, :] + branch).astype(BF)
+        return carry + root(branch)
+
+    last.wait_recv()
+    final = lax.fori_loop(0, TOK // 32, finish, zero)
+    terms[...] = lax.fori_loop(0, 2 * TOK // 32, backward, jnp.zeros((1, D), F32))
+    for i, v in enumerate(roots + (final,)):
+        stats[i : i + 1, :] = jnp.broadcast_to(v, (1, 128))
+    grad_attn[...] = jnp.dot(low_mid[...], wo[...], preferred_element_type=F32).astype(BF)
+    grad_mid[...] = mid[pl.ds(pl.multiple_of(core * TOK, TOK), TOK), :]
+    for c in sent + late + [last]:
+        c.wait_send()
+
+
+def feed(attn, x, dy, gains, w_out, w_gate, w_up, w_down, cid):
+    vmem = pl.BlockSpec(memory_space=pltpu.VMEM)
+    anywhere = pl.BlockSpec(memory_space=pl.ANY)
+    tokens = 2 * TOK
+    return pl.pallas_call(
+        feed_kernel,
+        out_shape=[
+            jax.ShapeDtypeStruct((TOK, D), BF),
+            jax.ShapeDtypeStruct((TOK, D), F32),
+            jax.ShapeDtypeStruct((tokens, QW), BF),
+            jax.ShapeDtypeStruct((tokens, D), BF),
+            jax.ShapeDtypeStruct((tokens, FH), BF),
+            jax.ShapeDtypeStruct((tokens, FH), BF),
+            jax.ShapeDtypeStruct((tokens, FH), BF),
+            jax.ShapeDtypeStruct((tokens, D), BF),
+            jax.ShapeDtypeStruct((4, 128), F32),
+            jax.ShapeDtypeStruct((1, D), F32),
+        ],
+        in_specs=[vmem] * 4 + [anywhere] * 4,
+        out_specs=[vmem] * 10,
+        scratch_shapes=[
+            pltpu.VMEM((D, QW), BF),
+            pltpu.VMEM((D, FH), BF),
+            pltpu.VMEM((D, FH), BF),
+            pltpu.VMEM((D, FH), BF),
+            pltpu.VMEM((tokens, D), F32),
+            pltpu.VMEM((2, 2, tokens, D // 2), F32),
+            pltpu.VMEM((2, 2, tokens, D // 2), F32),
+            pltpu.VMEM((tokens, D), F32),
+            pltpu.VMEM((TOK, D), F32),
+            pltpu.SemaphoreType.DMA((4,)),
+            pltpu.SemaphoreType.DMA((5, 2)),
+        ],
+        compiler_params=pltpu.CompilerParams(
+            collective_id=cid, has_side_effects=True, vmem_limit_bytes=62 * 1024 * 1024
+        ),
+        name="feed",
+    )(attn, x, dy, gains, w_out, w_gate, w_up, w_down)
 
 
 def body(layer_input, w_qkv, w_out, w_gate_up, w_down, norm_gains, span_map, cotangent):
@@ -987,10 +1284,6 @@
     w_v = w_qkv[:, (HQ + HK) * HD :].reshape(16, 2, HH, HD)
     w_kv = jnp.concatenate([w_k, w_v], axis=3).reshape(16, 2, KVW).transpose(1, 0, 2)
     shard_one = jnp.concatenate([w_q, w_kv], axis=2)
-    shard_gate = w_gate_up[:, :FF].reshape(16, 2, FH).transpose(1, 0, 2)
-    shard_up = w_gate_up[:, FF:].reshape(16, 2, FH).transpose(1, 0, 2)
-    shard_down = w_down.reshape(16, 2, FH).transpose(1, 0, 2)
-    shard_out = w_out.reshape(16, 2, QW).transpose(1, 0, 2)
     share = norm_gains.shape[0]
     device = lax.axis_index(("ctx", "fsdp"))
     own_gain = lax.dynamic_update_slice_in_dim(jnp.zeros((40 * 128,), F32), norm_gains.astype(F32), device * share, 0)
@@ -1033,95 +1326,44 @@
     cosine = jnp.concatenate([cosine] * 4, axis=1)
     sine = jnp.concatenate([-sine, sine] * 2, axis=1)
 
-    weights = [shard_one, shard_gate, shard_up, shard_down, shard_out]
-    (w_joined, w_gate, w_up, w_back, w_proj, x_pair, dy_pair, gains, joined, normed_one, query, keys, attn_f32, attn_low, log_sum) = front(
+    weights = [shard_one, w_gate_up, w_down, w_out]
+    (w_one, w_gate, w_up, w_back, w_proj, x_pair, dy_pair, gains, joined, normed_one, query, keys, attn_f32, attn_low, log_sum) = front(
         tab, weights, layer_input[0], cotangent[0], own_gain.reshape(40, 128), cosine, sine, 1
     )
-    w_joined, w_gate, w_up, w_back, w_proj = (w.reshape(D, -1) for w in (w_joined, w_gate, w_up, w_back, w_proj))
-    gain_one, gain_two = gains[:16].reshape(D), gains[16:32].reshape(D)
-    stream_in = x_pair.reshape(2 * TOK, D).astype(F32)
+    w_gate, w_up, w_back, w_proj = (w.reshape(D, -1) for w in (w_gate, w_up, w_back, w_proj))
     dy = dy_pair.reshape(2 * TOK, D)
 
-    partial_a = lax.dot_general(attn_low, w_proj, NT, preferred_element_type=F32)
-    branch_a = partial_a + shift(partial_a, "core")
-    middle = stream_in + branch_a
-    normed_two, inverse_two = norm_rows(middle, gain_two)
-    normed_two = normed_two.astype(BF)
-    gate_part = jnp.dot(normed_two, w_gate, preferred_element_type=F32)
-    up_part = jnp.dot(normed_two, w_up, preferred_element_type=F32)
-    sigmoid_gate = jax.nn.sigmoid(gate_part)
-    silu_gate = gate_part * sigmoid_gate
-    hidden = (silu_gate * up_part).astype(BF)
-    partial_f = lax.dot_general(hidden, w_back, NT, preferred_element_type=F32)
-    grad_hidden = jnp.dot(dy, w_back, preferred_element_type=F32)
-    grad_gate = (grad_hidden * up_part * sigmoid_gate * (1.0 + gate_part * (1.0 - sigmoid_gate))).astype(BF)
-    grad_up = (grad_hidden * silu_gate).astype(BF)
-    partial_n = lax.dot_general(grad_gate, w_gate, NT, preferred_element_type=F32)
-    partial_n = partial_n + lax.dot_general(grad_up, w_up, NT, preferred_element_type=F32)
-
-    def own_rows(value):
-        return lax.dynamic_slice_in_dim(value, core * TOK, TOK, 0)
-
-    def other_rows(value):
-        return lax.dynamic_slice_in_dim(value, (1 - core) * TOK, TOK, 0)
-
-    branch_f = own_rows(partial_f) + shift(other_rows(partial_f), "core")
-    result = own_rows(middle) + branch_f
-    grad_normed_two = partial_n + shift(partial_n, "core")
-    back_two, gain_two_terms = norm_back(middle, inverse_two, gain_two, grad_normed_two)
-    grad_middle = dy.astype(F32) + back_two
-    grad_branch = grad_middle.astype(BF)
-
-    def outer(left, right):
-        return lax.dot_general(left, right, TN, preferred_element_type=F32).astype(BF)
-
-    early = [outer(normed_two, grad_gate), outer(normed_two, grad_up), outer(dy, hidden), outer(grad_branch, attn_low)]
-
-    grad_attn = jnp.dot(grad_branch, w_proj, preferred_element_type=F32).astype(BF)
-    dq, grad_kv, begun = attend_back(tab, query, grad_attn, attn_f32, log_sum, keys, early, 4)
-    grad_joined, head_terms = rope_back(joined, dq, grad_kv, gains, cosine, sine)
-    partial_one = lax.dot_general(grad_joined, w_joined, NT, preferred_element_type=F32)
-    grad_normed_one = own_rows(partial_one) + shift(other_rows(partial_one), "core")
-    own_in = layer_input[0].astype(F32)
-    inverse_one = lax.rsqrt(jnp.mean(own_in * own_in, axis=-1, keepdims=True) + EPSILON)
-    back_one, gain_one_terms = norm_back(own_in, inverse_one, gain_one, grad_normed_one)
-    grad_input = own_rows(grad_middle) + back_one
-
-    def mean_root(stream):
-        return jnp.sum(jnp.sqrt(jnp.mean(stream * stream, axis=-1)))
-
-    stats = jnp.stack([mean_root(s) for s in (own_in, own_rows(branch_a), own_rows(middle))] + [mean_root(branch_f)])
+    result, grad_middle, grad_attn, normed_two, hidden, grad_gate, grad_up, grad_branch, stats, gain_two_terms = feed(
+        attn_low, x_pair.reshape(2 * TOK, D), dy, gains, w_proj, w_gate, w_up, w_back, 2
+    )
+    operands = (tab, query, grad_attn, attn_f32, attn_low, log_sum, keys, normed_two, dy, grad_branch, hidden)
+    operands += (grad_gate, grad_up, joined, normed_one, w_one, gains, cosine, sine, grad_middle, layer_input[0])
+    grad_input, gain_one_terms, head_terms, grads, begun = attend_back(operands, 4)
     sums = jnp.concatenate(
         [
-            jnp.sum(gain_one_terms, axis=0),
-            jnp.sum(own_rows(gain_two_terms), axis=0),
+            gain_one_terms[0],
+            gain_two_terms[0],
             head_terms[0],
-            stats,
+            stats[:, 0],
         ]
     )
     sums = jnp.pad(sums, (0, 40 * 128 - sums.shape[0])).reshape(40, 128)
-    own_gate, own_up, own_down, own_out, own_qkv, sums = sum_weights(
-        early + [outer(normed_one, grad_joined)], sums, begun, SUMS, 5, 62 * 1024 * 1024
+    grad_mlp, grad_down, grad_proj, own_qkv, sums = sum_weights(
+        grads, sums, begun, SUMS, 5, 62 * 1024 * 1024
     )
     sums = sums.reshape(-1)
-    grad_mlp = jnp.concatenate([own_gate[0], own_gate[1], own_up[0], own_up[1]], axis=1)
-    grad_down = jnp.concatenate([own_down[0], own_down[1]], axis=1)
-    kv_cols = own_qkv[:, :, QW:].reshape(2, 16, HH, 2, HD)
+    own_qkv = own_qkv.reshape(16, 2, QW + KVW)
+    kv_cols = own_qkv[:, :, QW:].reshape(16, 2, HH, 2, HD)
     grad_qkv = jnp.concatenate(
-        [
-            own_qkv[0, :, :QW],
-            own_qkv[1, :, :QW],
-            *(kv_cols[half, :, :, kind].reshape(16, HH * HD) for kind in range(2) for half in range(2)),
-        ],
+        [own_qkv[:, 0, :QW], own_qkv[:, 1, :QW]]
+        + [kv_cols[:, half, :, kind].reshape(16, HH * HD) for kind in range(2) for half in range(2)],
         axis=1,
     )
-    grad_proj = jnp.concatenate([own_out[0], own_out[1]], axis=1)
-
     own_gains = lax.dynamic_slice_in_dim(sums, device * share, share, 0)
     stream_rms = sums[4224:4228] / (TOK * N_CTX * 4)
     return (
-        result[None].astype(BF),
-        grad_input[None].astype(BF),
+        result[None],
+        grad_input[None],
         grad_qkv,
         grad_proj,
         grad_mlp,

time: 508 us -> 469 us (0.923)
  matrix products: 56.3 us -> 0 us
  Pallas kernels: 383 us -> 431 us
  other arithmetic: 23 us -> 6.38 us
  local copies, waits for them, and re-layouts: 28.4 us -> 21 us
  starting transfers between devices: 6.65 us -> 0 us
    pallas_call x2, Pallas kernels: 114 us -> 188 us  [the longest x1 144 us: attend_back(): pl.pallas_call(attend_back_kernel, out_shape=[jax.ShapeDtypeStruct((TOK,...]
    dot_general x14 -> x0, matrix products: 56.3 us -> none  [the longest x5 21.4 us: outer(): lax.dot_general(left, right, TN, preferred_element_type=F32).astype(BF)]
    pallas_call x1, Pallas kernels: 85.1 us -> 63.4 us  [sum_weights(): pl.pallas_call(functools.partial(weight_sum_kernel, pieces, n), out_shape...]
    reduce_sum x10 -> x0, other arithmetic: 14.1 us -> none  [the longest x6 6.84 us: mean_root(): return jnp.sum(jnp.sqrt(jnp.mean(stream * stream, axis=-1)))]
    ppermute x4 -> x0, starting transfers between devices: 6.65 us -> none  [shift(): return lax.ppermute(value, ('ctx', 'fsdp'), permutation(axis, by))]
    unnamed x84 -> x50, local copies, waits for them, and re-layouts: 8.08 us -> 14.2 us
  transfers between devices with their start and end apart: 4 -> 0, of which waited for: 0 -> 0; matrix products, arithmetic and copies ran while one was open for 9% -> 0% of each run, Pallas kernels for 23% -> 0%
where the time goes in v4:
time: 469 us; the launch traced here: 460 us
  Pallas kernels  431 us (92%)
  local copies, waits for them, and re-layouts  21 us (4%)
  other arithmetic  6.38 us (1%)
    pallas_call x1, Pallas kernels, front(): pl.pallas_call(front_kernel, out_shape=full + [jax.ShapeDtypeStruct((2,)...  180 us
    pallas_call x1, Pallas kernels, attend_back(): pl.pallas_call(attend_back_kernel, out_shape=[jax.ShapeDtypeStruct((TOK,...  144 us
    pallas_call x1, Pallas kernels, sum_weights(): pl.pallas_call(functools.partial(weight_sum_kernel, pieces, n), out_shape...  63.4 us
    pallas_call x1, Pallas kernels, feed(): pl.pallas_call(feed_kernel, out_shape=[jax.ShapeDtypeStruct((TOK, D), BF)...  44 us
    unnamed x50, local copies, waits for them, and re-layouts  14.2 us

profile of v4, /device:TPU:1, one launch (start us, length us, event | category | flops | bytes accessed | tf_op | source)
XLA Modules:
  0.0 460.1 jit_solution(8542343736225597990)
XLA Ops:
  0.7 0.8 broadcast_subtract_fusion
  1.7 0.7 broadcast_subtract_fusion.1
  3.2 0.8 convert_dynamic-update-slice_fusion
  3.9 0.7 fusion.6
  5.0 0.8 slice.36
  6.7 1.1 copy-done.1
  7.8 1.0 copy-done.7
  8.9 1.0 copy-done.9
  9.8 0.9 copy-done.10
  10.7 0.8 copy-done.12
  11.5 179.5 %front.1 = (bf16[2,4,4,2,32,1152]{5,4,3,2,1,0:T(8,128)(2,1)}, bf16[2,4,4,2,32,2176]{5,4,3,2,1,0:T(8,128)(2,1)}, bf16[2,4,4,2,32,2176]{5,4,3,2,1,0:T(8,128)(2,1)}...) custom-call(s32[2,334]{1,0:T(2,128)S(1)} %concatenate.32.tab.refs_0_, ...), custom_call_target="tpu_custom_call" | custom-call | tf_op jit(solution)/shard_map/front/pallas_call | solution.py:368
  191.1 1.0 copy-done
  192.0 0.7 copy-done.2
  192.8 1.0 copy-done.5
  193.8 0.9 copy-done.6
  194.7 0.7 copy-done.8
  195.5 0.6 copy-done.11
  196.1 0.6 copy-done.14
  196.7 44.0 %feed.1 = (bf16[128,2048]{1,0:T(8,128)(2,1)}, f32[128,2048]{1,0:T(8,128)}, bf16[256,768]{1,0:T(8,128)(2,1)}, bf16[256,2048]{1,0:T(8,128)(2,1)}, bf16[256,2176]{1...) custom-call(bf16[256,768]{1,0:T(8,128)(2,1)} %copy-done.2, ...), custom_call_target="tpu_custom_call" | custom-call | tf_op jit(solution)/shard_map/feed/pallas_call | solution.py:1243
  240.7 0.8 slice_reduce_fusion.4
  241.5 144.4 %attend_back.1 = (bf16[128,2048]{1,0:T(8,128)(2,1)}, f32[1,2048]{1,0:T(1,128)}, f32[1,128]{1,0:T(1,128)}, bf16[2,4,4,2,32,2176]{5,4,3,2,1,0:T(8,128)(2,1)}, bf16...) custom-call(s32[2,334]{1,0:T(2,128)} %copy-done.13, ...), custom_call_target="tpu_custom_call" | custom-call | tf_op jit(solution)/shard_map/attend_back/pallas_call | solution.py:1081
  386.0 1.3 fusion.1.refs_5_
  387.3 63.4 %sum_weights.1 = (f32[16,8704]{1,0:T(8,128)}, f32[16,4352]{1,0:T(8,128)}, f32[16,1536]{1,0:T(8,128)}, f32[16,2304]{1,0:T(8,128)}, f32[40,128]{1,0:T(8,128)}) custom-call(bf16[2,4,4,2,32,2176]{5,4,3,2,1,0:T(8,128)(2,1)} %get-tuple-element.88.refs_0_, bf16[2,4,4,2,32,2176]{5,4,3,2,1,0:T(8,128)(2,1)} %get-tuple-element.89.refs_1_, ...), custom_call_target="tpu_custom_call" | custom-call | tf_op jit(solution)/shard_map/sum_weights/pallas_call | solution.py:663
  450.7 1.4 dynamic_slice.11
  452.1 1.0 reshape.121
  453.1 1.2 slice_multiply_fusion
  455.2 0.7 concatenate.39
  455.9 0.8 copy.63
  456.7 0.8 copy.64
  457.5 0.6 copy.65
  458.2 0.8 copy.66
  459.0 0.7 copy.67
  (67 shorter events, 3.1 us)
Async XLA Ops:
  3.2 237.5 %copy-start.13 = (s32[2,334]{1,0:T(2,128)}, s32[2,334]{1,0:T(2,128)S(1)}, u32[]{:S(2)}) copy-start(s32[2,334]{1,0:T(2,128)S(1)} %concatenate.32.tab.refs_0_) | copy-start | bytes 8020
  6.7 234.0 %copy-start.3 = (f32[256,128]{1,0:T(8,128)}, f32[256,128]{1,0:T(8,128)S(1)}, u32[]{:S(2)}) copy-start(f32[256,128]{1,0:T(8,128)S(1)} %get-tuple-element.144.cosine.refs_17_) | copy-start | bytes 393220
  6.7 234.0 %copy-start.4 = (f32[256,128]{1,0:T(8,128)}, f32[256,128]{1,0:T(8,128)S(1)}, u32[]{:S(2)}) copy-start(f32[256,128]{1,0:T(8,128)S(1)} %get-tuple-element.145.sine.refs_18_) | copy-start | bytes 393220
  6.7 1.1 copy-start.1
  7.8 1.0 copy-start.7
  8.9 1.0 copy-start.9
  9.8 0.9 copy-start.10
  10.7 0.8 copy-start.12
  191.0 1.0 copy-start
  192.0 0.7 copy-start.2
  192.8 1.0 copy-start.5
  193.8 0.9 copy-start.6
  194.7 0.7 copy-start.8
  195.5 0.6 copy-start.11
  196.1 0.6 copy-start.14
  241.5 144.4 %copy-start.20 = (f32[1,2048]{1,0:T(1,128)S(1)}, f32[1,2048]{1,0:T(1,128)}, u32[]{:S(2)}) copy-start(f32[1,2048]{1,0:T(1,128)} %get-tuple-element.94) | copy-start | bytes 24580
  387.3 68.6 %copy-start.16 = (bf16[128,2048]{1,0:T(8,128)(2,1)S(1)}, bf16[128,2048]{1,0:T(8,128)(2,1)}, u32[]{:S(2)}) copy-start(bf16[128,2048]{1,0:T(8,128)(2,1)} %get-tuple-element.72) | copy-start | bytes 1572868
  450.6 6.1 %copy-start.17 = (bf16[128,2048]{1,0:T(8,128)(2,1)S(1)}, bf16[128,2048]{1,0:T(8,128)(2,1)}, u32[]{:S(2)}) copy-start(bf16[128,2048]{1,0:T(8,128)(2,1)} %get-tuple-element.87) | copy-start | bytes 1572868
  450.7 6.9 %copy-start.19 = (f32[16,1536]{1,0:T(8,128)S(1)}, f32[16,1536]{1,0:T(8,128)}, u32[]{:S(2)}) copy-start(f32[16,1536]{1,0:T(8,128)} %get-tuple-element.157) | copy-start | bytes 294916
  450.7 7.5 %copy-start.15 = (f32[16,8704]{1,0:T(8,128)S(1)}, f32[16,8704]{1,0:T(8,128)}, u32[]{:S(2)}) copy-start(f32[16,8704]{1,0:T(8,128)} %get-tuple-element.158) | copy-start | bytes 1671172
  450.7 8.3 %copy-start.18 = (f32[16,4352]{1,0:T(8,128)S(1)}, f32[16,4352]{1,0:T(8,128)}, u32[]{:S(2)}) copy-start(f32[16,4352]{1,0:T(8,128)} %get-tuple-element.159) | copy-start | bytes 835588

commit v5 on v4

--- a/solution.py
+++ b/solution.py
@@ -58,6 +58,7 @@
     (4, 768, 384, ORDERS[2]),
 )
 N_EARLY = 9
+ADVANCE = (0, 4, 0, 6, 0, 2)
 SIZES = {"x": 4, "y": 4, "z": 4, "h": 2}
 
 
@@ -404,7 +405,7 @@
             pltpu.SemaphoreType.DMA((HH + 1,)),
         ],
         compiler_params=pltpu.CompilerParams(
-            collective_id=cid, has_side_effects=True, vmem_limit_bytes=48 * 1024 * 1024
+            collective_id=cid, has_side_effects=True, vmem_limit_bytes=60 * 1024 * 1024
         ),
         name="front",
     )(tab, *shards, x, dy, gains, cosine, sine)
@@ -620,7 +621,7 @@
 def weight_sum_kernel(pieces, n, *refs):
     ins, small, begun, refs = refs[:n], refs[n], refs[n + 1 : n + 1 + 2 * N_EARLY], refs[n + 1 + 2 * N_EARLY :]
     outs, small_out = refs[: n - 1], refs[n - 1]
-    buffers, stages, swapped, small_buf, ssem, rsem, lsem, csem, tssem, trsem = refs[n:]
+    buffers, stages, swapped, halves, small_buf, ssem, rsem, lsem, csem, tssem, trsem = refs[n:]
     at = here()
     core = at["core"]
     sibling = moved(at, "core", 1)
@@ -643,7 +644,11 @@
 
     def put(a, half, value):
         width = value.shape[1]
-        ref, start = ((outs[0], 0), (outs[0], FF), (outs[1], 0), (outs[2], 0), (outs[3], 0))[a]
+        if a == 4:
+            outs[3][:, pl.ds(pl.multiple_of(half * QW, 128), QW)] = value[:, :QW]
+            halves[half] = value[:, QW:]
+            return
+        ref, start = ((outs[0], 0), (outs[0], FF), (outs[1], 0), (outs[2], 0))[a]
         ref[:, pl.ds(pl.multiple_of(start + half * width, 128), width)] = value
 
     for a in range(n):
@@ -651,6 +656,10 @@
     for a in range(n):
         copies[a].wait_recv()
         put(a, 1 - core, swapped[a][...])
+    for kind in range(2):
+        at_ = [half_kv[:, (2 * h + kind) * HD : (2 * h + kind + 1) * HD] for half_kv in (halves[0], halves[1]) for h in range(HH)]
+        start = HQ * HD + kind * HK * HD
+        outs[3][:, start : start + HK * HD] = jnp.concatenate(at_, axis=1)
     for c in copies + total.sent:
         c.wait_send()
 
@@ -662,7 +671,7 @@
     widths = [g.shape[-1] for g in grads]
     return pl.pallas_call(
         functools.partial(weight_sum_kernel, pieces, n),
-        out_shape=[jax.ShapeDtypeStruct((16, w), F32) for w in (2 * FF, FF, HQ * HD, 2 * (QW + KVW))]
+        out_shape=[jax.ShapeDtypeStruct((16, w), F32) for w in (2 * FF, FF, HQ * HD, (HQ + 2 * HK) * HD)]
         + [jax.ShapeDtypeStruct(small.shape, F32)],
         in_specs=[anywhere] * n + [vmem] + [anywhere] * len(begun),
         out_specs=[vmem] * n,
@@ -670,6 +679,7 @@
             [sum_scratch(order, W_DIMS, 32, width, k < N_EARLY) for k, (a, start, width, order) in enumerate(pieces)],
             [pltpu.VMEM((32, w), F32) for w in widths],
             [pltpu.VMEM((16, w), F32) for w in widths],
+            pltpu.VMEM((2, 16, KVW), F32),
             pltpu.VMEM((4, 4) + small.shape, F32),
             pltpu.SemaphoreType.DMA((count, 3, 6)),
             pltpu.SemaphoreType.DMA((count, 3, 6)),
@@ -836,10 +846,11 @@
     for c in load_keys(0):
         c.start()
 
-    def load_w(c):
-        return pltpu.make_async_copy(w_one.at[c], w_ref, psem.at[0])
-
-    load_w(0).start()
+    def load_w(start, width):
+        src = w_one.at[:, :, :, :, :, pl.ds(start, width)]
+        return pltpu.make_async_copy(src, w_ref.at[:, :, :, :, :, pl.ds(0, width)], psem.at[0])
+
+    load_w(0, QW).start()
     greet([sibling] + neighbours(at, ("x", "y", "z", "h")))
     sides = ((normed, dgate), (normed, dup), (dy, hid), (low_mid, attn_low), (normed_one, d_joined))
 
@@ -925,9 +936,9 @@
 
     def fetch():
         k, n = units[ahead[0]]
-        pool, slots, first = (mix_z, 2, 3) if early[k].axis == "z" else (mix, 3, 0)
-        slot = used.get(slots, 0) % slots
-        used[slots] = used.get(slots, 0) + 1
+        pool, slots, first = (mix_z, 2, 2) if early[k].axis == "z" else (mix, 2, 0)
+        slot = used.get(first, 0) % slots
+        used[first] = used.get(first, 0) + 1
         flying.append((k, n, early[k].load(n, pool.at[slot], msem.at[first + slot])))
         ahead[0] += 1
 
@@ -1002,16 +1013,14 @@
             lax.fori_loop(0, N_CTX, put, 0)
             return carry
 
-        lax.fori_loop(0, 2, sequence, 0)
-        for k in range(h):
-            move(k)
-        for st in streams[h]:
-            st.start()
-        advance((4, 6, 2)[h])
-    while any(todo):
-        for h in range(HH):
-            move(h)
-        advance(1)
+        for s in range(2):
+            sequence(s, 0)
+            if s == 1:
+                for k in range(h):
+                    move(k)
+                for st in streams[h]:
+                    st.start()
+            advance(ADVANCE[2 * h + s])
 
     head_gains = gains[32:33]
 
@@ -1028,7 +1037,27 @@
         d_joined[:, t * 128 : (t + 1) * 128] = result.astype(BF)
         return jnp.sum(back * v * inverse, axis=0, keepdims=True)
 
-    q_terms = sum(tile(t, False, dq_ref[:, t * 128 : (t + 1) * 128]) for t in range(QW // 128))
+    def undo_queries():
+        return sum(tile(t, False, dq_ref[:, t * 128 : (t + 1) * 128]) for t in range(QW // 128))
+
+    def back_part(c, start, width):
+        w = w_ref[c, :, :, :, :, :width].reshape(D // 2, width)
+        return lax.dot_general(d_joined[:, start : start + width], w, NT, preferred_element_type=F32)
+
+    def queries_back():
+        load_w(0, QW).wait()
+        for c in range(2):
+            part[c] = back_part(c, 0, QW)
+        load_w(QW, KVW).start()
+
+    q_terms = undo_queries()
+    tasks = [queries_back, lambda: outer((4, 0, QW), 0)]
+    while any(todo):
+        for h in range(HH):
+            move(h)
+        if tasks:
+            tasks.pop(0)()
+        advance(1)
     k_terms = 0.0
     for h in range(HH):
         grad = jnp.concatenate([buffers[h][j][2]["sum"][...] for j in range(len(KV_PARTS))], axis=0)
@@ -1036,17 +1065,14 @@
     q_terms = q_terms + pltpu.roll(q_terms, HD, 1)
     head_terms[...] = jnp.where(lane_of(q_terms.shape) < HD, q_terms, pltpu.roll(k_terms, HD, 1))
     other = pl.ds(pl.multiple_of((1 - core) * TOK, TOK), TOK)
+    load_w(QW, KVW).wait()
     swaps = []
     for c in range(2):
-        load_w(c).wait()
-        w = w_ref[...].reshape(D // 2, QW + KVW)
-        part[c] = lax.dot_general(d_joined[...], w, NT, preferred_element_type=F32)
-        if c == 0:
-            load_w(1).start()
+        part[c] += back_part(c, QW, KVW)
         swaps.append(send(part.at[c, other], got.at[c], psem.at[1 + c], psem.at[3 + c], sibling))
-    advance(4)
-    outer((4, 0, QW + KVW), 0)
-    advance(4)
+    advance(2)
+    outer((4, QW, KVW), 1)
+    advance(2)
     gain_row = jnp.concatenate([gains[j : j + 1] for j in range(D // 128)], axis=1)
     for c in swaps:
         c.wait_recv()
@@ -1065,7 +1091,8 @@
 
     terms[...] = lax.fori_loop(0, TOK // 32, last, jnp.zeros((1, D), F32))
     advance(len(units))
-    drain((4, 0, QW + KVW), 0)
+    drain((4, 0, QW), 0)
+    drain((4, QW, KVW), 1)
     for e in early:
         e.wait()
     pending = [c for e in early for c in e.copies] + swaps + [c for group in streams for st in group for c in st.sent]
@@ -1107,13 +1134,13 @@
                 for h in range(HH)
             ],
             pltpu.VMEM((2, 2, 2, 4, 2, 32, 1152), BF),
-            pltpu.VMEM((3, 2, 4, 2, 16, 1152), BF),
+            pltpu.VMEM((2, 2, 4, 2, 16, 1152), BF),
             pltpu.VMEM((2, 4, 4, 16, 1152), BF),
             [
                 pltpu.VMEM((2,) + lead_shape(without(W_DIMS, order[0])) + (16, width), BF)
                 for a, start, width, order in SUMS[:N_EARLY]
             ],
-            pltpu.VMEM((4, 4, 2, 32, QW + KVW), BF),
+            pltpu.VMEM((2, 4, 4, 2, 32, QW), BF),
             pltpu.VMEM((tokens, QW + KVW), BF),
             pltpu.VMEM((2, tokens, D // 2), F32),
             pltpu.VMEM((2, TOK, D // 2), F32),
@@ -1144,13 +1171,13 @@
 def feed_kernel(
     attn, x, dy, gains, wo_h, wg_h, wu_h, wd_h,
     result, grad_mid, grad_attn, normed, hid, dgate, dup, low_mid, stats, terms,
-    wo, wg, wu, wd, mid, part, got, part_f, got_f, wsem, psem,
+    wo, wg, wu, wd, mid, part, got, part_f, got_f, back_ref, wsem, psem,
 ):
     at = here()
     core = at["core"]
     sibling = moved(at, "core", 1)
     loads = []
-    for i, (src, dst) in enumerate(((wo_h, wo), (wg_h, wg), (wu_h, wu), (wd_h, wd))):
+    for i, (src, dst) in enumerate(((wo_h, wo), (wd_h, wd), (wg_h, wg), (wu_h, wu))):
         loads.append(pltpu.make_async_copy(src, dst, wsem.at[i]))
         loads[-1].start()
     greet([sibling])
@@ -1161,6 +1188,10 @@
         cols = slice(c * 1024, (c + 1) * 1024)
         part[0, c] = lax.dot_general(attn[...], wo[cols, :], NT, preferred_element_type=F32)
         sent.append(send(part.at[0, c], got.at[0, c], psem.at[c, 0], psem.at[c, 1], sibling))
+    loads[1].wait()
+    for start, width in CHUNKS:
+        cols = slice(start, start + width)
+        back_ref[:, cols] = jnp.dot(dy[...], wd[:, cols], preferred_element_type=F32)
     for c in sent:
         c.wait_recv()
 
@@ -1180,13 +1211,13 @@
 
     zero = jnp.zeros((1, 1), F32)
     roots = lax.fori_loop(0, 2 * TOK // 32, middle, (zero, zero, zero))
-    for c in loads[1:]:
+    for c in loads[2:]:
         c.wait()
     for start, width in CHUNKS:
         cols = slice(start, start + width)
         gate = jnp.dot(normed[...], wg[:, cols], preferred_element_type=F32)
         up = jnp.dot(normed[...], wu[:, cols], preferred_element_type=F32)
-        back = jnp.dot(dy[...], wd[:, cols], preferred_element_type=F32)
+        back = back_ref[:, cols]
         sigmoid = lax.logistic(gate)
         silu = gate * sigmoid
         hid[:, cols] = (silu * up).astype(BF)
@@ -1266,6 +1297,7 @@
             pltpu.VMEM((2, 2, tokens, D // 2), F32),
             pltpu.VMEM((tokens, D), F32),
             pltpu.VMEM((TOK, D), F32),
+            pltpu.VMEM((tokens, FH), F32),
             pltpu.SemaphoreType.DMA((4,)),
             pltpu.SemaphoreType.DMA((5, 2)),
         ],
@@ -1348,22 +1380,17 @@
         ]
     )
     sums = jnp.pad(sums, (0, 40 * 128 - sums.shape[0])).reshape(40, 128)
-    grad_mlp, grad_down, grad_proj, own_qkv, sums = sum_weights(
+    grad_mlp, grad_down, grad_proj, grad_qkv, sums = sum_weights(
         grads, sums, begun, SUMS, 5, 62 * 1024 * 1024
     )
     sums = sums.reshape(-1)
-    own_qkv = own_qkv.reshape(16, 2, QW + KVW)
-    kv_cols = own_qkv[:, :, QW:].reshape(16, 2, HH, 2, HD)
-    grad_qkv = jnp.concatenate(
-        [own_qkv[:, 0, :QW], own_qkv[:, 1, :QW]]
-        + [kv_cols[:, half, :, kind].reshape(16, HH * HD) for kind in range(2) for half in range(2)],
-        axis=1,
-    )
     own_gains = lax.dynamic_slice_in_dim(sums, device * share, share, 0)
     stream_rms = sums[4224:4228] / (TOK * N_CTX * 4)
+    arrays = [result[None], grad_input[None], grad_qkv, grad_proj, grad_mlp, grad_down]
+    result, grad_input, grad_qkv, grad_proj, grad_mlp, grad_down = publish(arrays)
     return (
-        result[None],
-        grad_input[None],
+        result,
+        grad_input,
         grad_qkv,
         grad_proj,
         grad_mlp,
@@ -1371,6 +1398,27 @@
         own_gains,
         stream_rms,
     )
+
+
+def publish_kernel(n, *refs):
+    copies = [pltpu.make_async_copy(refs[i], refs[n + i], refs[2 * n].at[i]) for i in range(n)]
+    for c in copies:
+        c.start()
+    for c in copies:
+        c.wait()
+
+
+def publish(arrays):
+    n = len(arrays)
+    anywhere = pl.BlockSpec(memory_space=pl.ANY)
+    return pl.pallas_call(
+        functools.partial(publish_kernel, n),
+        out_shape=[jax.ShapeDtypeStruct(a.shape, a.dtype) for a in arrays],
+        in_specs=[pl.BlockSpec(memory_space=pltpu.VMEM)] * n,
+        out_specs=[anywhere] * n,
+        scratch_shapes=[pltpu.SemaphoreType.DMA((n,))],
+        name="publish",
+    )(*arrays)
 
 
 def solution(mesh):

time: 469 us -> 447 us (0.953); the launches traced: 460 us -> 444 us
  local copies, waits for them, and re-layouts: 21 us -> 4.72 us
    unnamed x50 -> x4, local copies, waits for them, and re-layouts: 14.2 us -> 0.01 us
where the time goes in v5:
time: 447 us; the launch traced here: 444 us
  Pallas kernels  430 us (96%)
  other arithmetic  7.67 us (2%)
  local copies, waits for them, and re-layouts  4.72 us (1%)
    pallas_call x1, Pallas kernels, front(): pl.pallas_call(front_kernel, out_shape=full + [jax.ShapeDtypeStruct((2,)...  181 us
    pallas_call x1, Pallas kernels, attend_back(): pl.pallas_call(attend_back_kernel, out_shape=[jax.ShapeDtypeStruct((TOK,...  143 us
    pallas_call x1, Pallas kernels, sum_weights(): pl.pallas_call(functools.partial(weight_sum_kernel, pieces, n), out_shape...  63 us
    pallas_call x1, Pallas kernels, feed(): pl.pallas_call(feed_kernel, out_shape=[jax.ShapeDtypeStruct((TOK, D), BF)...  40.6 us

profile of v5, /device:TPU:1, one launch (start us, length us, event | category | flops | bytes accessed | tf_op | source)
XLA Modules:
  0.0 443.6 jit_solution(17084639904198104791)
XLA Ops:
  0.7 0.8 broadcast_subtract_fusion
  1.5 0.1 add_multiply_fusion
  1.5 0.1 add_convert_fusion
  1.6 0.1 convert_element_type.33
  1.7 0.7 broadcast_subtract_fusion.1
  2.4 0.1 select_reduce_fusion
  2.5 0.1 rev.3
  2.6 0.1 and_select_fusion.2
  2.7 0.1 reduce
  2.8 0.1 compare_select_fusion.2
  2.9 0.1 compare_convert_fusion
  3.0 0.1 compare_convert_fusion.1
  3.0 0.7 concatenate.29.tab.refs_0_
  3.7 0.7 convert_dynamic-update-slice_fusion
  4.5 0.7 fusion.5
  5.2 0.1 reshape.104
  5.3 0.1 reshape.105
  5.4 0.1 pad_maximum_fusion.3
  5.5 0.8 slice.15
  6.4 0.6 pad_maximum_fusion.2.shard_one
  7.0 0.5 fusion
  7.5 1.0 pad_maximum_fusion
  8.5 0.0 copy-done
  8.5 180.7 %front.1 = (bf16[2,4,4,2,32,1152]{5,4,3,2,1,0:T(8,128)(2,1)}, bf16[2,4,4,2,32,2176]{5,4,3,2,1,0:T(8,128)(2,1)}, bf16[2,4,4,2,32,2176]{5,4,3,2,1,0:T(8,128)(2,1)}...) custom-call(s32[2,334]{1,0:T(2,128)} %concatenate.29.tab.refs_0_, ...), custom_call_target="tpu_custom_call" | custom-call | tf_op jit(solution)/shard_map/front/pallas_call | solution.py:369
  189.2 40.6 %feed.1 = (bf16[128,2048]{1,0:T(8,128)(2,1)}, f32[128,2048]{1,0:T(8,128)}, bf16[256,768]{1,0:T(8,128)(2,1)}, bf16[256,2048]{1,0:T(8,128)(2,1)}, bf16[256,2176]{1...) custom-call(bf16[256,768]{1,0:T(8,128)(2,1)} %get-tuple-element.70.a, ...), custom_call_target="tpu_custom_call" | custom-call | tf_op jit(solution)/shard_map/feed/pallas_call | solution.py:1274
  229.8 0.8 slice_reduce_fusion
  230.6 143.0 %attend_back.1 = (bf16[128,2048]{1,0:T(8,128)(2,1)}, f32[1,2048]{1,0:T(1,128)}, f32[1,128]{1,0:T(1,128)}, bf16[2,4,4,2,32,2176]{5,4,3,2,1,0:T(8,128)(2,1)}, bf16...) custom-call(s32[2,334]{1,0:T(2,128)} %concatenate.29.tab.refs_0_, ...), custom_call_target="tpu_custom_call" | custom-call | tf_op jit(solution)/shard_map/attend_back/pallas_call | solution.py:1108
  373.6 1.3 fusion.1.refs_5_
  375.0 63.0 %sum_weights.1 = (f32[16,8704]{1,0:T(8,128)}, f32[16,4352]{1,0:T(8,128)}, f32[16,1536]{1,0:T(8,128)}, f32[16,2304]{1,0:T(8,128)}, f32[40,128]{1,0:T(8,128)}) custom-call(bf16[2,4,4,2,32,2176]{5,4,3,2,1,0:T(8,128)(2,1)} %get-tuple-element.94.refs_0_, bf16[2,4,4,2,32,2176]{5,4,3,2,1,0:T(8,128)(2,1)} %get-tuple-element.95.refs_1_, ...), custom_call_target="tpu_custom_call" | custom-call | tf_op jit(solution)/shard_map/sum_weights/pallas_call | solution.py:672
  438.0 1.3 dynamic_slice.11
  439.3 2.9 publish.1
  442.2 1.2 slice_multiply_fusion
  (12 shorter events, 0.1 us)
Async XLA Ops:
  4.5 4.0 copy-start
  230.6 143.0 %copy-start.1 = (f32[1,2048]{1,0:T(1,128)S(1)}, f32[1,2048]{1,0:T(1,128)}, u32[]{:S(2)}) copy-start(f32[1,2048]{1,0:T(1,128)} %get-tuple-element.100) | copy-start | bytes 24580

commit v6 on v5

--- a/solution.py
+++ b/solution.py
@@ -319,22 +319,21 @@
     every(rest, "pass_on")
     product(0, 384)
     every(keys, "pass_on")
-    every(rest[:3], "finish", "start")
     every(keys, "finish", "start")
     product(384, 384)
     every(keys, "pass_on")
     for t in range(QW // 128):
         query[:, t * 128 : (t + 1) * 128] = rope(t, False)
     every(keys, "finish", "start")
-    every(rest[3:], "finish")
     blank = jnp.zeros((QROWS, HD), BF)
     for s in range(2):
         for h in range(HH):
             for half in range(2):
                 q_ref[s, h, half] = jnp.concatenate([heads_at(query, s, h, half), blank], axis=1)
     every(keys, "pass_on")
-    every(rest[3:], "start")
     every(keys, "finish")
+    every(rest[:3] + rest[6:], "finish", "start")
+    every(rest[3:6], "finish")
 
     def sort(p, carry):
         for s in range(2):
@@ -350,8 +349,8 @@
     attend_heads(tab, 0, q_ref, kvs, o_ref, low_ref, l_ref, acc, sum_ref)
     every(rest[:3], "pass_on")
     attend_heads(tab, 1, q_ref, kvs, o_ref, low_ref, l_ref, acc, sum_ref)
-    every(rest[3:], "pass_on")
-    every(rest, "finish")
+    every(rest[6:], "pass_on")
+    every(rest[:3] + rest[6:], "finish")
     keep_keys.wait()
     arrived(6)
     keep.wait()
@@ -581,7 +580,11 @@
 def run_sums(streams, total):
     todo = []
     for s in streams:
-        s.start()
+        if s.begun is None:
+            s.start()
+    for s in streams:
+        if s.begun is not None:
+            s.start()
         steps = [("pass_on",), ("finish", "start"), ("pass_on",), ("finish", "start"), ("pass_on",), ("finish",)]
         todo.append(steps[1:] if s.begun is not None else steps)
     while any(todo):
@@ -1161,7 +1164,8 @@
     return out[0], out[1], out[2], out[3:8], out[8:]
 
 
-CHUNKS = ((0, 768), (768, 768), (1536, 640))
+FIRST = ((0, 768), (768, 384))
+SECOND = ((1152, 1024),)
 
 
 def rows_at(r, n=32):
@@ -1171,27 +1175,54 @@
 def feed_kernel(
     attn, x, dy, gains, wo_h, wg_h, wu_h, wd_h,
     result, grad_mid, grad_attn, normed, hid, dgate, dup, low_mid, stats, terms,
-    wo, wg, wu, wd, mid, part, got, part_f, got_f, back_ref, wsem, psem,
+    wo, wg, wu, wd, mid, part, got, part_f, got_f, back_ref, wsem, psem, gssem, grsem,
 ):
     at = here()
     core = at["core"]
     sibling = moved(at, "core", 1)
-    loads = []
+    late_cols = pl.ds(1152, 1024)
+    weights = ((wg_h, wg), (wu_h, wu), (wd_h, wd))
+    quarters, loads = [], []
+    for k, (src, dst) in enumerate(weights):
+        held = labels(ORDERS[k][2], at[ORDERS[k][2]])
+        tail = (slice(None), late_cols)
+        quarters.append(
+            pltpu.make_async_copy(pick(src, W_DIMS, held, tail), pick(dst, W_DIMS, held, tail), wsem.at[4 + k])
+        )
+        quarters[-1].start()
+    whole = (slice(None),) * 5
     for i, (src, dst) in enumerate(((wo_h, wo), (wd_h, wd), (wg_h, wg), (wu_h, wu))):
-        loads.append(pltpu.make_async_copy(src, dst, wsem.at[i]))
+        cols = whole + (pl.ds(0, QW if i == 0 else 1152),)
+        loads.append(pltpu.make_async_copy(src.at[cols], dst.at[cols], wsem.at[i]))
         loads[-1].start()
-    greet([sibling])
+    greet([sibling] + neighbours(at, ("x", "y", "z")))
+    gathers = []
+    for k, (src, dst) in enumerate(weights):
+        quarters[k].wait()
+        g = Gathering(dst, W_DIMS, at, ORDERS[k], 32, late_cols, gssem.at[k], grsem.at[k])
+        g.phase = 2
+        g.start()
+        gathers.append(g)
+
+    def columns(ref, start, width):
+        return ref[:, :, :, :, :, start : start + width].reshape(D, width)
+
+    def half_rows(ref, c, start, width):
+        return ref[c, :, :, :, :, start : start + width].reshape(D // 2, width)
+
     gain_row = jnp.concatenate([gains[16 + j : 17 + j] for j in range(D // 128)], axis=1)
     sent = []
     loads[0].wait()
     for c in range(2):
-        cols = slice(c * 1024, (c + 1) * 1024)
-        part[0, c] = lax.dot_general(attn[...], wo[cols, :], NT, preferred_element_type=F32)
+        part[0, c] = lax.dot_general(attn[...], half_rows(wo, c, 0, QW), NT, preferred_element_type=F32)
         sent.append(send(part.at[0, c], got.at[0, c], psem.at[c, 0], psem.at[c, 1], sibling))
     loads[1].wait()
-    for start, width in CHUNKS:
-        cols = slice(start, start + width)
-        back_ref[:, cols] = jnp.dot(dy[...], wd[:, cols], preferred_element_type=F32)
+
+    def product(out, left, right, pieces):
+        for start, width in pieces:
+            out[:, start : start + width] = jnp.dot(left[...], columns(right, start, width), preferred_element_type=F32)
+
+    product(back_ref, dy, wd, FIRST)
     for c in sent:
         c.wait_recv()
 
@@ -1213,23 +1244,44 @@
     roots = lax.fori_loop(0, 2 * TOK // 32, middle, (zero, zero, zero))
     for c in loads[2:]:
         c.wait()
-    for start, width in CHUNKS:
+
+    def hidden(pieces):
+        for start, width in pieces:
+            cols = slice(start, start + width)
+            gate = jnp.dot(normed[...], columns(wg, start, width), preferred_element_type=F32)
+            up = jnp.dot(normed[...], columns(wu, start, width), preferred_element_type=F32)
+            back = back_ref[:, cols]
+            sigmoid = lax.logistic(gate)
+            silu = gate * sigmoid
+            hid[:, cols] = (silu * up).astype(BF)
+            dup[:, cols] = (back * silu).astype(BF)
+            dgate[:, cols] = (back * up * sigmoid * (1.0 + gate * (1.0 - sigmoid))).astype(BF)
+
+    def back_half(c, start, width):
         cols = slice(start, start + width)
-        gate = jnp.dot(normed[...], wg[:, cols], preferred_element_type=F32)
-        up = jnp.dot(normed[...], wu[:, cols], preferred_element_type=F32)
-        back = back_ref[:, cols]
-        sigmoid = lax.logistic(gate)
-        silu = gate * sigmoid
-        hid[:, cols] = (silu * up).astype(BF)
-        dup[:, cols] = (back * silu).astype(BF)
-        dgate[:, cols] = (back * up * sigmoid * (1.0 + gate * (1.0 - sigmoid))).astype(BF)
+        one = lax.dot_general(dgate[:, cols], half_rows(wg, c, start, width), NT, preferred_element_type=F32)
+        return one + lax.dot_general(dup[:, cols], half_rows(wu, c, start, width), NT, preferred_element_type=F32)
+
+    def forward_half(c, start, width):
+        cols = slice(start, start + width)
+        return lax.dot_general(hid[:, cols], half_rows(wd, c, start, width), NT, preferred_element_type=F32)
+
+    hidden(FIRST)
+    for g in gathers:
+        g.pass_on()
+    for c in range(2):
+        part[1, c] = back_half(c, 0, 1152)
+        part_f[:, c * 1024 : (c + 1) * 1024] = forward_half(c, 0, 1152)
+    for g in gathers:
+        g.finish()
+    product(back_ref, dy, wd, SECOND)
+    hidden(SECOND)
     late = []
     for c in range(2):
-        cols = slice(c * 1024, (c + 1) * 1024)
-        one = lax.dot_general(dgate[...], wg[cols, :], NT, preferred_element_type=F32)
-        part[1, c] = one + lax.dot_general(dup[...], wu[cols, :], NT, preferred_element_type=F32)
+        part[1, c] += back_half(c, 1152, 1024)
         late.append(send(part.at[1, c], got.at[1, c], psem.at[2 + c, 0], psem.at[2 + c, 1], sibling))
-    part_f[...] = lax.dot_general(hid[...], wd[...], NT, preferred_element_type=F32)
+    for c in range(2):
+        part_f[:, c * 1024 : (c + 1) * 1024] += forward_half(c, 1152, 1024)
     other = pl.ds(pl.multiple_of((1 - core) * TOK, TOK), TOK)
     last = send(part_f.at[other], got_f, psem.at[4, 0], psem.at[4, 1], sibling)
 
@@ -1261,10 +1313,12 @@
     terms[...] = lax.fori_loop(0, 2 * TOK // 32, backward, jnp.zeros((1, D), F32))
     for i, v in enumerate(roots + (final,)):
         stats[i : i + 1, :] = jnp.broadcast_to(v, (1, 128))
-    grad_attn[...] = jnp.dot(low_mid[...], wo[...], preferred_element_type=F32).astype(BF)
+    grad_attn[...] = jnp.dot(low_mid[...], columns(wo, 0, QW), preferred_element_type=F32).astype(BF)
     grad_mid[...] = mid[pl.ds(pl.multiple_of(core * TOK, TOK), TOK), :]
     for c in sent + late + [last]:
         c.wait_send()
+    for g in gathers:
+        g.wait_sent()
 
 
 def feed(attn, x, dy, gains, w_out, w_gate, w_up, w_down, cid):
@@ -1288,18 +1342,20 @@
         in_specs=[vmem] * 4 + [anywhere] * 4,
         out_specs=[vmem] * 10,
         scratch_shapes=[
-            pltpu.VMEM((D, QW), BF),
-            pltpu.VMEM((D, FH), BF),
-            pltpu.VMEM((D, FH), BF),
-            pltpu.VMEM((D, FH), BF),
+            pltpu.VMEM((2, 4, 4, 2, 32, QW), BF),
+            pltpu.VMEM((2, 4, 4, 2, 32, FH), BF),
+            pltpu.VMEM((2, 4, 4, 2, 32, FH), BF),
+            pltpu.VMEM((2, 4, 4, 2, 32, FH), BF),
             pltpu.VMEM((tokens, D), F32),
             pltpu.VMEM((2, 2, tokens, D // 2), F32),
             pltpu.VMEM((2, 2, tokens, D // 2), F32),
             pltpu.VMEM((tokens, D), F32),
             pltpu.VMEM((TOK, D), F32),
             pltpu.VMEM((tokens, FH), F32),
-            pltpu.SemaphoreType.DMA((4,)),
+            pltpu.SemaphoreType.DMA((7,)),
             pltpu.SemaphoreType.DMA((5, 2)),
+            pltpu.SemaphoreType.DMA((3, 3, 4)),
+            pltpu.SemaphoreType.DMA((3, 3, 4)),
         ],
         compiler_params=pltpu.CompilerParams(
             collective_id=cid, has_side_effects=True, vmem_limit_bytes=62 * 1024 * 1024
@@ -1362,7 +1418,6 @@
     (w_one, w_gate, w_up, w_back, w_proj, x_pair, dy_pair, gains, joined, normed_one, query, keys, attn_f32, attn_low, log_sum) = front(
         tab, weights, layer_input[0], cotangent[0], own_gain.reshape(40, 128), cosine, sine, 1
     )
-    w_gate, w_up, w_back, w_proj = (w.reshape(D, -1) for w in (w_gate, w_up, w_back, w_proj))
     dy = dy_pair.reshape(2 * TOK, D)
 
     result, grad_middle, grad_attn, normed_two, hidden, grad_gate, grad_up, grad_branch, stats, gain_two_terms = feed(

time: 447 us -> 443 us (level)
    pallas_call x1, Pallas kernels: 40.6 us -> 73.3 us  [feed(): pl.pallas_call(feed_kernel, out_shape=[jax.ShapeDtypeStruct((TOK, D), BF)...]
    pallas_call x1, Pallas kernels: 181 us -> 148 us  [front(): pl.pallas_call(front_kernel, out_shape=full + [jax.ShapeDtypeStruct((2,)...]
where the time goes in v6:
time: 443 us; the launch traced here: 440 us
  Pallas kernels  426 us (96%)
  other arithmetic  7.67 us (2%)
  local copies, waits for them, and re-layouts  4.72 us (1%)
    pallas_call x1, Pallas kernels, front(): pl.pallas_call(front_kernel, out_shape=full + [jax.ShapeDtypeStruct((2,)...  148 us
    pallas_call x1, Pallas kernels, attend_back(): pl.pallas_call(attend_back_kernel, out_shape=[jax.ShapeDtypeStruct((TOK,...  139 us
    pallas_call x1, Pallas kernels, feed(): pl.pallas_call(feed_kernel, out_shape=[jax.ShapeDtypeStruct((TOK, D), BF)...  73.3 us
    pallas_call x1, Pallas kernels, sum_weights(): pl.pallas_call(functools.partial(weight_sum_kernel, pieces, n), out_shape...  62.5 us

profile of v6, /device:TPU:1, one launch (start us, length us, event | category | flops | bytes accessed | tf_op | source)
XLA Modules:
  0.0 439.9 jit_solution(7892563386288718302)
XLA Ops:
  0.7 0.8 broadcast_subtract_fusion
  1.5 0.1 add_multiply_fusion
  1.5 0.1 add_convert_fusion
  1.6 0.1 convert_element_type.33
  1.7 0.7 broadcast_subtract_fusion.1
  2.4 0.1 select_reduce_fusion
  2.5 0.1 rev.3
  2.6 0.1 and_select_fusion.2
  2.7 0.1 reduce
  2.8 0.1 compare_select_fusion.2
  2.9 0.1 compare_convert_fusion
  3.0 0.1 compare_convert_fusion.1
  3.0 0.7 concatenate.29.tab.refs_0_
  3.7 0.7 convert_dynamic-update-slice_fusion
  4.5 0.7 fusion.5
  5.2 0.1 reshape.92
  5.3 0.1 reshape.93
  5.4 0.1 pad_maximum_fusion.3
  5.5 0.8 slice.15
  6.4 0.6 pad_maximum_fusion.2.shard_one
  7.0 0.5 fusion
  7.5 1.0 pad_maximum_fusion
  8.5 0.0 copy-done
  8.5 148.4 %front.1 = (bf16[2,4,4,2,32,1152]{5,4,3,2,1,0:T(8,128)(2,1)}, bf16[2,4,4,2,32,2176]{5,4,3,2,1,0:T(8,128)(2,1)}, bf16[2,4,4,2,32,2176]{5,4,3,2,1,0:T(8,128)(2,1)}...) custom-call(s32[2,334]{1,0:T(2,128)} %concatenate.29.tab.refs_0_, ...), custom_call_target="tpu_custom_call" | custom-call | tf_op jit(solution)/shard_map/front/pallas_call | solution.py:368
  156.9 73.3 %feed.1 = (bf16[128,2048]{1,0:T(8,128)(2,1)}, f32[128,2048]{1,0:T(8,128)}, bf16[256,768]{1,0:T(8,128)(2,1)}, bf16[256,2048]{1,0:T(8,128)(2,1)}, bf16[256,2176]{1...) custom-call(bf16[256,768]{1,0:T(8,128)(2,1)} %get-tuple-element.70.a, ...), custom_call_target="tpu_custom_call" | custom-call | tf_op jit(solution)/shard_map/feed/pallas_call | solution.py:1328
  230.2 0.8 slice_reduce_fusion
  231.0 139.4 %attend_back.1 = (bf16[128,2048]{1,0:T(8,128)(2,1)}, f32[1,2048]{1,0:T(1,128)}, f32[1,128]{1,0:T(1,128)}, bf16[2,4,4,2,32,2176]{5,4,3,2,1,0:T(8,128)(2,1)}, bf16...) custom-call(s32[2,334]{1,0:T(2,128)} %concatenate.29.tab.refs_0_, ...), custom_call_target="tpu_custom_call" | custom-call | tf_op jit(solution)/shard_map/attend_back/pallas_call | solution.py:1111
  370.4 1.3 fusion.1.refs_5_
  371.7 62.5 %sum_weights.1 = (f32[16,8704]{1,0:T(8,128)}, f32[16,4352]{1,0:T(8,128)}, f32[16,1536]{1,0:T(8,128)}, f32[16,2304]{1,0:T(8,128)}, f32[40,128]{1,0:T(8,128)}) custom-call(bf16[2,4,4,2,32,2176]{5,4,3,2,1,0:T(8,128)(2,1)} %get-tuple-element.94.refs_0_, bf16[2,4,4,2,32,2176]{5,4,3,2,1,0:T(8,128)(2,1)} %get-tuple-element.95.refs_1_, ...), custom_call_target="tpu_custom_call" | custom-call | tf_op jit(solution)/shard_map/sum_weights/pallas_call | solution.py:675
  434.2 1.3 dynamic_slice.11
  435.5 2.9 publish.1
  438.4 1.2 slice_multiply_fusion
  (12 shorter events, 0.1 us)
Async XLA Ops:
  4.5 4.0 copy-start
  231.0 139.4 %copy-start.1 = (f32[1,2048]{1,0:T(1,128)S(1)}, f32[1,2048]{1,0:T(1,128)}, u32[]{:S(2)}) copy-start(f32[1,2048]{1,0:T(1,128)} %get-tuple-element.100) | copy-start | bytes 24580

commit v7 on v6

--- a/solution.py
+++ b/solution.py
@@ -169,13 +169,14 @@
     return out
 
 
+SPLIT = 1664
 GATHER = (
-    (0, 0, 1152, ORDERS[0]),
-    (1, 0, 1152, ORDERS[1]),
-    (2, 0, 1152, ORDERS[2]),
-    (0, 1152, 1024, ORDERS[0]),
-    (1, 1152, 1024, ORDERS[1]),
-    (2, 1152, 1024, ORDERS[2]),
+    (0, 0, SPLIT, ORDERS[0]),
+    (1, 0, SPLIT, ORDERS[1]),
+    (2, 0, SPLIT, ORDERS[2]),
+    (0, SPLIT, FH - SPLIT, ORDERS[0]),
+    (1, SPLIT, FH - SPLIT, ORDERS[1]),
+    (2, SPLIT, FH - SPLIT, ORDERS[2]),
     (3, 0, 256, ORDERS[0]),
     (3, 256, 256, ORDERS[1]),
     (3, 512, 256, ORDERS[2]),
@@ -1164,8 +1165,8 @@
     return out[0], out[1], out[2], out[3:8], out[8:]
 
 
-FIRST = ((0, 768), (768, 384))
-SECOND = ((1152, 1024),)
+FIRST = ((0, 768), (768, SPLIT - 768))
+SECOND = ((SPLIT, FH - SPLIT),)
 
 
 def rows_at(r, n=32):
@@ -1180,7 +1181,7 @@
     at = here()
     core = at["core"]
     sibling = moved(at, "core", 1)
-    late_cols = pl.ds(1152, 1024)
+    late_cols = pl.ds(SPLIT, FH - SPLIT)
     weights = ((wg_h, wg), (wu_h, wu), (wd_h, wd))
     quarters, loads = [], []
     for k, (src, dst) in enumerate(weights):
@@ -1192,7 +1193,7 @@
         quarters[-1].start()
     whole = (slice(None),) * 5
     for i, (src, dst) in enumerate(((wo_h, wo), (wd_h, wd), (wg_h, wg), (wu_h, wu))):
-        cols = whole + (pl.ds(0, QW if i == 0 else 1152),)
+        cols = whole + (pl.ds(0, QW if i == 0 else SPLIT),)
         loads.append(pltpu.make_async_copy(src.at[cols], dst.at[cols], wsem.at[i]))
         loads[-1].start()
     greet([sibling] + neighbours(at, ("x", "y", "z")))
@@ -1270,18 +1271,18 @@
     for g in gathers:
         g.pass_on()
     for c in range(2):
-        part[1, c] = back_half(c, 0, 1152)
-        part_f[:, c * 1024 : (c + 1) * 1024] = forward_half(c, 0, 1152)
+        part[1, c] = back_half(c, 0, SPLIT)
+        part_f[:, c * 1024 : (c + 1) * 1024] = forward_half(c, 0, SPLIT)
     for g in gathers:
         g.finish()
     product(back_ref, dy, wd, SECOND)
     hidden(SECOND)
     late = []
     for c in range(2):
-        part[1, c] += back_half(c, 1152, 1024)
+        part[1, c] += back_half(c, SPLIT, FH - SPLIT)
         late.append(send(part.at[1, c], got.at[1, c], psem.at[2 + c, 0], psem.at[2 + c, 1], sibling))
     for c in range(2):
-        part_f[:, c * 1024 : (c + 1) * 1024] += forward_half(c, 1152, 1024)
+        part_f[:, c * 1024 : (c + 1) * 1024] += forward_half(c, SPLIT, FH - SPLIT)
     other = pl.ds(pl.multiple_of((1 - core) * TOK, TOK), TOK)
     last = send(part_f.at[other], got_f, psem.at[4, 0], psem.at[4, 1], sibling)
 

time: 443 us -> 438 us (0.989)
    pallas_call x1, Pallas kernels: 73.3 us -> 50.3 us  [feed(): pl.pallas_call(feed_kernel, out_shape=[jax.ShapeDtypeStruct((TOK, D), BF)...]
    pallas_call x1, Pallas kernels: 148 us -> 165 us  [front(): pl.pallas_call(front_kernel, out_shape=full + [jax.ShapeDtypeStruct((2,)...]
where the time goes in v7:
time: 438 us; the launch traced here: 435 us
  Pallas kernels  422 us (96%)
  other arithmetic  7.67 us (2%)
  local copies, waits for them, and re-layouts  4.72 us (1%)
    pallas_call x1, Pallas kernels, front(): pl.pallas_call(front_kernel, out_shape=full + [jax.ShapeDtypeStruct((2,)...  165 us
    pallas_call x1, Pallas kernels, attend_back(): pl.pallas_call(attend_back_kernel, out_shape=[jax.ShapeDtypeStruct((TOK,...  141 us
    pallas_call x1, Pallas kernels, sum_weights(): pl.pallas_call(functools.partial(weight_sum_kernel, pieces, n), out_shape...  62.8 us
    pallas_call x1, Pallas kernels, feed(): pl.pallas_call(feed_kernel, out_shape=[jax.ShapeDtypeStruct((TOK, D), BF)...  50.3 us

profile of v7, /device:TPU:1, one launch (start us, length us, event | category | flops | bytes accessed | tf_op | source)
XLA Modules:
  0.0 435.1 jit_solution(8981443111588625771)
XLA Ops:
  0.7 0.8 broadcast_subtract_fusion
  1.5 0.1 add_multiply_fusion
  1.5 0.1 add_convert_fusion
  1.6 0.1 convert_element_type.33
  1.7 0.7 broadcast_subtract_fusion.1
  2.4 0.1 select_reduce_fusion
  2.5 0.1 rev.3
  2.6 0.1 and_select_fusion.2
  2.7 0.1 reduce
  2.8 0.1 compare_select_fusion.2
  2.9 0.1 compare_convert_fusion
  3.0 0.1 compare_convert_fusion.1
  3.0 0.7 concatenate.29.tab.refs_0_
  3.7 0.7 convert_dynamic-update-slice_fusion
  4.5 0.7 fusion.5
  5.2 0.1 reshape.92
  5.3 0.1 reshape.93
  5.4 0.1 pad_maximum_fusion.3
  5.5 0.8 slice.15
  6.4 0.6 pad_maximum_fusion.2.shard_one
  7.0 0.5 fusion
  7.5 1.0 pad_maximum_fusion
  8.5 0.0 copy-done
  8.5 164.8 %front.1 = (bf16[2,4,4,2,32,1152]{5,4,3,2,1,0:T(8,128)(2,1)}, bf16[2,4,4,2,32,2176]{5,4,3,2,1,0:T(8,128)(2,1)}, bf16[2,4,4,2,32,2176]{5,4,3,2,1,0:T(8,128)(2,1)}...) custom-call(s32[2,334]{1,0:T(2,128)} %concatenate.29.tab.refs_0_, ...), custom_call_target="tpu_custom_call" | custom-call | tf_op jit(solution)/shard_map/front/pallas_call | solution.py:369
  173.3 50.3 %feed.1 = (bf16[128,2048]{1,0:T(8,128)(2,1)}, f32[128,2048]{1,0:T(8,128)}, bf16[256,768]{1,0:T(8,128)(2,1)}, bf16[256,2048]{1,0:T(8,128)(2,1)}, bf16[256,2176]{1...) custom-call(bf16[256,768]{1,0:T(8,128)(2,1)} %get-tuple-element.70.a, ...), custom_call_target="tpu_custom_call" | custom-call | tf_op jit(solution)/shard_map/feed/pallas_call | solution.py:1329
  223.6 0.8 slice_reduce_fusion
  224.4 140.9 %attend_back.1 = (bf16[128,2048]{1,0:T(8,128)(2,1)}, f32[1,2048]{1,0:T(1,128)}, f32[1,128]{1,0:T(1,128)}, bf16[2,4,4,2,32,2176]{5,4,3,2,1,0:T(8,128)(2,1)}, bf16...) custom-call(s32[2,334]{1,0:T(2,128)} %concatenate.29.tab.refs_0_, ...), custom_call_target="tpu_custom_call" | custom-call | tf_op jit(solution)/shard_map/attend_back/pallas_call | solution.py:1112
  365.3 1.3 fusion.1.refs_5_
  366.6 62.8 %sum_weights.1 = (f32[16,8704]{1,0:T(8,128)}, f32[16,4352]{1,0:T(8,128)}, f32[16,1536]{1,0:T(8,128)}, f32[16,2304]{1,0:T(8,128)}, f32[40,128]{1,0:T(8,128)}) custom-call(bf16[2,4,4,2,32,2176]{5,4,3,2,1,0:T(8,128)(2,1)} %get-tuple-element.94.refs_0_, bf16[2,4,4,2,32,2176]{5,4,3,2,1,0:T(8,128)(2,1)} %get-tuple-element.95.refs_1_, ...), custom_call_target="tpu_custom_call" | custom-call | tf_op jit(solution)/shard_map/sum_weights/pallas_call | solution.py:676
  429.5 1.3 dynamic_slice.11
  430.7 2.9 publish.1
  433.6 1.2 slice_multiply_fusion
  (12 shorter events, 0.1 us)
Async XLA Ops:
  4.5 4.0 copy-start
  224.4 140.9 %copy-start.1 = (f32[1,2048]{1,0:T(1,128)S(1)}, f32[1,2048]{1,0:T(1,128)}, u32[]{:S(2)}) copy-start(f32[1,2048]{1,0:T(1,128)} %get-tuple-element.100) | copy-start | bytes 24580

commit v8 on v7

--- a/solution.py
+++ b/solution.py
@@ -58,7 +58,7 @@
     (4, 768, 384, ORDERS[2]),
 )
 N_EARLY = 9
-ADVANCE = (0, 4, 0, 6, 0, 2)
+ADVANCE = (0, 4, 0, 8, 0, 4)
 SIZES = {"x": 4, "y": 4, "z": 4, "h": 2}
 
 
@@ -1432,7 +1432,7 @@
             gain_one_terms[0],
             gain_two_terms[0],
             head_terms[0],
-            stats[:, 0],
+            stats[:, 0] / (TOK * N_CTX * 4),
         ]
     )
     sums = jnp.pad(sums, (0, 40 * 128 - sums.shape[0])).reshape(40, 128)
@@ -1441,7 +1441,7 @@
     )
     sums = sums.reshape(-1)
     own_gains = lax.dynamic_slice_in_dim(sums, device * share, share, 0)
-    stream_rms = sums[4224:4228] / (TOK * N_CTX * 4)
+    stream_rms = sums[4224:4228]
     arrays = [result[None], grad_input[None], grad_qkv, grad_proj, grad_mlp, grad_down]
     result, grad_input, grad_qkv, grad_proj, grad_mlp, grad_down = publish(arrays)
     return (

time: 438 us -> 440 us (level)
  no operation moved by 1% of the time
where the time goes in v8:
time: 440 us; the launch traced here: 436 us
  Pallas kernels  423 us (96%)
  other arithmetic  7.25 us (2%)
  local copies, waits for them, and re-layouts  5.13 us (1%)
    pallas_call x1, Pallas kernels, front(): pl.pallas_call(front_kernel, out_shape=full + [jax.ShapeDtypeStruct((2,)...  165 us
    pallas_call x1, Pallas kernels, attend_back(): pl.pallas_call(attend_back_kernel, out_shape=[jax.ShapeDtypeStruct((TOK,...  143 us
    pallas_call x1, Pallas kernels, sum_weights(): pl.pallas_call(functools.partial(weight_sum_kernel, pieces, n), out_shape...  62.4 us
    pallas_call x1, Pallas kernels, feed(): pl.pallas_call(feed_kernel, out_shape=[jax.ShapeDtypeStruct((TOK, D), BF)...  50.3 us

profile of v8, /device:TPU:1, one launch (start us, length us, event | category | flops | bytes accessed | tf_op | source)
XLA Modules:
  0.0 436.5 jit_solution(17787628296349165640)
XLA Ops:
  0.7 0.8 broadcast_subtract_fusion
  1.5 0.1 add_multiply_fusion
  1.5 0.1 add_convert_fusion
  1.6 0.1 convert_element_type.33
  1.7 0.7 broadcast_subtract_fusion.1
  2.4 0.1 select_reduce_fusion
  2.5 0.1 rev.3
  2.6 0.1 and_select_fusion.2
  2.7 0.1 reduce
  2.8 0.1 compare_select_fusion.2
  2.9 0.1 compare_convert_fusion
  3.0 0.1 compare_convert_fusion.1
  3.0 0.7 concatenate.29.tab.refs_0_
  3.7 0.7 convert_dynamic-update-slice_fusion
  4.5 0.7 fusion.5
  5.2 0.1 reshape.94
  5.3 0.1 reshape.95
  5.4 0.1 pad_maximum_fusion.3
  5.5 0.8 slice.15
  6.4 0.6 pad_maximum_fusion.2.shard_one
  7.0 0.5 fusion
  7.5 1.0 pad_maximum_fusion
  8.5 0.0 copy-done
  8.5 164.8 %front.1 = (bf16[2,4,4,2,32,1152]{5,4,3,2,1,0:T(8,128)(2,1)}, bf16[2,4,4,2,32,2176]{5,4,3,2,1,0:T(8,128)(2,1)}, bf16[2,4,4,2,32,2176]{5,4,3,2,1,0:T(8,128)(2,1)}...) custom-call(s32[2,334]{1,0:T(2,128)} %concatenate.29.tab.refs_0_, ...), custom_call_target="tpu_custom_call" | custom-call | tf_op jit(solution)/shard_map/front/pallas_call | solution.py:369
  173.3 50.3 %feed.1 = (bf16[128,2048]{1,0:T(8,128)(2,1)}, f32[128,2048]{1,0:T(8,128)}, bf16[256,768]{1,0:T(8,128)(2,1)}, bf16[256,2048]{1,0:T(8,128)(2,1)}, bf16[256,2176]{1...) custom-call(bf16[256,768]{1,0:T(8,128)(2,1)} %get-tuple-element.70.a, ...), custom_call_target="tpu_custom_call" | custom-call | tf_op jit(solution)/shard_map/feed/pallas_call | solution.py:1329
  223.6 0.8 multiply_reduce_fusion
  224.4 142.7 %attend_back.1 = (bf16[128,2048]{1,0:T(8,128)(2,1)}, f32[1,2048]{1,0:T(1,128)}, f32[1,128]{1,0:T(1,128)}, bf16[2,4,4,2,32,2176]{5,4,3,2,1,0:T(8,128)(2,1)}, bf16...) custom-call(s32[2,334]{1,0:T(2,128)} %concatenate.29.tab.refs_0_, ...), custom_call_target="tpu_custom_call" | custom-call | tf_op jit(solution)/shard_map/attend_back/pallas_call | solution.py:1112
  367.1 1.3 fusion.1.refs_5_
  368.4 62.4 %sum_weights.1 = (f32[16,8704]{1,0:T(8,128)}, f32[16,4352]{1,0:T(8,128)}, f32[16,1536]{1,0:T(8,128)}, f32[16,2304]{1,0:T(8,128)}, f32[40,128]{1,0:T(8,128)}) custom-call(bf16[2,4,4,2,32,2176]{5,4,3,2,1,0:T(8,128)(2,1)} %get-tuple-element.94.refs_0_, bf16[2,4,4,2,32,2176]{5,4,3,2,1,0:T(8,128)(2,1)} %get-tuple-element.95.refs_1_, ...), custom_call_target="tpu_custom_call" | custom-call | tf_op jit(solution)/shard_map/sum_weights/pallas_call | solution.py:676
  430.9 1.3 dynamic_slice.11
  432.1 2.9 publish.1
  435.0 1.2 slice.20
  (12 shorter events, 0.1 us)
Async XLA Ops:
  4.5 4.0 copy-start
  224.4 142.7 %copy-start.1 = (f32[1,2048]{1,0:T(1,128)S(1)}, f32[1,2048]{1,0:T(1,128)}, u32[]{:S(2)}) copy-start(f32[1,2048]{1,0:T(1,128)} %get-tuple-element.100) | copy-start | bytes 24580
